TPU v7x, 128 devices: a whole 4x4x4 slice. The times are simulated.
128 devices in a mesh: elem: 64 (over z, y_lo, x, core), section: 2 (over y_hi).
Axes of the slice: x: 4, y: 4 (y_hi: 2, y_lo: 2; y = y_hi * 2 + y_lo), z: 4, core: 2. Of those that a mesh axis runs over, the one named last changes fastest.
Arguments:
- u_start: float32 [2048, 320], P('elem'), may hold values from -6 to 6
- inverses: float32 [2048, 320, 320], P('elem'), may hold values from -1 to 2
- neighbours: int32 [2048, 5], P('elem'), may hold values from 0 to 2047, as said below
- partners: int32 [2048], replicated, may hold values from 0 to 2047, as said below
Outputs:
- section_states: float32 [4, 2048, 320], P('section', 'elem')
Inputs may be any that keep to these rules, and one draw needn't show every extreme that they name: `neighbours`: every entry names an element on the same device as the row's element, or on the device just before or after it along elem, cyclically. The partners of the 32 elements of device d along elem lie on devices d + 16 and d + 17, cyclically, 16 on each.
All inputs are finite; a program needn't handle non-finite values.
Results may differ from a plain program's by a relative error of at most 0.0001.
Values sent between devices are 32-bit elements; how exact they have to be, the bound alone decides.
No kernel may reach another device: no remote copies, remote signals or barrier semaphores. Data moves between devices by JAX's collectives and lax.ppermute only.
A program may use at most 64 MiB of HBM per device.

v0:
```python
import functools
import math

import jax
import jax.numpy as jnp
from jax import lax
from jax.experimental import pallas as pl
from jax.experimental.pallas import tpu as pltpu
from jax.sharding import PartitionSpec as P

ELEMS = 32
FIELDS = 5
UNK = 320
ROWS = 80
LANES = 128
GROUPS = 10
SECTIONS = 4

time_step = 0.03
dissipation = 2.0
enthalpy_factor = 3.5
radau_nodes = [0.08858795951270394, 0.4094668644407347, 0.787659461760847, 1.0]


def lobatto():
    inner = 1.0 / math.sqrt(5.0)
    nodes = [-1.0, -inner, inner, 1.0]
    products = []
    for row in range(4):
        value = 1.0
        for other in range(4):
            if other != row:
                value = value * (nodes[row] - nodes[other])
        products.append(value)
    return [
        [
            0.0 if row == column
            else 2.0 * (products[row] / products[column]) / (nodes[row] - nodes[column])
            for column in range(4)
        ]
        for row in range(4)
    ]


def radau_table():
    columns = []
    for column in range(SECTIONS):
        coeffs = [1.0]
        scale = 1.0
        for other in range(SECTIONS):
            if other != column:
                shifted = [0.0] + coeffs
                for position in range(len(coeffs)):
                    shifted[position] = shifted[position] - radau_nodes[other] * coeffs[position]
                coeffs = shifted
                scale = scale * (radau_nodes[column] - radau_nodes[other])
        columns.append([0.0] + [c / (k + 1.0) / scale for k, c in enumerate(coeffs)])
    butcher = []
    for row in range(SECTIONS):
        entries = []
        for column in range(SECTIONS):
            value = 0.0
            for coefficient in reversed(columns[column]):
                value = value * radau_nodes[row] + coefficient
            entries.append(value)
        butcher.append(entries)
    return butcher


DERIV = lobatto()
WEIGHT = 6.0
BUTCHER = radau_table()
ROW_SUM = [sum(row) for row in BUTCHER]
COUPLING = [time_step * BUTCHER[i][i] * dissipation * WEIGHT for i in range(SECTIONS)]
STEP_X = [time_step * ROW_SUM[i] for i in range(SECTIONS)]
STEP_Y = [time_step * ROW_SUM[i] * COUPLING[i] for i in range(SECTIONS)]


def sublane():
    return lax.broadcasted_iota(jnp.int32, (8, LANES), 0)


def lane():
    return lax.broadcasted_iota(jnp.int32, (8, LANES), 1)


def by_row(values):
    s = sublane()
    out = jnp.full((8, LANES), values[7], jnp.float32)
    for row in range(6, -1, -1):
        out = jnp.where(s == row, values[row], out)
    return out


def by_group(values):
    group = lane() // 32
    out = jnp.full((8, LANES), values[3], jnp.float32)
    for g in range(2, -1, -1):
        out = jnp.where(group == g, values[g], out)
    return out


def roll_rows(x, shift):
    shape = x.shape
    y = x.reshape(-1, 8, LANES)
    return pltpu.roll(y, shift % 8, axis=1).reshape(shape)


def roll_lanes(x, shift):
    if shift % LANES == 0:
        return x
    shape = x.shape
    y = x.reshape(-1, LANES)
    return pltpu.roll(y, shift % LANES, axis=1).reshape(shape)


def pick_lanes(x, index):
    shape = x.shape
    y = x.reshape(-1, LANES)
    wide = jnp.broadcast_to(index[None], (y.shape[0] // 8, 8, LANES)).reshape(y.shape)
    return jnp.take_along_axis(y, wide, axis=1, mode="promise_in_bounds").reshape(shape)


def prepared(u):
    half = [0.5 * u[f] for f in range(FIELDS)]
    square = half[1] * half[1] + half[2] * half[2] + half[3] * half[3]
    return half + [enthalpy_factor * half[4], square]


def take(state, index):
    return [x[index] for x in state]


def pair_flux(a, b, direction):
    density, v0, v1, v2, pressure, energy, square = [x + y for x, y in zip(a, b)]
    velocity = [v0, v1, v2]
    normal = velocity[direction]
    mass = density * normal
    out = [mass]
    for comp in range(3):
        momentum = mass * velocity[comp]
        out.append(momentum + pressure if comp == direction else momentum)
    out.append(normal * (energy + density * square))
    return out


def volume(u):
    n = prepared(u)
    d = DERIV
    rows = [[None] * 4 for _ in range(FIELDS)]

    def add(f, i, value):
        rows[f][i] = value if rows[f][i] is None else rows[f][i] + value

    for i in range(4):
        for other in range(i + 1, 4):
            flux = pair_flux(take(n, i), take(n, other), 0)
            for f in range(FIELDS):
                add(f, i, d[i][other] * flux[f])
                add(f, other, d[other][i] * flux[f])
    low = [(s // 4) for s in range(8)]
    c_same_low = by_row([d[j][1 - j] for j in low])
    c_same_high = by_row([d[2 + j][3 - j] for j in low])
    c_up = by_row([d[j][2 + j] for j in low])
    c_down = by_row([d[2 + j][j] for j in low])
    c_up_turn = by_row([d[j][3 - j] for j in low])
    c_down_turn = by_row([d[2 + j][1 - j] for j in low])
    c_next = [by_row([d[s % 4][(s % 4 + r) % 4] for s in range(8)]) for r in (1, 2, 3)]
    within = sublane() % 4

    def spin(x, r):
        return jnp.where(within + r < 4, roll_rows(x, 8 - r), roll_rows(x, 4 - r))

    for i in range(4):
        a = [x[i, 0] for x in n]
        b = [x[i, 1] for x in n]
        ra = [roll_rows(x, 4) for x in a]
        rb = [roll_rows(x, 4) for x in b]
        f1 = pair_flux(a, ra, 1)
        f2 = pair_flux(b, rb, 1)
        f3 = pair_flux(a, b, 1)
        f4 = pair_flux(a, rb, 1)
        f5 = pair_flux(b, ra, 1)
        n_i = [x[i] for x in n]
        z1 = pair_flux(n_i, [spin(x, 1) for x in n_i], 2)
        z2 = pair_flux(n_i, [spin(x, 2) for x in n_i], 2)
        for f in range(FIELDS):
            upper = c_same_low * f1[f] + c_up * f3[f] + c_up_turn * f4[f]
            lower = c_same_high * f2[f] + c_down * f3[f] + c_down_turn * f5[f]
            add(f, i, jnp.stack([upper, lower]))
            add(f, i, c_next[0] * z1[f] + c_next[1] * z2[f] + c_next[2] * spin(z1[f], 3))
    return jnp.stack([jnp.stack(rows[f]) for f in range(FIELDS)])


def face_terms(u, nx, ny, nz):
    n = prepared(u)
    px, py, pz = prepared(nx), prepared(ny), prepared(nz)
    half = 0.5 * dissipation
    s = sublane()
    low_x = pair_flux(take(n, 0), [x[0] for x in px], 0)
    high_x = pair_flux(take(n, 3), [x[1] for x in px], 0)
    y0 = pair_flux([x[:, 0] for x in n], [x[:, 0] for x in py], 1)
    y1 = pair_flux([x[:, 1] for x in n], [x[:, 1] for x in py], 1)
    z = pair_flux(n, pz, 2)
    k = s % 4
    sign_z = jnp.where(k == 0, -WEIGHT, WEIGHT)
    on_z = (k == 0) | (k == 3)
    out = []
    for f in range(FIELDS):
        part_z = jnp.where(on_z, sign_z * z[f] - (WEIGHT * half) * (nz[f] - u[f]), 0.0)
        part_y0 = jnp.where(s < 4, -WEIGHT * y0[f] - (WEIGHT * half) * (ny[f][:, 0] - u[f][:, 0]), 0.0)
        part_y1 = jnp.where(s < 4, 0.0, WEIGHT * y1[f] - (WEIGHT * half) * (ny[f][:, 1] - u[f][:, 1]))
        total = part_z + jnp.stack([part_y0, part_y1], axis=1)
        x0 = -WEIGHT * low_x[f] - (WEIGHT * half) * (nx[f][0] - u[f][0])
        x3 = WEIGHT * high_x[f] - (WEIGHT * half) * (nx[f][1] - u[f][3])
        out.append(jnp.stack([total[0] + x0, total[1], total[2], total[3] + x3]))
    return jnp.stack(out)


def lifted(nx, ny, nz):
    s = sublane()
    k = s % 4
    y = jnp.stack([jnp.where(s < 4, ny[:, :, 0], 0.0), jnp.where(s < 4, 0.0, ny[:, :, 1])], axis=2)
    total = y + jnp.where((k == 0) | (k == 3), nz, 0.0)
    return jnp.stack([total[:, 0] + nx[:, 0], total[:, 1], total[:, 2], total[:, 3] + nx[:, 1]], axis=1)


def aligned(near, far, index):
    nx = jnp.stack([pick_lanes(near[:, 3], index[0]), pick_lanes(near[:, 0], index[1])], axis=1)
    ny = jnp.stack(
        [
            roll_rows(pick_lanes(near[:, :, 1], index[2]), 4),
            roll_rows(pick_lanes(near[:, :, 0], index[3]), 4),
        ],
        axis=2,
    )
    lower = roll_rows(pick_lanes(near, index[4]), 5)
    upper = roll_rows(pick_lanes(far, index[5]), 3)
    nz = jnp.where(sublane() % 4 == 0, lower, upper)
    return nx, ny, nz


def nodes_of(parts):
    return jnp.stack([p.reshape(FIELDS, 2, 8, LANES) for p in parts], axis=1)


def group_of(x, groups):
    at = lane()[:1] // 32
    parts = [roll_lanes(y, 32 * (g - group)) for g, (y, group) in enumerate(zip(x, groups))]
    out = parts[-1]
    for g in range(len(parts) - 2, -1, -1):
        out = jnp.where(at == g, parts[g], out)
    return out


def near_far(before, own, after, ahead, beyond):
    near = nodes_of([group_of([before, own, after], [i] * 3) for i in range(4)])
    far = nodes_of([group_of([ahead, beyond], [i] * 2) for i in range(4)])
    return near, far


def spread(compact):
    base = lane() % 32
    return nodes_of([pick_lanes(compact, base + 32 * i) for i in range(4)])


def squeezed(nodes):
    at = lane() // 32
    parts = [nodes[:, i].reshape(ROWS // 8, 8, LANES) for i in range(4)]
    out = parts[3]
    for i in range(2, -1, -1):
        out = jnp.where(at == i, parts[i], out)
    return out.reshape(ROWS, LANES)


def flipped(x):
    pieces = [
        x[:, 0:128].T,
        x[:, 128:256].T,
        jnp.concatenate([x[:, 256:320], jnp.zeros((LANES, 64), jnp.float32)], axis=1).T[:64],
    ]
    return jnp.concatenate(pieces, axis=0).reshape(FIELDS, 4, 2, 8, LANES)


def multiply(t_ref, v_ref, out_ref, count, finish):
    def block(g, carry):
        rows = pl.ds(pl.multiple_of(g * 8, 8), 8)
        sums = [jnp.zeros((8, 8, LANES), jnp.float32) for _ in range(count)]
        for q in range(UNK // 8):
            piece = t_ref[rows, 8 * q : 8 * q + 8, :]
            for c in range(count):
                sums[c] = sums[c] + piece * v_ref[c, 8 * q : 8 * q + 8, :][None]
        for c in range(count):
            finish(c, rows, jnp.sum(sums[c], axis=1))
        return carry

    lax.fori_loop(0, GROUPS, block, 0)


def prepare_kernel(inv_ref, neighbours_ref, partners_ref, u_ref, t_ref, index_ref, nodes_ref, acc_ref, buf, square, sems):
    copies = []
    for g in range(GROUPS):
        f, half = g // 2, g % 2
        for i in range(4):
            start = f * 64 + i * 16 + half * 8
            copy = pltpu.make_async_copy(inv_ref.at[:, pl.ds(start, 8), :], buf.at[g, i], sems.at[g, i])
            copy.start()
            copies.append(copy)
    count = lax.axis_size("elem")
    rank = lax.axis_index("elem")
    square[...] = jnp.zeros((LANES, LANES), jnp.int32)
    square[0:ELEMS, 0:5] = neighbours_ref[...]
    turned = square[...].T[0:8, :]
    base = lane() % 32
    turned = jnp.take_along_axis(turned, base, axis=1, mode="promise_in_bounds")

    def slots(values, first):
        block = lax.shift_right_logical(values, 5) - rank - first
        block = jnp.where(block < 0, block + count, block)
        block = jnp.where(block < 0, block + count, block)
        block = jnp.where(block >= count, block - count, block)
        return block * ELEMS + (values & 31)

    near = slots(turned, -1)
    for face in range(5):
        index_ref[face] = jnp.broadcast_to(near[face : face + 1], (8, LANES))
    line = jnp.broadcast_to(partners_ref[pl.ds(rank // 4, 1), :], (8, LANES))
    line = jnp.take_along_axis(line, base + (rank % 4) * 32, axis=1, mode="promise_in_bounds")
    index_ref[5] = slots(line, count // 4)
    u = flipped(jnp.concatenate([u_ref[...]] * 4, axis=0))
    nodes_ref[...] = u
    acc_ref[...] = volume(u)

    def turn_group(g, carry):
        for i in range(4):
            pltpu.make_async_copy(inv_ref.at[:, pl.ds(0, 8), :], buf.at[g, i], sems.at[g, i]).wait()
        for r in range(8):
            x = buf[g, :, :, r, :].reshape(LANES, UNK)
            t_ref[g * 8 + r] = jnp.concatenate(
                [
                    x[:, 0:128].T,
                    x[:, 128:256].T,
                    jnp.concatenate([x[:, 256:320], x[:, 256:320]], axis=1).T[:64],
                ],
                axis=0,
            )
        return carry

    lax.fori_loop(0, GROUPS, turn_group, 0)


def first_kernel(t_ref, index_ref, nodes_ref, acc_ref, before_ref, own_ref, after_ref, ahead_ref, beyond_ref,
                 x_ref, nx_ref, ny_ref, nz_ref, v_ref):
    near = flipped(jnp.concatenate([before_ref[...], own_ref[...], after_ref[...], own_ref[...]], axis=0))
    far = flipped(jnp.concatenate([ahead_ref[...], beyond_ref[...]] * 2, axis=0))
    nx, ny, nz = aligned(near, far, index_ref[...])
    nx_ref[...], ny_ref[...], nz_ref[...] = nx, ny, nz
    total = acc_ref[...] + face_terms(nodes_ref[...], nx, ny, nz)
    v_ref[0] = (-2.0 * total).reshape(UNK, LANES)

    def finish(c, rows, value):
        x_ref[rows, :] = value

    multiply(t_ref, v_ref, x_ref, 1, finish)


def second_kernel(t_ref, index_ref, before_ref, own_ref, after_ref, ahead_ref, beyond_ref,
                  y_ref, nx_ref, ny_ref, nz_ref, v_ref):
    near, far = near_far(before_ref[...], own_ref[...], after_ref[...], ahead_ref[...], beyond_ref[...])
    nx, ny, nz = aligned(near, far, index_ref[...])
    nx_ref[...], ny_ref[...], nz_ref[...] = nx, ny, nz
    v_ref[0] = lifted(nx, ny, nz).reshape(UNK, LANES)

    def finish(c, rows, value):
        y_ref[rows, :] = value

    multiply(t_ref, v_ref, y_ref, 1, finish)


def middle_kernel(u_ref, x_ref, y_ref, states_ref, acc_ref):
    u = u_ref[...]
    x, y = spread(x_ref[...]), spread(y_ref[...])
    states = u + by_group(STEP_X) * x + by_group(STEP_Y) * y
    states_ref[...] = states
    acc_ref[...] = volume(states)


def section_value(table, which):
    first = lax.axis_index("section") == 0
    return jnp.where(first, table[which], table[2 + which]).astype(jnp.float32)


def third_kernel(t_ref, index_ref, u_ref, states_ref, acc_ref, x_ref,
                 ux_ref, uy_ref, uz_ref, xx_ref, xy_ref, xz_ref,
                 before_ref, own_ref, after_ref, ahead_ref, beyond_ref,
                 first_ref, base_ref, v_ref):
    near, far = near_far(before_ref[...], own_ref[...], after_ref[...], ahead_ref[...], beyond_ref[...])
    yx, yy, yz = aligned(near, far, index_ref[...])
    a, b = by_group(STEP_X), by_group(STEP_Y)
    nx = ux_ref[...] + a * xx_ref[...] + b * yx
    ny = uy_ref[...] + a * xy_ref[...] + b * yy
    nz = uz_ref[...] + a * xz_ref[...] + b * yz
    total = (acc_ref[...] + face_terms(states_ref[...], nx, ny, nz)).reshape(UNK, LANES)
    turned = [total] + [roll_lanes(total, 32 * r) for r in (1, 2, 3)]
    x, y = x_ref[...], own_ref[...]
    xs, ys = spread(x).reshape(UNK, LANES), spread(y).reshape(UNK, LANES)
    u = squeezed(u_ref[...])
    shape = (UNK // 8, 8, LANES)
    for c in range(2):
        v = -section_value(STEP_X, c) * xs - section_value(STEP_Y, c) * ys
        v = v.reshape(shape)
        for r in range(4):
            factor = by_group(
                [
                    section_value([-2.0 * time_step * BUTCHER[s][(g - r) % 4] for s in range(4)], c)
                    for g in range(4)
                ]
            )
            v = v + factor * turned[r].reshape(shape)
        v_ref[c] = v.reshape(UNK, LANES)
        base_ref[c] = u + section_value(STEP_X, c) * x + section_value(STEP_Y, c) * y

    def finish(c, rows, value):
        first_ref[c, rows, :] = value
        base_ref[c, rows, :] = base_ref[c, rows, :] + value

    multiply(t_ref, v_ref, first_ref, 2, finish)


def fourth_kernel(t_ref, index_ref, base_ref, before_ref, own_ref, after_ref, ahead_ref, beyond_ref, out_ref, v_ref, done_ref):
    for c in range(2):
        near, far = near_far(before_ref[c], own_ref[c], after_ref[c], ahead_ref[c], beyond_ref[c])
        v_ref[c] = lifted(*aligned(near, far, index_ref[...])).reshape(UNK, LANES)

    def finish(c, rows, value):
        done_ref[c, rows, :] = base_ref[c, rows, :] + section_value(COUPLING, c) * value

    multiply(t_ref, v_ref, done_ref, 2, finish)
    both = nodes_of([group_of([done_ref[0], done_ref[1]], [i] * 2) for i in range(4)]).reshape(UNK, LANES)
    turned = [
        both[0:128].T,
        both[128:256].T,
        jnp.concatenate([both[256:320], both[256:320]], axis=0).T[:, :64],
    ]
    for c in range(2):
        rows = slice(c * ELEMS, (c + 1) * ELEMS)
        out_ref[c, :, 0:128] = turned[0][rows]
        out_ref[c, :, 128:256] = turned[1][rows]
        out_ref[c, :, 256:320] = turned[2][rows]


VMEM = pltpu.VMEM
F32 = jnp.float32
NODES = (FIELDS, 4, 2, 8, LANES)
NX = (FIELDS, 2, 2, 8, LANES)
COMPACT = (ROWS, LANES)


def call(kernel, inputs, outputs, scratch=(), anywhere=(), flops=10**7, room=8):
    in_specs = [pl.BlockSpec(memory_space=pltpu.HBM if i in anywhere else VMEM) for i in range(len(inputs))]
    return pl.pallas_call(
        kernel,
        out_shape=outputs,
        in_specs=in_specs,
        out_specs=[pl.BlockSpec(memory_space=VMEM)] * len(outputs),
        scratch_shapes=list(scratch),
        compiler_params=pltpu.CompilerParams(vmem_limit_bytes=room * 2**20),
        cost_estimate=pl.CostEstimate(flops=flops, bytes_accessed=10**6, transcendentals=0),
    )(*inputs)


def vm(shape, dtype=F32):
    return pltpu.VMEM(shape, dtype)


def passed(block, distance):
    count = lax.axis_size("elem")
    return lax.ppermute(block, "elem", [((i - distance) % count, i) for i in range(count)])


def exchanged(block):
    far = lax.axis_size("elem") // 4
    before, after = passed(block, 1), passed(block, -1)
    ahead, beyond = passed(block, -far), passed(block, -(far + 1))
    return [before, block, after, ahead, beyond]


def keep(x):
    return pltpu.with_memory_space_constraint(x, VMEM)


def on_device(u_start, inverses, neighbours, partners):
    partners = partners.reshape(-1, LANES)
    u_all = exchanged(u_start)
    t, index, nodes, acc = call(
        prepare_kernel,
        [pltpu.with_memory_space_constraint(inverses, pltpu.HBM), neighbours, partners, u_start],
        [vm((ROWS, UNK, LANES)), vm((6, 8, LANES), jnp.int32), vm(NODES), vm(NODES)],
        [
            pltpu.VMEM((GROUPS, 4, ELEMS, 8, UNK), F32),
            pltpu.VMEM((LANES, LANES), jnp.int32),
            pltpu.SemaphoreType.DMA((GROUPS, 4)),
        ],
        anywhere=(0,),
        flops=10**9,
        room=24,
    )
    t, index, nodes = keep(t), keep(index), keep(nodes)
    x, ux, uy, uz = call(
        first_kernel, [t, index, nodes, keep(acc), *u_all],
        [vm(COMPACT), vm(NX), vm(NODES), vm(NODES)], [pltpu.VMEM((1, UNK, LANES), F32)],
    )
    y, xx, xy, xz = call(
        second_kernel, [t, index, *exchanged(x)],
        [vm(COMPACT), vm(NX), vm(NODES), vm(NODES)], [pltpu.VMEM((1, UNK, LANES), F32)],
    )
    y_all = exchanged(y)
    states, acc = call(middle_kernel, [nodes, x, y], [vm(NODES), vm(NODES)])
    first, base = call(
        third_kernel,
        [t, index, nodes, keep(states), keep(acc), x, *[keep(k) for k in (ux, uy, uz, xx, xy, xz)], *y_all],
        [vm((2,) + COMPACT), vm((2,) + COMPACT)], [pltpu.VMEM((2, UNK, LANES), F32)],
    )
    [out] = call(
        fourth_kernel, [t, index, keep(base), *exchanged(first)],
        [jax.ShapeDtypeStruct((2, ELEMS, UNK), F32)],
        [pltpu.VMEM((2, UNK, LANES), F32), pltpu.VMEM((2,) + COMPACT, F32)],
    )
    return out


def solution(mesh):
    placed = (P("elem", None), P("elem", None, None), P("elem", None), P())
    return jax.shard_map(
        on_device, mesh=mesh, in_specs=placed, out_specs=P("section", "elem", None), check_vma=False
    )
```

profile of v0, /device:TPU:0, one launch (start us, length us, event | category | flops | bytes accessed | tf_op | source)
XLA Modules:
  0.0 62.2 jit_solution(4008180077267045907)
XLA Ops:
  0.0 4.1 %collective-permute-start.2 = (f32[32,320]{1,0:T(8,128)}, f32[32,320]{1,0:T(8,128)S(1)}, u32[]{:S(2)}, u32[]{:S(2)}) collective-permute-start(f32[32,320]{1,0:T(8,128)} %own_ref.1), channel_id=1, source_target_pairs={{32,0},{34,2},{36,4},{38,6},{40,8},{42,10},{44,12},{46,14},{48,16}... | collective-permute-start | bytes 122888 | tf_op jit(solution)/shard_map/ppermute | solution.py:478
  4.1 2.8 %collective-permute-start.1 = (f32[32,320]{1,0:T(8,128)}, f32[32,320]{1,0:T(8,128)S(1)}, u32[]{:S(2)}, u32[]{:S(2)}) collective-permute-start(f32[32,320]{1,0:T(8,128)} %own_ref.1), channel_id=1, source_target_pairs={{2,0},{4,2},{6,4},{8,6},{10,8},{12,10},{14,12},{16,14},{18,16},{20... | collective-permute-start | bytes 122888 | tf_op jit(solution)/shard_map/ppermute | solution.py:478
  6.9 0.0 collective-permute-start
  6.9 4.5 %collective-permute-start.3 = (f32[32,320]{1,0:T(8,128)}, f32[32,320]{1,0:T(8,128)S(1)}, u32[]{:S(2)}, u32[]{:S(2)}) collective-permute-start(f32[32,320]{1,0:T(8,128)} %own_ref.1), channel_id=1, source_target_pairs={{34,0},{36,2},{38,4},{40,6},{42,8},{44,10},{46,12},{48,14},{50,16}... | collective-permute-start | bytes 122888 | tf_op jit(solution)/shard_map/ppermute | solution.py:478
  11.4 0.8 %copy.5.neighbours_ref = s32[32,5]{1,0:T(8,128)S(1)} copy(s32[32,5]{0,1:T(8,128)} %param.6) | data formatting | bytes 1280 | tf_op args[2]
  12.1 0.0 copy-start
  12.1 0.8 %copy-done = f32[32,320]{1,0:T(8,128)S(1)} copy-done((f32[32,320]{1,0:T(8,128)S(1)}, f32[32,320]{1,0:T(8,128)}, u32[]{:S(2)}) %copy-start) | copy-done | bytes 40984
  12.9 0.0 copy-start.1
  12.9 0.7 %copy-done.1 = s32[2048]{0:T(1024)S(1)} copy-done((s32[2048]{0:T(1024)S(1)}, s32[2048]{0:T(1024)}, u32[]{:S(2)}) %copy-start.1) | copy-done | bytes 8216
  13.6 11.1 %shard_map.46 = (f32[80,320,128]{2,1,0:T(8,128)S(1)}, s32[6,8,128]{2,1,0:T(8,128)S(1)}, f32[5,4,2,8,128]{4,3,2,1,0:T(8,128)S(1)}, f32[5,4,2,8,128]{4,3,2,1,0:T(8,128)S(1)}) custom-call(f32[32,320,320]{2,1,0:T(8,128)} %inv_ref.1, s32[32,5]{1,0:T(8,128)S(1)} %copy.5.neighbours_ref, s32[16,128]{1,0:T(8,128)S(1)} %bitcast.1, f32[32,320]{1,0:T(8,128)S(1)} %copy-done), custom_call_target="tpu_custom_call" | custom-call | flops 1000000000 | bytes 1000000 | tf_op jit(solution)/shard_map/pallas_call | solution.py:461
  24.8 0.0 collective-permute-done.2.ahead_ref
  24.8 0.0 collective-permute-done.1.after_ref
  24.8 0.0 collective-permute-done.before_ref
  24.8 0.0 collective-permute-done.3.beyond_ref
  24.8 1.4 %shard_map.47 = (f32[80,128]{1,0:T(8,128)S(1)}, f32[5,2,2,8,128]{4,3,2,1,0:T(8,128)S(1)}, f32[5,4,2,8,128]{4,3,2,1,0:T(8,128)S(1)}, f32[5,4,2,8,128]{4,3,2,1,0:T(8,128)S(1)}) custom-call(f32[80,320,128]{2,1,0:T(8,128)S(1)} %get-tuple-element.21.t_ref, s32[6,8,128]{2,1,0:T(8,128)S(1)} %get-tuple-element.22.index_ref, ...), custom_call_target="tpu_custom_call" | custom-call | flops 10000000 | bytes 1000000 | tf_op jit(solution)/shard_map/pallas_call | solution.py:461
  26.2 0.1 collective-permute-start.7
  26.3 0.9 %collective-permute-start.6 = (f32[80,128]{1,0:T(8,128)S(1)}, f32[80,128]{1,0:T(8,128)S(1)}, u32[]{:S(2)}, u32[]{:S(2)}) collective-permute-start(f32[80,128]{1,0:T(8,128)S(1)} %get-tuple-element.25.own_ref.x_ref), channel_id=1, source_target_pairs={{32,0},{34,2},{36,4},{38,6},{40,8},{42,10},{44,12},{46,14},{48,16}... | collective-permute-start | bytes 122888 | tf_op jit(solution)/shard_map/ppermute | solution.py:478
  27.2 0.8 %collective-permute-start.5 = (f32[80,128]{1,0:T(8,128)S(1)}, f32[80,128]{1,0:T(8,128)S(1)}, u32[]{:S(2)}, u32[]{:S(2)}) collective-permute-start(f32[80,128]{1,0:T(8,128)S(1)} %get-tuple-element.25.own_ref.x_ref), channel_id=1, source_target_pairs={{2,0},{4,2},{6,4},{8,6},{10,8},{12,10},{14,12},{16,14},{18,16},{20... | collective-permute-start | bytes 122888 | tf_op jit(solution)/shard_map/ppermute | solution.py:478
  27.9 2.2 %collective-permute-start.4 = (f32[80,128]{1,0:T(8,128)S(1)}, f32[80,128]{1,0:T(8,128)S(1)}, u32[]{:S(2)}, u32[]{:S(2)}) collective-permute-start(f32[80,128]{1,0:T(8,128)S(1)} %get-tuple-element.25.own_ref.x_ref), channel_id=1, source_target_pairs={{126,0},{0,2},{2,4},{4,6},{6,8},{8,10},{10,12},{12,14},{14,16},{16... | collective-permute-start | bytes 122888 | tf_op jit(solution)/shard_map/ppermute | solution.py:478
  30.1 0.0 collective-permute-done.7.beyond_ref
  30.1 0.6 collective-permute-done.6.ahead_ref
  30.7 0.1 collective-permute-done.5.after_ref
  30.8 4.8 %collective-permute-done.4.before_ref = f32[80,128]{1,0:T(8,128)S(1)} collective-permute-done((f32[80,128]{1,0:T(8,128)S(1)}, f32[80,128]{1,0:T(8,128)S(1)}, u32[]{:S(2)}, u32[]{:S(2)}) %collective-permute-start.4) | collective-permute-done | bytes 40992 | tf_op jit(solution)/shard_map/ppermute | solution.py:478
  35.6 1.4 %shard_map.48 = (f32[80,128]{1,0:T(8,128)S(1)}, f32[5,2,2,8,128]{4,3,2,1,0:T(8,128)S(1)}, f32[5,4,2,8,128]{4,3,2,1,0:T(8,128)S(1)}, f32[5,4,2,8,128]{4,3,2,1,0:T(8,128)S(1)}) custom-call(f32[80,320,128]{2,1,0:T(8,128)S(1)} %get-tuple-element.21.t_ref, s32[6,8,128]{2,1,0:T(8,128)S(1)} %get-tuple-element.22.index_ref, ...), custom_call_target="tpu_custom_call" | custom-call | flops 10000000 | bytes 1000000 | tf_op jit(solution)/shard_map/pallas_call | solution.py:461
  37.0 0.7 %collective-permute-start.11 = (f32[80,128]{1,0:T(8,128)S(1)}, f32[80,128]{1,0:T(8,128)S(1)}, u32[]{:S(2)}, u32[]{:S(2)}) collective-permute-start(f32[80,128]{1,0:T(8,128)S(1)} %get-tuple-element.26.y_ref.own_ref), channel_id=1, source_target_pairs={{34,0},{36,2},{38,4},{40,6},{42,8},{44,10},{46,12},{48,14},{50,16}... | collective-permute-start | bytes 122888 | tf_op jit(solution)/shard_map/ppermute | solution.py:478
  37.7 1.6 %collective-permute-start.10 = (f32[80,128]{1,0:T(8,128)S(1)}, f32[80,128]{1,0:T(8,128)S(1)}, u32[]{:S(2)}, u32[]{:S(2)}) collective-permute-start(f32[80,128]{1,0:T(8,128)S(1)} %get-tuple-element.26.y_ref.own_ref), channel_id=1, source_target_pairs={{32,0},{34,2},{36,4},{38,6},{40,8},{42,10},{44,12},{46,14},{48,16}... | collective-permute-start | bytes 122888 | tf_op jit(solution)/shard_map/ppermute | solution.py:478
  39.3 0.0 collective-permute-start.9
  39.3 0.5 collective-permute-start.8
  39.8 0.4 shard_map.49
  40.2 0.2 collective-permute-done.11.beyond_ref
  40.5 1.3 %collective-permute-done.10.ahead_ref = f32[80,128]{1,0:T(8,128)S(1)} collective-permute-done((f32[80,128]{1,0:T(8,128)S(1)}, f32[80,128]{1,0:T(8,128)S(1)}, u32[]{:S(2)}, u32[]{:S(2)}) %collective-permute-start.10) | collective-permute-done | bytes 40992 | tf_op jit(solution)/shard_map/ppermute | solution.py:478
  41.8 0.0 collective-permute-done.9.after_ref
  41.8 5.1 %collective-permute-done.8.before_ref = f32[80,128]{1,0:T(8,128)S(1)} collective-permute-done((f32[80,128]{1,0:T(8,128)S(1)}, f32[80,128]{1,0:T(8,128)S(1)}, u32[]{:S(2)}, u32[]{:S(2)}) %collective-permute-start.8) | collective-permute-done | bytes 40992 | tf_op jit(solution)/shard_map/ppermute | solution.py:478
  46.9 2.7 %shard_map.50 = (f32[2,80,128]{2,1,0:T(8,128)S(1)}, f32[2,80,128]{2,1,0:T(8,128)S(1)}) custom-call(f32[80,320,128]{2,1,0:T(8,128)S(1)} %get-tuple-element.21.t_ref, s32[6,8,128]{2,1,0:T(8,128)S(1)} %get-tuple-element.22.index_ref, f32[5,4,2,8,128]{4,3,2,1,0:T(8,128)S(1)} %get-tuple-element.23.nodes_ref.u_ref, ...), custom_call_target="tpu_custom_call" | custom-call | flops 10000000 | bytes 1000000 | tf_op jit(solution)/shard_map/pallas_call | solution.py:461
  49.6 0.1 collective-permute-start.15
  49.7 0.7 %collective-permute-start.14 = (f32[2,80,128]{2,1,0:T(8,128)S(1)}, f32[2,80,128]{2,1,0:T(8,128)S(1)}, u32[]{:S(2)}, u32[]{:S(2)}) collective-permute-start(f32[2,80,128]{2,1,0:T(8,128)S(1)} %get-tuple-element.36.own_ref), channel_id=1, source_target_pairs={{32,0},{34,2},{36,4},{38,6},{40,8},{42,10},{44,12},{46,14},{48,16}... | collective-permute-start | bytes 245768 | tf_op jit(solution)/shard_map/ppermute | solution.py:478
  50.4 0.0 collective-permute-start.13
  50.4 0.5 collective-permute-start.12
  51.0 2.9 %collective-permute-done.15.beyond_ref = f32[2,80,128]{2,1,0:T(8,128)S(1)} collective-permute-done((f32[2,80,128]{2,1,0:T(8,128)S(1)}, f32[2,80,128]{2,1,0:T(8,128)S(1)}, u32[]{:S(2)}, u32[]{:S(2)}) %collective-permute-start.15) | collective-permute-done | bytes 81952 | tf_op jit(solution)/shard_map/ppermute | solution.py:478
  53.8 1.2 %collective-permute-done.14.ahead_ref = f32[2,80,128]{2,1,0:T(8,128)S(1)} collective-permute-done((f32[2,80,128]{2,1,0:T(8,128)S(1)}, f32[2,80,128]{2,1,0:T(8,128)S(1)}, u32[]{:S(2)}, u32[]{:S(2)}) %collective-permute-start.14) | collective-permute-done | bytes 81952 | tf_op jit(solution)/shard_map/ppermute | solution.py:478
  55.1 0.0 collective-permute-done.13.after_ref
  55.1 3.5 %collective-permute-done.12.before_ref = f32[2,80,128]{2,1,0:T(8,128)S(1)} collective-permute-done((f32[2,80,128]{2,1,0:T(8,128)S(1)}, f32[2,80,128]{2,1,0:T(8,128)S(1)}, u32[]{:S(2)}, u32[]{:S(2)}) %collective-permute-start.12) | collective-permute-done | bytes 81952 | tf_op jit(solution)/shard_map/ppermute | solution.py:478
  58.5 3.7 %shard_map.51 = f32[2,32,320]{2,1,0:T(8,128)} custom-call(f32[80,320,128]{2,1,0:T(8,128)S(1)} %get-tuple-element.21.t_ref, s32[6,8,128]{2,1,0:T(8,128)S(1)} %get-tuple-element.22.index_ref, f32[2,80,128]{2,1,0:T(8,128)S(1)} %get-tuple-element.35.base_ref, f32[2,80,128]{2,1,0:T(8,128)S(1)} %collective-permute-done.12.before_ref, ...), custom_call_target="tpu_custom_call" | custom-call | flops 10000000 | bytes 1000000 | tf_op jit(solution)/shard_map/pallas_call | solution.py:461
Async XLA Ops:
  0.0 24.8 %collective-permute-start.2 = (f32[32,320]{1,0:T(8,128)}, f32[32,320]{1,0:T(8,128)S(1)}, u32[]{:S(2)}, u32[]{:S(2)}) collective-permute-start(f32[32,320]{1,0:T(8,128)} %own_ref.1), channel_id=1, source_target_pairs={{32,0},{34,2},{36,4},{38,6},{40,8},{42,10},{44,12},{46,14},{48,16}... | collective-permute-start | bytes 122888 | tf_op jit(solution)/shard_map/ppermute | solution.py:478
  4.1 20.7 %collective-permute-start.1 = (f32[32,320]{1,0:T(8,128)}, f32[32,320]{1,0:T(8,128)S(1)}, u32[]{:S(2)}, u32[]{:S(2)}) collective-permute-start(f32[32,320]{1,0:T(8,128)} %own_ref.1), channel_id=1, source_target_pairs={{2,0},{4,2},{6,4},{8,6},{10,8},{12,10},{14,12},{16,14},{18,16},{20... | collective-permute-start | bytes 122888 | tf_op jit(solution)/shard_map/ppermute | solution.py:478
  6.9 17.9 %collective-permute-start = (f32[32,320]{1,0:T(8,128)}, f32[32,320]{1,0:T(8,128)S(1)}, u32[]{:S(2)}, u32[]{:S(2)}) collective-permute-start(f32[32,320]{1,0:T(8,128)} %own_ref.1), channel_id=1, source_target_pairs={{126,0},{0,2},{2,4},{4,6},{6,8},{8,10},{10,12},{12,14},{14,16},{16... | collective-permute-start | bytes 122888 | tf_op jit(solution)/shard_map/ppermute | solution.py:478
  6.9 17.9 %collective-permute-start.3 = (f32[32,320]{1,0:T(8,128)}, f32[32,320]{1,0:T(8,128)S(1)}, u32[]{:S(2)}, u32[]{:S(2)}) collective-permute-start(f32[32,320]{1,0:T(8,128)} %own_ref.1), channel_id=1, source_target_pairs={{34,0},{36,2},{38,4},{40,6},{42,8},{44,10},{46,12},{48,14},{50,16}... | collective-permute-start | bytes 122888 | tf_op jit(solution)/shard_map/ppermute | solution.py:478
  12.1 0.8 %copy-start = (f32[32,320]{1,0:T(8,128)S(1)}, f32[32,320]{1,0:T(8,128)}, u32[]{:S(2)}) copy-start(f32[32,320]{1,0:T(8,128)} %own_ref.1) | copy-start | bytes 122884
  12.9 0.7 %copy-start.1 = (s32[2048]{0:T(1024)S(1)}, s32[2048]{0:T(1024)}, u32[]{:S(2)}) copy-start(s32[2048]{0:T(1024)} %param.7) | copy-start | bytes 24580
  26.2 3.9 %collective-permute-start.7 = (f32[80,128]{1,0:T(8,128)S(1)}, f32[80,128]{1,0:T(8,128)S(1)}, u32[]{:S(2)}, u32[]{:S(2)}) collective-permute-start(f32[80,128]{1,0:T(8,128)S(1)} %get-tuple-element.25.own_ref.x_ref), channel_id=1, source_target_pairs={{34,0},{36,2},{38,4},{40,6},{42,8},{44,10},{46,12},{48,14},{50,16}... | collective-permute-start | bytes 122888 | tf_op jit(solution)/shard_map/ppermute | solution.py:478
  26.3 4.4 %collective-permute-start.6 = (f32[80,128]{1,0:T(8,128)S(1)}, f32[80,128]{1,0:T(8,128)S(1)}, u32[]{:S(2)}, u32[]{:S(2)}) collective-permute-start(f32[80,128]{1,0:T(8,128)S(1)} %get-tuple-element.25.own_ref.x_ref), channel_id=1, source_target_pairs={{32,0},{34,2},{36,4},{38,6},{40,8},{42,10},{44,12},{46,14},{48,16}... | collective-permute-start | bytes 122888 | tf_op jit(solution)/shard_map/ppermute | solution.py:478
  27.2 3.6 %collective-permute-start.5 = (f32[80,128]{1,0:T(8,128)S(1)}, f32[80,128]{1,0:T(8,128)S(1)}, u32[]{:S(2)}, u32[]{:S(2)}) collective-permute-start(f32[80,128]{1,0:T(8,128)S(1)} %get-tuple-element.25.own_ref.x_ref), channel_id=1, source_target_pairs={{2,0},{4,2},{6,4},{8,6},{10,8},{12,10},{14,12},{16,14},{18,16},{20... | collective-permute-start | bytes 122888 | tf_op jit(solution)/shard_map/ppermute | solution.py:478
  27.9 7.6 %collective-permute-start.4 = (f32[80,128]{1,0:T(8,128)S(1)}, f32[80,128]{1,0:T(8,128)S(1)}, u32[]{:S(2)}, u32[]{:S(2)}) collective-permute-start(f32[80,128]{1,0:T(8,128)S(1)} %get-tuple-element.25.own_ref.x_ref), channel_id=1, source_target_pairs={{126,0},{0,2},{2,4},{4,6},{6,8},{8,10},{10,12},{12,14},{14,16},{16... | collective-permute-start | bytes 122888 | tf_op jit(solution)/shard_map/ppermute | solution.py:478
  37.0 3.5 %collective-permute-start.11 = (f32[80,128]{1,0:T(8,128)S(1)}, f32[80,128]{1,0:T(8,128)S(1)}, u32[]{:S(2)}, u32[]{:S(2)}) collective-permute-start(f32[80,128]{1,0:T(8,128)S(1)} %get-tuple-element.26.y_ref.own_ref), channel_id=1, source_target_pairs={{34,0},{36,2},{38,4},{40,6},{42,8},{44,10},{46,12},{48,14},{50,16}... | collective-permute-start | bytes 122888 | tf_op jit(solution)/shard_map/ppermute | solution.py:478
  37.7 4.1 %collective-permute-start.10 = (f32[80,128]{1,0:T(8,128)S(1)}, f32[80,128]{1,0:T(8,128)S(1)}, u32[]{:S(2)}, u32[]{:S(2)}) collective-permute-start(f32[80,128]{1,0:T(8,128)S(1)} %get-tuple-element.26.y_ref.own_ref), channel_id=1, source_target_pairs={{32,0},{34,2},{36,4},{38,6},{40,8},{42,10},{44,12},{46,14},{48,16}... | collective-permute-start | bytes 122888 | tf_op jit(solution)/shard_map/ppermute | solution.py:478
  39.3 2.5 %collective-permute-start.9 = (f32[80,128]{1,0:T(8,128)S(1)}, f32[80,128]{1,0:T(8,128)S(1)}, u32[]{:S(2)}, u32[]{:S(2)}) collective-permute-start(f32[80,128]{1,0:T(8,128)S(1)} %get-tuple-element.26.y_ref.own_ref), channel_id=1, source_target_pairs={{2,0},{4,2},{6,4},{8,6},{10,8},{12,10},{14,12},{16,14},{18,16},{20... | collective-permute-start | bytes 122888 | tf_op jit(solution)/shard_map/ppermute | solution.py:478
  39.3 7.6 %collective-permute-start.8 = (f32[80,128]{1,0:T(8,128)S(1)}, f32[80,128]{1,0:T(8,128)S(1)}, u32[]{:S(2)}, u32[]{:S(2)}) collective-permute-start(f32[80,128]{1,0:T(8,128)S(1)} %get-tuple-element.26.y_ref.own_ref), channel_id=1, source_target_pairs={{126,0},{0,2},{2,4},{4,6},{6,8},{8,10},{10,12},{12,14},{14,16},{16... | collective-permute-start | bytes 122888 | tf_op jit(solution)/shard_map/ppermute | solution.py:478
  49.6 4.2 %collective-permute-start.15 = (f32[2,80,128]{2,1,0:T(8,128)S(1)}, f32[2,80,128]{2,1,0:T(8,128)S(1)}, u32[]{:S(2)}, u32[]{:S(2)}) collective-permute-start(f32[2,80,128]{2,1,0:T(8,128)S(1)} %get-tuple-element.36.own_ref), channel_id=1, source_target_pairs={{34,0},{36,2},{38,4},{40,6},{42,8},{44,10},{46,12},{48,14},{50,16}... | collective-permute-start | bytes 245768 | tf_op jit(solution)/shard_map/ppermute | solution.py:478
  49.7 5.3 %collective-permute-start.14 = (f32[2,80,128]{2,1,0:T(8,128)S(1)}, f32[2,80,128]{2,1,0:T(8,128)S(1)}, u32[]{:S(2)}, u32[]{:S(2)}) collective-permute-start(f32[2,80,128]{2,1,0:T(8,128)S(1)} %get-tuple-element.36.own_ref), channel_id=1, source_target_pairs={{32,0},{34,2},{36,4},{38,6},{40,8},{42,10},{44,12},{46,14},{48,16}... | collective-permute-start | bytes 245768 | tf_op jit(solution)/shard_map/ppermute | solution.py:478
  50.4 4.6 %collective-permute-start.13 = (f32[2,80,128]{2,1,0:T(8,128)S(1)}, f32[2,80,128]{2,1,0:T(8,128)S(1)}, u32[]{:S(2)}, u32[]{:S(2)}) collective-permute-start(f32[2,80,128]{2,1,0:T(8,128)S(1)} %get-tuple-element.36.own_ref), channel_id=1, source_target_pairs={{2,0},{4,2},{6,4},{8,6},{10,8},{12,10},{14,12},{16,14},{18,16},{20... | collective-permute-start | bytes 245768 | tf_op jit(solution)/shard_map/ppermute | solution.py:478
  50.4 8.1 %collective-permute-start.12 = (f32[2,80,128]{2,1,0:T(8,128)S(1)}, f32[2,80,128]{2,1,0:T(8,128)S(1)}, u32[]{:S(2)}, u32[]{:S(2)}) collective-permute-start(f32[2,80,128]{2,1,0:T(8,128)S(1)} %get-tuple-element.36.own_ref), channel_id=1, source_target_pairs={{126,0},{0,2},{2,4},{4,6},{6,8},{8,10},{10,12},{12,14},{14,16},{16... | collective-permute-start | bytes 245768 | tf_op jit(solution)/shard_map/ppermute | solution.py:478
where the time goes:
time: 62.5 us; the launch traced here: 62.2 us
  Pallas kernels  20.7 us (33%)
  waiting for transfers between devices  19.8 us (32%)
  starting transfers between devices  19.4 us (31%)
  local copies, waits for them, and re-layouts  2.26 us (4%)
    pallas_call x6, Pallas kernels, call(): pl.pallas_call(kernel, out_shape=outputs, in_specs=in_specs, out_specs=[p...  20.7 us
    ppermute x16, waiting for transfers between devices, passed(): lax.ppermute(block, 'elem', [((i - distance) % count, i) for i in range(c...  19.8 us
    ppermute x16, starting transfers between devices, passed(): lax.ppermute(block, 'elem', [((i - distance) % count, i) for i in range(c...  19.4 us
    unnamed x5, local copies, waits for them, and re-layouts  2.26 us
  transfers between devices with their start and end apart: 16, of which 9 were waited for; matrix products, arithmetic and copies ran while one was open for 1% of the time, Pallas kernels for 19%

commit v1 on v0

--- a/solution.py
+++ b/solution.py
@@ -297,22 +297,37 @@
     lax.fori_loop(0, GROUPS, block, 0)
 
 
-def prepare_kernel(inv_ref, neighbours_ref, partners_ref, u_ref, t_ref, index_ref, nodes_ref, acc_ref, buf, square, sems):
-    copies = []
+def prepare_kernel(inv_ref, neighbours_ref, partners_ref, u_ref, t_ref, index_ref, nodes_ref, acc_ref,
+                   wide, tail, square, line_ref, own, sems, small):
+    smalls = [
+        pltpu.make_async_copy(u_ref, own, small.at[0]),
+        pltpu.make_async_copy(neighbours_ref, square, small.at[1]),
+        pltpu.make_async_copy(partners_ref, line_ref, small.at[2]),
+    ]
+    for copy in smalls:
+        copy.start()
+
+    def pieces(g, i, start):
+        rows = pl.ds(start, 8)
+        return [
+            pltpu.make_async_copy(inv_ref.at[:, rows, pl.ds(0, 128)], wide.at[g, 0, i], sems.at[g, i, 0]),
+            pltpu.make_async_copy(inv_ref.at[:, rows, pl.ds(128, 128)], wide.at[g, 1, i], sems.at[g, i, 1]),
+            pltpu.make_async_copy(inv_ref.at[:, rows, pl.ds(256, 64)], tail.at[g, i], sems.at[g, i, 2]),
+        ]
+
     for g in range(GROUPS):
         f, half = g // 2, g % 2
         for i in range(4):
-            start = f * 64 + i * 16 + half * 8
-            copy = pltpu.make_async_copy(inv_ref.at[:, pl.ds(start, 8), :], buf.at[g, i], sems.at[g, i])
-            copy.start()
-            copies.append(copy)
+            for copy in pieces(g, i, f * 64 + i * 16 + half * 8):
+                copy.start()
+    for copy in smalls:
+        copy.wait()
     count = lax.axis_size("elem")
     rank = lax.axis_index("elem")
-    square[...] = jnp.zeros((LANES, LANES), jnp.int32)
-    square[0:ELEMS, 0:5] = neighbours_ref[...]
-    turned = square[...].T[0:8, :]
     base = lane() % 32
-    turned = jnp.take_along_axis(turned, base, axis=1, mode="promise_in_bounds")
+    blank = jnp.zeros((ELEMS, LANES - 5), jnp.int32)
+    padded = jnp.concatenate([square[...], blank], axis=1)
+    turned = jnp.concatenate([padded] * 4, axis=0).T[0:8, :]
 
     def slots(values, first):
         block = lax.shift_right_logical(values, 5) - rank - first
@@ -324,34 +339,31 @@
     near = slots(turned, -1)
     for face in range(5):
         index_ref[face] = jnp.broadcast_to(near[face : face + 1], (8, LANES))
-    line = jnp.broadcast_to(partners_ref[pl.ds(rank // 4, 1), :], (8, LANES))
+    line = jnp.broadcast_to(line_ref[pl.ds(rank // 4, 1), :], (8, LANES))
     line = jnp.take_along_axis(line, base + (rank % 4) * 32, axis=1, mode="promise_in_bounds")
     index_ref[5] = slots(line, count // 4)
-    u = flipped(jnp.concatenate([u_ref[...]] * 4, axis=0))
+    u = flipped(jnp.concatenate([own[...]] * 4, axis=0))
     nodes_ref[...] = u
     acc_ref[...] = volume(u)
 
     def turn_group(g, carry):
         for i in range(4):
-            pltpu.make_async_copy(inv_ref.at[:, pl.ds(0, 8), :], buf.at[g, i], sems.at[g, i]).wait()
+            for copy in pieces(g, i, 0):
+                copy.wait()
         for r in range(8):
-            x = buf[g, :, :, r, :].reshape(LANES, UNK)
-            t_ref[g * 8 + r] = jnp.concatenate(
-                [
-                    x[:, 0:128].T,
-                    x[:, 128:256].T,
-                    jnp.concatenate([x[:, 256:320], x[:, 256:320]], axis=1).T[:64],
-                ],
-                axis=0,
-            )
+            rows = pl.ds(r, LANES, stride=8)
+            t_ref[g * 8 + r, 0:128] = wide.at[g, 0].reshape(1024, LANES)[rows, :].T
+            t_ref[g * 8 + r, 128:256] = wide.at[g, 1].reshape(1024, LANES)[rows, :].T
+            t_ref[g * 8 + r, 256:320] = tail[g, :, :, r, :].reshape(LANES, 64).T
         return carry
 
     lax.fori_loop(0, GROUPS, turn_group, 0)
 
 
-def first_kernel(t_ref, index_ref, nodes_ref, acc_ref, before_ref, own_ref, after_ref, ahead_ref, beyond_ref,
+def first_kernel(t_ref, index_ref, nodes_ref, acc_ref, beyond_ref, ahead_ref, after_ref, before_ref,
                  x_ref, nx_ref, ny_ref, nz_ref, v_ref):
-    near = flipped(jnp.concatenate([before_ref[...], own_ref[...], after_ref[...], own_ref[...]], axis=0))
+    near = flipped(jnp.concatenate([before_ref[...], before_ref[...], after_ref[...], after_ref[...]], axis=0))
+    near = jnp.where(lane() // 32 == 1, nodes_ref[...], near)
     far = flipped(jnp.concatenate([ahead_ref[...], beyond_ref[...]] * 2, axis=0))
     nx, ny, nz = aligned(near, far, index_ref[...])
     nx_ref[...], ny_ref[...], nz_ref[...] = nx, ny, nz
@@ -364,7 +376,7 @@
     multiply(t_ref, v_ref, x_ref, 1, finish)
 
 
-def second_kernel(t_ref, index_ref, before_ref, own_ref, after_ref, ahead_ref, beyond_ref,
+def second_kernel(t_ref, index_ref, beyond_ref, ahead_ref, own_ref, after_ref, before_ref,
                   y_ref, nx_ref, ny_ref, nz_ref, v_ref):
     near, far = near_far(before_ref[...], own_ref[...], after_ref[...], ahead_ref[...], beyond_ref[...])
     nx, ny, nz = aligned(near, far, index_ref[...])
@@ -377,38 +389,39 @@
     multiply(t_ref, v_ref, y_ref, 1, finish)
 
 
-def middle_kernel(u_ref, x_ref, y_ref, states_ref, acc_ref):
-    u = u_ref[...]
-    x, y = spread(x_ref[...]), spread(y_ref[...])
-    states = u + by_group(STEP_X) * x + by_group(STEP_Y) * y
-    states_ref[...] = states
-    acc_ref[...] = volume(states)
-
-
 def section_value(table, which):
     first = lax.axis_index("section") == 0
     return jnp.where(first, table[which], table[2 + which]).astype(jnp.float32)
 
 
-def third_kernel(t_ref, index_ref, u_ref, states_ref, acc_ref, x_ref,
-                 ux_ref, uy_ref, uz_ref, xx_ref, xy_ref, xz_ref,
-                 before_ref, own_ref, after_ref, ahead_ref, beyond_ref,
-                 first_ref, base_ref, v_ref):
+def middle_kernel(u_ref, x_ref, y_ref, ux_ref, uy_ref, uz_ref, xx_ref, xy_ref, xz_ref,
+                  states_ref, acc_ref, nx_ref, ny_ref, nz_ref, part_ref, base_ref):
+    u = u_ref[...]
+    x, y = spread(x_ref[...]), spread(y_ref[...])
+    a = by_group(STEP_X)
+    states = u + a * x + by_group(STEP_Y) * y
+    states_ref[...] = states
+    acc_ref[...] = volume(states)
+    nx_ref[...] = ux_ref[...] + a * xx_ref[...]
+    ny_ref[...] = uy_ref[...] + a * xy_ref[...]
+    nz_ref[...] = uz_ref[...] + a * xz_ref[...]
+    compact = squeezed(u)
+    for c in range(2):
+        part_ref[c] = -section_value(STEP_X, c) * x - section_value(STEP_Y, c) * y
+        base_ref[c] = compact + section_value(STEP_X, c) * x_ref[...] + section_value(STEP_Y, c) * y_ref[...]
+
+
+def third_kernel(t_ref, index_ref, states_ref, acc_ref, nx_ref, ny_ref, nz_ref, part_ref, base_ref,
+                 beyond_ref, ahead_ref, own_ref, after_ref, before_ref, first_ref, sum_ref, v_ref):
     near, far = near_far(before_ref[...], own_ref[...], after_ref[...], ahead_ref[...], beyond_ref[...])
     yx, yy, yz = aligned(near, far, index_ref[...])
-    a, b = by_group(STEP_X), by_group(STEP_Y)
-    nx = ux_ref[...] + a * xx_ref[...] + b * yx
-    ny = uy_ref[...] + a * xy_ref[...] + b * yy
-    nz = uz_ref[...] + a * xz_ref[...] + b * yz
-    total = (acc_ref[...] + face_terms(states_ref[...], nx, ny, nz)).reshape(UNK, LANES)
+    b = by_group(STEP_Y)
+    total = acc_ref[...] + face_terms(
+        states_ref[...], nx_ref[...] + b * yx, ny_ref[...] + b * yy, nz_ref[...] + b * yz
+    )
     turned = [total] + [roll_lanes(total, 32 * r) for r in (1, 2, 3)]
-    x, y = x_ref[...], own_ref[...]
-    xs, ys = spread(x).reshape(UNK, LANES), spread(y).reshape(UNK, LANES)
-    u = squeezed(u_ref[...])
-    shape = (UNK // 8, 8, LANES)
     for c in range(2):
-        v = -section_value(STEP_X, c) * xs - section_value(STEP_Y, c) * ys
-        v = v.reshape(shape)
+        v = part_ref[c]
         for r in range(4):
             factor = by_group(
                 [
@@ -416,18 +429,17 @@
                     for g in range(4)
                 ]
             )
-            v = v + factor * turned[r].reshape(shape)
+            v = v + factor * turned[r]
         v_ref[c] = v.reshape(UNK, LANES)
-        base_ref[c] = u + section_value(STEP_X, c) * x + section_value(STEP_Y, c) * y
 
     def finish(c, rows, value):
         first_ref[c, rows, :] = value
-        base_ref[c, rows, :] = base_ref[c, rows, :] + value
+        sum_ref[c, rows, :] = base_ref[c, rows, :] + value
 
     multiply(t_ref, v_ref, first_ref, 2, finish)
 
 
-def fourth_kernel(t_ref, index_ref, base_ref, before_ref, own_ref, after_ref, ahead_ref, beyond_ref, out_ref, v_ref, done_ref):
+def fourth_kernel(t_ref, index_ref, base_ref, beyond_ref, ahead_ref, own_ref, after_ref, before_ref, out_ref, v_ref, done_ref):
     for c in range(2):
         near, far = near_far(before_ref[c], own_ref[c], after_ref[c], ahead_ref[c], beyond_ref[c])
         v_ref[c] = lifted(*aligned(near, far, index_ref[...])).reshape(UNK, LANES)
@@ -480,9 +492,9 @@
 
 def exchanged(block):
     far = lax.axis_size("elem") // 4
-    before, after = passed(block, 1), passed(block, -1)
-    ahead, beyond = passed(block, -far), passed(block, -(far + 1))
-    return [before, block, after, ahead, beyond]
+    beyond, ahead = passed(block, -(far + 1)), passed(block, -far)
+    after, before = passed(block, -1), passed(block, 1)
+    return [beyond, ahead, block, after, before]
 
 
 def keep(x):
@@ -494,20 +506,24 @@
     u_all = exchanged(u_start)
     t, index, nodes, acc = call(
         prepare_kernel,
-        [pltpu.with_memory_space_constraint(inverses, pltpu.HBM), neighbours, partners, u_start],
+        [pltpu.with_memory_space_constraint(k, pltpu.HBM) for k in (inverses, neighbours, partners, u_start)],
         [vm((ROWS, UNK, LANES)), vm((6, 8, LANES), jnp.int32), vm(NODES), vm(NODES)],
         [
-            pltpu.VMEM((GROUPS, 4, ELEMS, 8, UNK), F32),
-            pltpu.VMEM((LANES, LANES), jnp.int32),
-            pltpu.SemaphoreType.DMA((GROUPS, 4)),
+            pltpu.VMEM((GROUPS, 2, 4, ELEMS, 8, LANES), F32),
+            pltpu.VMEM((GROUPS, 4, ELEMS, 8, 64), F32),
+            pltpu.VMEM((ELEMS, 5), jnp.int32),
+            pltpu.VMEM((partners.shape[0], LANES), jnp.int32),
+            pltpu.VMEM((ELEMS, UNK), F32),
+            pltpu.SemaphoreType.DMA((GROUPS, 4, 3)),
+            pltpu.SemaphoreType.DMA((3,)),
         ],
-        anywhere=(0,),
+        anywhere=(0, 1, 2, 3),
         flops=10**9,
         room=24,
     )
     t, index, nodes = keep(t), keep(index), keep(nodes)
     x, ux, uy, uz = call(
-        first_kernel, [t, index, nodes, keep(acc), *u_all],
+        first_kernel, [t, index, nodes, keep(acc), *u_all[:2], *u_all[3:]],
         [vm(COMPACT), vm(NX), vm(NODES), vm(NODES)], [pltpu.VMEM((1, UNK, LANES), F32)],
     )
     y, xx, xy, xz = call(
@@ -515,10 +531,14 @@
         [vm(COMPACT), vm(NX), vm(NODES), vm(NODES)], [pltpu.VMEM((1, UNK, LANES), F32)],
     )
     y_all = exchanged(y)
-    states, acc = call(middle_kernel, [nodes, x, y], [vm(NODES), vm(NODES)])
+    states, acc, nx, ny, nz, part, base = call(
+        middle_kernel,
+        [nodes, keep(x), keep(y), *[keep(k) for k in (ux, uy, uz, xx, xy, xz)]],
+        [vm(NODES), vm(NODES), vm(NX), vm(NODES), vm(NODES), vm((2,) + NODES), vm((2,) + COMPACT)],
+    )
     first, base = call(
         third_kernel,
-        [t, index, nodes, keep(states), keep(acc), x, *[keep(k) for k in (ux, uy, uz, xx, xy, xz)], *y_all],
+        [t, index, *[keep(k) for k in (states, acc, nx, ny, nz, part, base)], *y_all],
         [vm((2,) + COMPACT), vm((2,) + COMPACT)], [pltpu.VMEM((2, UNK, LANES), F32)],
     )
     [out] = call(

time: 62.5 us -> 69.4 us (1.11)
  starting transfers between devices: 19.4 us -> 27.4 us
  waiting for transfers between devices: 19.8 us -> 18.5 us
  Pallas kernels: 20.7 us -> 21.9 us
  local copies, waits for them, and re-layouts: 2.26 us -> 1.37 us
    ppermute x16, starting transfers between devices: 19.4 us -> 27.4 us  [passed(): lax.ppermute(block, 'elem', [((i - distance) % count, i) for i in range(c...]
    ppermute x16, waiting for transfers between devices: 19.8 us -> 18.5 us  [passed(): lax.ppermute(block, 'elem', [((i - distance) % count, i) for i in range(c...]
    pallas_call x6, Pallas kernels: 20.7 us -> 21.9 us  [call(): pl.pallas_call(kernel, out_shape=outputs, in_specs=in_specs, out_specs=[p...]
    unnamed x5 -> x1, local copies, waits for them, and re-layouts: 2.26 us -> 1.37 us
  transfers between devices with their start and end apart: 16 -> 16, of which waited for: 9 -> 6; matrix products, arithmetic and copies ran while one was open for 1% -> 2% of each run, Pallas kernels for 19% -> 19%
where the time goes in v1:
time: 69.4 us; the launch traced here: 69.3 us
  starting transfers between devices  27.4 us (39%)
  Pallas kernels  21.9 us (32%)
  waiting for transfers between devices  18.5 us (27%)
  local copies, waits for them, and re-layouts  1.37 us (2%)
    ppermute x16, starting transfers between devices, passed(): lax.ppermute(block, 'elem', [((i - distance) % count, i) for i in range(c...  27.4 us
    pallas_call x6, Pallas kernels, call(): pl.pallas_call(kernel, out_shape=outputs, in_specs=in_specs, out_specs=[p...  21.9 us
    ppermute x16, waiting for transfers between devices, passed(): lax.ppermute(block, 'elem', [((i - distance) % count, i) for i in range(c...  18.5 us
  transfers between devices with their start and end apart: 16, of which 6 were waited for; matrix products, arithmetic and copies ran while one was open for 2% of the time, Pallas kernels for 19%

profile of v1, /device:TPU:0, one launch (start us, length us, event | category | flops | bytes accessed | tf_op | source)
XLA Modules:
  0.0 69.3 jit_solution(10367836537168626609)
XLA Ops:
  0.0 6.6 %collective-permute-start = (f32[32,320]{1,0:T(8,128)}, f32[32,320]{1,0:T(8,128)S(1)}, u32[]{:S(2)}, u32[]{:S(2)}) collective-permute-start(f32[32,320]{1,0:T(8,128)} %u_ref.1), channel_id=1, source_target_pairs={{34,0},{36,2},{38,4},{40,6},{42,8},{44,10},{46,12},{48,14},{50,16}... | collective-permute-start | bytes 122888 | tf_op jit(solution)/shard_map/ppermute | solution.py:490
  6.6 0.7 %collective-permute-start.1 = (f32[32,320]{1,0:T(8,128)}, f32[32,320]{1,0:T(8,128)S(1)}, u32[]{:S(2)}, u32[]{:S(2)}) collective-permute-start(f32[32,320]{1,0:T(8,128)} %u_ref.1), channel_id=1, source_target_pairs={{32,0},{34,2},{36,4},{38,6},{40,8},{42,10},{44,12},{46,14},{48,16}... | collective-permute-start | bytes 122888 | tf_op jit(solution)/shard_map/ppermute | solution.py:490
  7.3 0.1 collective-permute-start.2
  7.5 0.4 collective-permute-start.3
  7.8 1.4 %copy.5.neighbours_ref = s32[32,5]{1,0:T(8,128)} copy(s32[32,5]{0,1:T(8,128)} %param.6) | data formatting | bytes 1280 | tf_op args[2]
  9.2 12.6 %shard_map.46 = (f32[80,320,128]{2,1,0:T(8,128)S(1)}, s32[6,8,128]{2,1,0:T(8,128)S(1)}, f32[5,4,2,8,128]{4,3,2,1,0:T(8,128)S(1)}, f32[5,4,2,8,128]{4,3,2,1,0:T(8,128)S(1)}) custom-call(f32[32,320,320]{2,1,0:T(8,128)} %inv_ref.1, s32[32,5]{1,0:T(8,128)} %copy.5.neighbours_ref, s32[16,128]{1,0:T(8,128)} %bitcast.1, f32[32,320]{1,0:T(8,128)} %u_ref.1), custom_call_target="tpu_custom_call" | custom-call | flops 1000000000 | bytes 1000000 | tf_op jit(solution)/shard_map/pallas_call | solution.py:473
  21.8 0.0 collective-permute-done.beyond_ref
  21.9 0.0 collective-permute-done.1.ahead_ref
  21.9 0.0 collective-permute-done.2.after_ref
  21.9 0.0 collective-permute-done.3.before_ref
  21.9 1.4 %shard_map.47 = (f32[80,128]{1,0:T(8,128)S(1)}, f32[5,2,2,8,128]{4,3,2,1,0:T(8,128)S(1)}, f32[5,4,2,8,128]{4,3,2,1,0:T(8,128)S(1)}, f32[5,4,2,8,128]{4,3,2,1,0:T(8,128)S(1)}) custom-call(f32[80,320,128]{2,1,0:T(8,128)S(1)} %get-tuple-element.26.t_ref, s32[6,8,128]{2,1,0:T(8,128)S(1)} %get-tuple-element.27.index_ref, ...), custom_call_target="tpu_custom_call" | custom-call | flops 10000000 | bytes 1000000 | tf_op jit(solution)/shard_map/pallas_call | solution.py:473
  23.3 4.0 %collective-permute-start.4 = (f32[80,128]{1,0:T(8,128)S(1)}, f32[80,128]{1,0:T(8,128)S(1)}, u32[]{:S(2)}, u32[]{:S(2)}) collective-permute-start(f32[80,128]{1,0:T(8,128)S(1)} %get-tuple-element.30.own_ref.x_ref), channel_id=1, source_target_pairs={{34,0},{36,2},{38,4},{40,6},{42,8},{44,10},{46,12},{48,14},{50,16}... | collective-permute-start | bytes 122888 | tf_op jit(solution)/shard_map/ppermute | solution.py:490
  27.3 4.5 %collective-permute-start.5 = (f32[80,128]{1,0:T(8,128)S(1)}, f32[80,128]{1,0:T(8,128)S(1)}, u32[]{:S(2)}, u32[]{:S(2)}) collective-permute-start(f32[80,128]{1,0:T(8,128)S(1)} %get-tuple-element.30.own_ref.x_ref), channel_id=1, source_target_pairs={{32,0},{34,2},{36,4},{38,6},{40,8},{42,10},{44,12},{46,14},{48,16}... | collective-permute-start | bytes 122888 | tf_op jit(solution)/shard_map/ppermute | solution.py:490
  31.8 0.0 collective-permute-start.6
  31.8 0.5 collective-permute-start.7
  32.3 0.0 collective-permute-done.4.beyond_ref
  32.3 1.2 %collective-permute-done.5.ahead_ref = f32[80,128]{1,0:T(8,128)S(1)} collective-permute-done((f32[80,128]{1,0:T(8,128)S(1)}, f32[80,128]{1,0:T(8,128)S(1)}, u32[]{:S(2)}, u32[]{:S(2)}) %collective-permute-start.5) | collective-permute-done | bytes 40992 | tf_op jit(solution)/shard_map/ppermute | solution.py:490
  33.4 0.0 collective-permute-done.6.after_ref
  33.4 6.0 %collective-permute-done.7.before_ref = f32[80,128]{1,0:T(8,128)S(1)} collective-permute-done((f32[80,128]{1,0:T(8,128)S(1)}, f32[80,128]{1,0:T(8,128)S(1)}, u32[]{:S(2)}, u32[]{:S(2)}) %collective-permute-start.7) | collective-permute-done | bytes 40992 | tf_op jit(solution)/shard_map/ppermute | solution.py:490
  39.4 1.4 %shard_map.48 = (f32[80,128]{1,0:T(8,128)S(1)}, f32[5,2,2,8,128]{4,3,2,1,0:T(8,128)S(1)}, f32[5,4,2,8,128]{4,3,2,1,0:T(8,128)S(1)}, f32[5,4,2,8,128]{4,3,2,1,0:T(8,128)S(1)}) custom-call(f32[80,320,128]{2,1,0:T(8,128)S(1)} %get-tuple-element.26.t_ref, s32[6,8,128]{2,1,0:T(8,128)S(1)} %get-tuple-element.27.index_ref, ...), custom_call_target="tpu_custom_call" | custom-call | flops 10000000 | bytes 1000000 | tf_op jit(solution)/shard_map/pallas_call | solution.py:473
  40.8 0.1 collective-permute-start.10
  40.9 0.5 collective-permute-start.11
  41.4 2.9 %collective-permute-start.8 = (f32[80,128]{1,0:T(8,128)S(1)}, f32[80,128]{1,0:T(8,128)S(1)}, u32[]{:S(2)}, u32[]{:S(2)}) collective-permute-start(f32[80,128]{1,0:T(8,128)S(1)} %get-tuple-element.31.y_ref.own_ref), channel_id=1, source_target_pairs={{34,0},{36,2},{38,4},{40,6},{42,8},{44,10},{46,12},{48,14},{50,16}... | collective-permute-start | bytes 122888 | tf_op jit(solution)/shard_map/ppermute | solution.py:490
  44.3 1.6 %collective-permute-start.9 = (f32[80,128]{1,0:T(8,128)S(1)}, f32[80,128]{1,0:T(8,128)S(1)}, u32[]{:S(2)}, u32[]{:S(2)}) collective-permute-start(f32[80,128]{1,0:T(8,128)S(1)} %get-tuple-element.31.y_ref.own_ref), channel_id=1, source_target_pairs={{32,0},{34,2},{36,4},{38,6},{40,8},{42,10},{44,12},{46,14},{48,16}... | collective-permute-start | bytes 122888 | tf_op jit(solution)/shard_map/ppermute | solution.py:490
  45.9 0.5 shard_map.49
  46.4 0.0 collective-permute-done.10.after_ref
  46.4 2.1 %collective-permute-done.11.before_ref = f32[80,128]{1,0:T(8,128)S(1)} collective-permute-done((f32[80,128]{1,0:T(8,128)S(1)}, f32[80,128]{1,0:T(8,128)S(1)}, u32[]{:S(2)}, u32[]{:S(2)}) %collective-permute-start.11) | collective-permute-done | bytes 40992 | tf_op jit(solution)/shard_map/ppermute | solution.py:490
  48.6 0.0 collective-permute-done.8.beyond_ref
  48.6 1.2 %collective-permute-done.9.ahead_ref = f32[80,128]{1,0:T(8,128)S(1)} collective-permute-done((f32[80,128]{1,0:T(8,128)S(1)}, f32[80,128]{1,0:T(8,128)S(1)}, u32[]{:S(2)}, u32[]{:S(2)}) %collective-permute-start.9) | collective-permute-done | bytes 40992 | tf_op jit(solution)/shard_map/ppermute | solution.py:490
  49.7 2.5 %shard_map.50 = (f32[2,80,128]{2,1,0:T(8,128)S(1)}, f32[2,80,128]{2,1,0:T(8,128)S(1)}) custom-call(f32[80,320,128]{2,1,0:T(8,128)S(1)} %get-tuple-element.26.t_ref, s32[6,8,128]{2,1,0:T(8,128)S(1)} %get-tuple-element.27.index_ref, f32[5,4,2,8,128]{4,3,2,1,0:T(8,128)S(1)} %get-tuple-element.38.states_ref, f32[5,4,2,8,128]{4,3,2,1,0:T(8,128)S(1)} %get-tuple-element.39.acc_ref, ...), custom_call_target="tpu_custom_call" | custom-call | flops 10000000 | bytes 1000000 | tf_op jit(solution)/shard_map/pallas_call | solution.py:473
  52.2 2.5 %collective-permute-start.12 = (f32[2,80,128]{2,1,0:T(8,128)S(1)}, f32[2,80,128]{2,1,0:T(8,128)S(1)}, u32[]{:S(2)}, u32[]{:S(2)}) collective-permute-start(f32[2,80,128]{2,1,0:T(8,128)S(1)} %get-tuple-element.46.own_ref), channel_id=1, source_target_pairs={{34,0},{36,2},{38,4},{40,6},{42,8},{44,10},{46,12},{48,14},{50,16}... | collective-permute-start | bytes 245768 | tf_op jit(solution)/shard_map/ppermute | solution.py:490
  54.8 1.6 %collective-permute-start.13 = (f32[2,80,128]{2,1,0:T(8,128)S(1)}, f32[2,80,128]{2,1,0:T(8,128)S(1)}, u32[]{:S(2)}, u32[]{:S(2)}) collective-permute-start(f32[2,80,128]{2,1,0:T(8,128)S(1)} %get-tuple-element.46.own_ref), channel_id=1, source_target_pairs={{32,0},{34,2},{36,4},{38,6},{40,8},{42,10},{44,12},{46,14},{48,16}... | collective-permute-start | bytes 245768 | tf_op jit(solution)/shard_map/ppermute | solution.py:490
  56.4 1.3 %collective-permute-start.14 = (f32[2,80,128]{2,1,0:T(8,128)S(1)}, f32[2,80,128]{2,1,0:T(8,128)S(1)}, u32[]{:S(2)}, u32[]{:S(2)}) collective-permute-start(f32[2,80,128]{2,1,0:T(8,128)S(1)} %get-tuple-element.46.own_ref), channel_id=1, source_target_pairs={{2,0},{4,2},{6,4},{8,6},{10,8},{12,10},{14,12},{16,14},{18,16},{20... | collective-permute-start | bytes 245768 | tf_op jit(solution)/shard_map/ppermute | solution.py:490
  57.7 0.0 collective-permute-start.15
  57.7 0.0 collective-permute-done.12.beyond_ref
  57.7 3.1 %collective-permute-done.13.ahead_ref = f32[2,80,128]{2,1,0:T(8,128)S(1)} collective-permute-done((f32[2,80,128]{2,1,0:T(8,128)S(1)}, f32[2,80,128]{2,1,0:T(8,128)S(1)}, u32[]{:S(2)}, u32[]{:S(2)}) %collective-permute-start.13) | collective-permute-done | bytes 81952 | tf_op jit(solution)/shard_map/ppermute | solution.py:490
  60.8 0.0 collective-permute-done.14.after_ref
  60.8 5.0 %collective-permute-done.15.before_ref = f32[2,80,128]{2,1,0:T(8,128)S(1)} collective-permute-done((f32[2,80,128]{2,1,0:T(8,128)S(1)}, f32[2,80,128]{2,1,0:T(8,128)S(1)}, u32[]{:S(2)}, u32[]{:S(2)}) %collective-permute-start.15) | collective-permute-done | bytes 81952 | tf_op jit(solution)/shard_map/ppermute | solution.py:490
  65.8 3.5 %shard_map.51 = f32[2,32,320]{2,1,0:T(8,128)} custom-call(f32[80,320,128]{2,1,0:T(8,128)S(1)} %get-tuple-element.26.t_ref, s32[6,8,128]{2,1,0:T(8,128)S(1)} %get-tuple-element.27.index_ref, f32[2,80,128]{2,1,0:T(8,128)S(1)} %get-tuple-element.45.base_ref, f32[2,80,128]{2,1,0:T(8,128)S(1)} %collective-permute-done.12.beyond_ref, ...), custom_call_target="tpu_custom_call" | custom-call | flops 10000000 | bytes 1000000 | tf_op jit(solution)/shard_map/pallas_call | solution.py:473
Async XLA Ops:
  0.0 21.9 %collective-permute-start = (f32[32,320]{1,0:T(8,128)}, f32[32,320]{1,0:T(8,128)S(1)}, u32[]{:S(2)}, u32[]{:S(2)}) collective-permute-start(f32[32,320]{1,0:T(8,128)} %u_ref.1), channel_id=1, source_target_pairs={{34,0},{36,2},{38,4},{40,6},{42,8},{44,10},{46,12},{48,14},{50,16}... | collective-permute-start | bytes 122888 | tf_op jit(solution)/shard_map/ppermute | solution.py:490
  6.6 15.3 %collective-permute-start.1 = (f32[32,320]{1,0:T(8,128)}, f32[32,320]{1,0:T(8,128)S(1)}, u32[]{:S(2)}, u32[]{:S(2)}) collective-permute-start(f32[32,320]{1,0:T(8,128)} %u_ref.1), channel_id=1, source_target_pairs={{32,0},{34,2},{36,4},{38,6},{40,8},{42,10},{44,12},{46,14},{48,16}... | collective-permute-start | bytes 122888 | tf_op jit(solution)/shard_map/ppermute | solution.py:490
  7.3 14.6 %collective-permute-start.2 = (f32[32,320]{1,0:T(8,128)}, f32[32,320]{1,0:T(8,128)S(1)}, u32[]{:S(2)}, u32[]{:S(2)}) collective-permute-start(f32[32,320]{1,0:T(8,128)} %u_ref.1), channel_id=1, source_target_pairs={{2,0},{4,2},{6,4},{8,6},{10,8},{12,10},{14,12},{16,14},{18,16},{20... | collective-permute-start | bytes 122888 | tf_op jit(solution)/shard_map/ppermute | solution.py:490
  7.5 14.4 %collective-permute-start.3 = (f32[32,320]{1,0:T(8,128)}, f32[32,320]{1,0:T(8,128)S(1)}, u32[]{:S(2)}, u32[]{:S(2)}) collective-permute-start(f32[32,320]{1,0:T(8,128)} %u_ref.1), channel_id=1, source_target_pairs={{126,0},{0,2},{2,4},{4,6},{6,8},{8,10},{10,12},{12,14},{14,16},{16... | collective-permute-start | bytes 122888 | tf_op jit(solution)/shard_map/ppermute | solution.py:490
  23.3 9.0 %collective-permute-start.4 = (f32[80,128]{1,0:T(8,128)S(1)}, f32[80,128]{1,0:T(8,128)S(1)}, u32[]{:S(2)}, u32[]{:S(2)}) collective-permute-start(f32[80,128]{1,0:T(8,128)S(1)} %get-tuple-element.30.own_ref.x_ref), channel_id=1, source_target_pairs={{34,0},{36,2},{38,4},{40,6},{42,8},{44,10},{46,12},{48,14},{50,16}... | collective-permute-start | bytes 122888 | tf_op jit(solution)/shard_map/ppermute | solution.py:490
  27.3 6.2 %collective-permute-start.5 = (f32[80,128]{1,0:T(8,128)S(1)}, f32[80,128]{1,0:T(8,128)S(1)}, u32[]{:S(2)}, u32[]{:S(2)}) collective-permute-start(f32[80,128]{1,0:T(8,128)S(1)} %get-tuple-element.30.own_ref.x_ref), channel_id=1, source_target_pairs={{32,0},{34,2},{36,4},{38,6},{40,8},{42,10},{44,12},{46,14},{48,16}... | collective-permute-start | bytes 122888 | tf_op jit(solution)/shard_map/ppermute | solution.py:490
  31.8 1.7 %collective-permute-start.6 = (f32[80,128]{1,0:T(8,128)S(1)}, f32[80,128]{1,0:T(8,128)S(1)}, u32[]{:S(2)}, u32[]{:S(2)}) collective-permute-start(f32[80,128]{1,0:T(8,128)S(1)} %get-tuple-element.30.own_ref.x_ref), channel_id=1, source_target_pairs={{2,0},{4,2},{6,4},{8,6},{10,8},{12,10},{14,12},{16,14},{18,16},{20... | collective-permute-start | bytes 122888 | tf_op jit(solution)/shard_map/ppermute | solution.py:490
  31.8 7.6 %collective-permute-start.7 = (f32[80,128]{1,0:T(8,128)S(1)}, f32[80,128]{1,0:T(8,128)S(1)}, u32[]{:S(2)}, u32[]{:S(2)}) collective-permute-start(f32[80,128]{1,0:T(8,128)S(1)} %get-tuple-element.30.own_ref.x_ref), channel_id=1, source_target_pairs={{126,0},{0,2},{2,4},{4,6},{6,8},{8,10},{10,12},{12,14},{14,16},{16... | collective-permute-start | bytes 122888 | tf_op jit(solution)/shard_map/ppermute | solution.py:490
  40.8 5.6 %collective-permute-start.10 = (f32[80,128]{1,0:T(8,128)S(1)}, f32[80,128]{1,0:T(8,128)S(1)}, u32[]{:S(2)}, u32[]{:S(2)}) collective-permute-start(f32[80,128]{1,0:T(8,128)S(1)} %get-tuple-element.31.y_ref.own_ref), channel_id=1, source_target_pairs={{2,0},{4,2},{6,4},{8,6},{10,8},{12,10},{14,12},{16,14},{18,16},{20... | collective-permute-start | bytes 122888 | tf_op jit(solution)/shard_map/ppermute | solution.py:490
  40.9 7.7 %collective-permute-start.11 = (f32[80,128]{1,0:T(8,128)S(1)}, f32[80,128]{1,0:T(8,128)S(1)}, u32[]{:S(2)}, u32[]{:S(2)}) collective-permute-start(f32[80,128]{1,0:T(8,128)S(1)} %get-tuple-element.31.y_ref.own_ref), channel_id=1, source_target_pairs={{126,0},{0,2},{2,4},{4,6},{6,8},{8,10},{10,12},{12,14},{14,16},{16... | collective-permute-start | bytes 122888 | tf_op jit(solution)/shard_map/ppermute | solution.py:490
  41.4 7.2 %collective-permute-start.8 = (f32[80,128]{1,0:T(8,128)S(1)}, f32[80,128]{1,0:T(8,128)S(1)}, u32[]{:S(2)}, u32[]{:S(2)}) collective-permute-start(f32[80,128]{1,0:T(8,128)S(1)} %get-tuple-element.31.y_ref.own_ref), channel_id=1, source_target_pairs={{34,0},{36,2},{38,4},{40,6},{42,8},{44,10},{46,12},{48,14},{50,16}... | collective-permute-start | bytes 122888 | tf_op jit(solution)/shard_map/ppermute | solution.py:490
  44.3 5.5 %collective-permute-start.9 = (f32[80,128]{1,0:T(8,128)S(1)}, f32[80,128]{1,0:T(8,128)S(1)}, u32[]{:S(2)}, u32[]{:S(2)}) collective-permute-start(f32[80,128]{1,0:T(8,128)S(1)} %get-tuple-element.31.y_ref.own_ref), channel_id=1, source_target_pairs={{32,0},{34,2},{36,4},{38,6},{40,8},{42,10},{44,12},{46,14},{48,16}... | collective-permute-start | bytes 122888 | tf_op jit(solution)/shard_map/ppermute | solution.py:490
  52.2 5.5 %collective-permute-start.12 = (f32[2,80,128]{2,1,0:T(8,128)S(1)}, f32[2,80,128]{2,1,0:T(8,128)S(1)}, u32[]{:S(2)}, u32[]{:S(2)}) collective-permute-start(f32[2,80,128]{2,1,0:T(8,128)S(1)} %get-tuple-element.46.own_ref), channel_id=1, source_target_pairs={{34,0},{36,2},{38,4},{40,6},{42,8},{44,10},{46,12},{48,14},{50,16}... | collective-permute-start | bytes 245768 | tf_op jit(solution)/shard_map/ppermute | solution.py:490
  54.8 6.0 %collective-permute-start.13 = (f32[2,80,128]{2,1,0:T(8,128)S(1)}, f32[2,80,128]{2,1,0:T(8,128)S(1)}, u32[]{:S(2)}, u32[]{:S(2)}) collective-permute-start(f32[2,80,128]{2,1,0:T(8,128)S(1)} %get-tuple-element.46.own_ref), channel_id=1, source_target_pairs={{32,0},{34,2},{36,4},{38,6},{40,8},{42,10},{44,12},{46,14},{48,16}... | collective-permute-start | bytes 245768 | tf_op jit(solution)/shard_map/ppermute | solution.py:490
  56.4 4.4 %collective-permute-start.14 = (f32[2,80,128]{2,1,0:T(8,128)S(1)}, f32[2,80,128]{2,1,0:T(8,128)S(1)}, u32[]{:S(2)}, u32[]{:S(2)}) collective-permute-start(f32[2,80,128]{2,1,0:T(8,128)S(1)} %get-tuple-element.46.own_ref), channel_id=1, source_target_pairs={{2,0},{4,2},{6,4},{8,6},{10,8},{12,10},{14,12},{16,14},{18,16},{20... | collective-permute-start | bytes 245768 | tf_op jit(solution)/shard_map/ppermute | solution.py:490
  57.7 8.1 %collective-permute-start.15 = (f32[2,80,128]{2,1,0:T(8,128)S(1)}, f32[2,80,128]{2,1,0:T(8,128)S(1)}, u32[]{:S(2)}, u32[]{:S(2)}) collective-permute-start(f32[2,80,128]{2,1,0:T(8,128)S(1)} %get-tuple-element.46.own_ref), channel_id=1, source_target_pairs={{126,0},{0,2},{2,4},{4,6},{6,8},{8,10},{10,12},{12,14},{14,16},{16... | collective-permute-start | bytes 245768 | tf_op jit(solution)/shard_map/ppermute | solution.py:490

commit v2 on v1

--- a/solution.py
+++ b/solution.py
@@ -14,6 +14,7 @@
 ROWS = 80
 LANES = 128
 GROUPS = 10
+EARLY = 3
 SECTIONS = 4
 
 time_step = 0.03
@@ -75,6 +76,8 @@
 STEP_X = [time_step * ROW_SUM[i] for i in range(SECTIONS)]
 STEP_Y = [time_step * ROW_SUM[i] * COUPLING[i] for i in range(SECTIONS)]
 
+ORDERS = [('ahead', 'after', 'before', 'beyond'), ('beyond', 'ahead', 'after', 'before'), ('after', 'before', 'beyond', 'ahead'), ('beyond', 'ahead', 'after', 'before')]
+
 
 def sublane():
     return lax.broadcasted_iota(jnp.int32, (8, LANES), 0)
@@ -253,7 +256,7 @@
     return out
 
 
-def near_far(before, own, after, ahead, beyond):
+def near_far(own, before, after, ahead, beyond):
     near = nodes_of([group_of([before, own, after], [i] * 3) for i in range(4)])
     far = nodes_of([group_of([ahead, beyond], [i] * 2) for i in range(4)])
     return near, far
@@ -320,32 +323,6 @@
         for i in range(4):
             for copy in pieces(g, i, f * 64 + i * 16 + half * 8):
                 copy.start()
-    for copy in smalls:
-        copy.wait()
-    count = lax.axis_size("elem")
-    rank = lax.axis_index("elem")
-    base = lane() % 32
-    blank = jnp.zeros((ELEMS, LANES - 5), jnp.int32)
-    padded = jnp.concatenate([square[...], blank], axis=1)
-    turned = jnp.concatenate([padded] * 4, axis=0).T[0:8, :]
-
-    def slots(values, first):
-        block = lax.shift_right_logical(values, 5) - rank - first
-        block = jnp.where(block < 0, block + count, block)
-        block = jnp.where(block < 0, block + count, block)
-        block = jnp.where(block >= count, block - count, block)
-        return block * ELEMS + (values & 31)
-
-    near = slots(turned, -1)
-    for face in range(5):
-        index_ref[face] = jnp.broadcast_to(near[face : face + 1], (8, LANES))
-    line = jnp.broadcast_to(line_ref[pl.ds(rank // 4, 1), :], (8, LANES))
-    line = jnp.take_along_axis(line, base + (rank % 4) * 32, axis=1, mode="promise_in_bounds")
-    index_ref[5] = slots(line, count // 4)
-    u = flipped(jnp.concatenate([own[...]] * 4, axis=0))
-    nodes_ref[...] = u
-    acc_ref[...] = volume(u)
-
     def turn_group(g, carry):
         for i in range(4):
             for copy in pieces(g, i, 0):
@@ -357,14 +334,39 @@
             t_ref[g * 8 + r, 256:320] = tail[g, :, :, r, :].reshape(LANES, 64).T
         return carry
 
-    lax.fori_loop(0, GROUPS, turn_group, 0)
-
-
-def first_kernel(t_ref, index_ref, nodes_ref, acc_ref, beyond_ref, ahead_ref, after_ref, before_ref,
+    lax.fori_loop(0, EARLY, turn_group, 0)
+    for copy in smalls:
+        copy.wait()
+    count = lax.axis_size("elem")
+    rank = lax.axis_index("elem")
+    base = lane() % 32
+    turned = jnp.concatenate([square[...]] * 4, axis=1)
+
+    def slots(values, first):
+        block = lax.shift_right_logical(values, 5) - rank - first
+        block = jnp.where(block < 0, block + count, block)
+        block = jnp.where(block < 0, block + count, block)
+        block = jnp.where(block >= count, block - count, block)
+        return block * ELEMS + (values & 31)
+
+    near = slots(turned, -1)
+    for face in range(5):
+        index_ref[face] = jnp.broadcast_to(near[face : face + 1], (8, LANES))
+    line = jnp.broadcast_to(line_ref[pl.ds(rank // 4, 1), :], (8, LANES))
+    line = jnp.take_along_axis(line, base + (rank % 4) * 32, axis=1, mode="promise_in_bounds")
+    index_ref[5] = slots(line, count // 4)
+    u = flipped(jnp.concatenate([own[...]] * 4, axis=0))
+    nodes_ref[...] = u
+    acc_ref[...] = volume(u)
+    lax.fori_loop(EARLY, GROUPS, turn_group, 0)
+
+
+def first_kernel(t_ref, index_ref, nodes_ref, acc_ref, moved,
                  x_ref, nx_ref, ny_ref, nz_ref, v_ref):
-    near = flipped(jnp.concatenate([before_ref[...], before_ref[...], after_ref[...], after_ref[...]], axis=0))
+    before, after, ahead, beyond = pulled(moved)
+    near = flipped(jnp.concatenate([before, before, after, after], axis=0))
     near = jnp.where(lane() // 32 == 1, nodes_ref[...], near)
-    far = flipped(jnp.concatenate([ahead_ref[...], beyond_ref[...]] * 2, axis=0))
+    far = flipped(jnp.concatenate([ahead, beyond] * 2, axis=0))
     nx, ny, nz = aligned(near, far, index_ref[...])
     nx_ref[...], ny_ref[...], nz_ref[...] = nx, ny, nz
     total = acc_ref[...] + face_terms(nodes_ref[...], nx, ny, nz)
@@ -376,9 +378,9 @@
     multiply(t_ref, v_ref, x_ref, 1, finish)
 
 
-def second_kernel(t_ref, index_ref, beyond_ref, ahead_ref, own_ref, after_ref, before_ref,
+def second_kernel(t_ref, index_ref, own_ref, moved,
                   y_ref, nx_ref, ny_ref, nz_ref, v_ref):
-    near, far = near_far(before_ref[...], own_ref[...], after_ref[...], ahead_ref[...], beyond_ref[...])
+    near, far = near_far(own_ref[...], *pulled(moved))
     nx, ny, nz = aligned(near, far, index_ref[...])
     nx_ref[...], ny_ref[...], nz_ref[...] = nx, ny, nz
     v_ref[0] = lifted(nx, ny, nz).reshape(UNK, LANES)
@@ -412,8 +414,8 @@
 
 
 def third_kernel(t_ref, index_ref, states_ref, acc_ref, nx_ref, ny_ref, nz_ref, part_ref, base_ref,
-                 beyond_ref, ahead_ref, own_ref, after_ref, before_ref, first_ref, sum_ref, v_ref):
-    near, far = near_far(before_ref[...], own_ref[...], after_ref[...], ahead_ref[...], beyond_ref[...])
+                 own_ref, moved, first_ref, sum_ref, v_ref):
+    near, far = near_far(own_ref[...], *pulled(moved))
     yx, yy, yz = aligned(near, far, index_ref[...])
     b = by_group(STEP_Y)
     total = acc_ref[...] + face_terms(
@@ -439,9 +441,9 @@
     multiply(t_ref, v_ref, first_ref, 2, finish)
 
 
-def fourth_kernel(t_ref, index_ref, base_ref, beyond_ref, ahead_ref, own_ref, after_ref, before_ref, out_ref, v_ref, done_ref):
+def fourth_kernel(t_ref, index_ref, base_ref, own_ref, moved, out_ref, v_ref, done_ref):
     for c in range(2):
-        near, far = near_far(before_ref[c], own_ref[c], after_ref[c], ahead_ref[c], beyond_ref[c])
+        near, far = near_far(own_ref[c], *pulled(moved, c))
         v_ref[c] = lifted(*aligned(near, far, index_ref[...])).reshape(UNK, LANES)
 
     def finish(c, rows, value):
@@ -485,16 +487,40 @@
     return pltpu.VMEM(shape, dtype)
 
 
-def passed(block, distance):
-    count = lax.axis_size("elem")
-    return lax.ppermute(block, "elem", [((i - distance) % count, i) for i in range(count)])
-
-
-def exchanged(block):
-    far = lax.axis_size("elem") // 4
-    beyond, ahead = passed(block, -(far + 1)), passed(block, -far)
-    after, before = passed(block, -1), passed(block, 1)
-    return [beyond, ahead, block, after, before]
+def routes(count):
+    far = count // 4
+    return {
+        "before": [(i - 1) % count for i in range(count)],
+        "after": [(i + 1) % count for i in range(count)],
+        "inner": [i ^ 1 for i in range(count)],
+        "outer": [(i - 1 + 2 * (i % 2)) % count for i in range(count)],
+        "ahead": [(i + far) % count for i in range(count)],
+        "beyond": [(i + far + 1) % count for i in range(count)],
+    }
+
+
+def pulled(moved, at=Ellipsis):
+    got = {name: ref[at] for name, ref in moved.items()}
+    if "inner" in got:
+        odd = lax.axis_index("elem") % 2 == 1
+        got["before"] = jnp.where(odd, got["inner"], got["outer"])
+        got["after"] = jnp.where(odd, got["outer"], got["inner"])
+    return got["before"], got["after"], got["ahead"], got["beyond"]
+
+
+def exchanged(block, order):
+    table = routes(lax.axis_size("elem"))
+    return {name: lax.ppermute(block, "elem", [(s, i) for i, s in enumerate(table[name])]) for name in order}
+
+
+def with_moved(kernel, inputs, moved, outputs, scratch):
+    count = len(inputs)
+    names = list(moved)
+
+    def whole(*refs):
+        kernel(*refs[:count], dict(zip(names, refs[count:])), *refs[count + len(names) :])
+
+    return call(whole, [*inputs, *moved.values()], outputs, scratch)
 
 
 def keep(x):
@@ -503,15 +529,15 @@
 
 def on_device(u_start, inverses, neighbours, partners):
     partners = partners.reshape(-1, LANES)
-    u_all = exchanged(u_start)
+    u_moved = exchanged(u_start, ORDERS[0])
     t, index, nodes, acc = call(
         prepare_kernel,
-        [pltpu.with_memory_space_constraint(k, pltpu.HBM) for k in (inverses, neighbours, partners, u_start)],
+        [pltpu.with_memory_space_constraint(k, pltpu.HBM) for k in (inverses, neighbours.T, partners, u_start)],
         [vm((ROWS, UNK, LANES)), vm((6, 8, LANES), jnp.int32), vm(NODES), vm(NODES)],
         [
             pltpu.VMEM((GROUPS, 2, 4, ELEMS, 8, LANES), F32),
             pltpu.VMEM((GROUPS, 4, ELEMS, 8, 64), F32),
-            pltpu.VMEM((ELEMS, 5), jnp.int32),
+            pltpu.VMEM((5, ELEMS), jnp.int32),
             pltpu.VMEM((partners.shape[0], LANES), jnp.int32),
             pltpu.VMEM((ELEMS, UNK), F32),
             pltpu.SemaphoreType.DMA((GROUPS, 4, 3)),
@@ -522,27 +548,27 @@
         room=24,
     )
     t, index, nodes = keep(t), keep(index), keep(nodes)
-    x, ux, uy, uz = call(
-        first_kernel, [t, index, nodes, keep(acc), *u_all[:2], *u_all[3:]],
-        [vm(COMPACT), vm(NX), vm(NODES), vm(NODES)], [pltpu.VMEM((1, UNK, LANES), F32)],
-    )
-    y, xx, xy, xz = call(
-        second_kernel, [t, index, *exchanged(x)],
-        [vm(COMPACT), vm(NX), vm(NODES), vm(NODES)], [pltpu.VMEM((1, UNK, LANES), F32)],
-    )
-    y_all = exchanged(y)
+    single = [pltpu.VMEM((1, UNK, LANES), F32)]
+    faces = [vm(COMPACT), vm(NX), vm(NODES), vm(NODES)]
+    x, ux, uy, uz = with_moved(first_kernel, [t, index, nodes, keep(acc)], u_moved, faces, single)
+    y, xx, xy, xz = with_moved(second_kernel, [t, index, x], exchanged(x, ORDERS[1]), faces, single)
+    y_moved = exchanged(y, ORDERS[2])
     states, acc, nx, ny, nz, part, base = call(
         middle_kernel,
         [nodes, keep(x), keep(y), *[keep(k) for k in (ux, uy, uz, xx, xy, xz)]],
         [vm(NODES), vm(NODES), vm(NX), vm(NODES), vm(NODES), vm((2,) + NODES), vm((2,) + COMPACT)],
     )
-    first, base = call(
+    first, base = with_moved(
         third_kernel,
-        [t, index, *[keep(k) for k in (states, acc, nx, ny, nz, part, base)], *y_all],
-        [vm((2,) + COMPACT), vm((2,) + COMPACT)], [pltpu.VMEM((2, UNK, LANES), F32)],
-    )
-    [out] = call(
-        fourth_kernel, [t, index, keep(base), *exchanged(first)],
+        [t, index, *[keep(k) for k in (states, acc, nx, ny, nz, part, base)], y],
+        y_moved,
+        [vm((2,) + COMPACT), vm((2,) + COMPACT)],
+        [pltpu.VMEM((2, UNK, LANES), F32)],
+    )
+    [out] = with_moved(
+        fourth_kernel,
+        [t, index, keep(base), first],
+        exchanged(first, ORDERS[3]),
         [jax.ShapeDtypeStruct((2, ELEMS, UNK), F32)],
         [pltpu.VMEM((2, UNK, LANES), F32), pltpu.VMEM((2,) + COMPACT, F32)],
     )

time: 69.4 us -> 59.5 us (0.86)
  starting transfers between devices: 27.4 us -> 19.4 us
  Pallas kernels: 21.9 us -> 20.2 us
  local copies, waits for them, and re-layouts: 1.37 us -> 0 us
  waiting for transfers between devices: 18.5 us -> 19.7 us
    ppermute x16, starting transfers between devices: 27.4 us -> 19.4 us  [exchanged(): lax.ppermute(block, 'elem', [(s, i) for i, s in enumerate(table[name])])]
    pallas_call x6, Pallas kernels: 21.9 us -> 20.2 us  [call(): pl.pallas_call(kernel, out_shape=outputs, in_specs=in_specs, out_specs=[p...]
    unnamed x1 -> x0, local copies, waits for them, and re-layouts: 1.37 us -> none
    ppermute x16, waiting for transfers between devices: 18.5 us -> 19.7 us  [exchanged(): lax.ppermute(block, 'elem', [(s, i) for i, s in enumerate(table[name])])]
  transfers between devices with their start and end apart: 16 -> 16, of which waited for: 6 -> 9; matrix products, arithmetic and copies ran while one was open for 2% -> 0% of each run, Pallas kernels for 19% -> 19%
where the time goes in v2:
time: 59.5 us; the launch traced here: 59.4 us
  Pallas kernels  20.2 us (34%)
  waiting for transfers between devices  19.7 us (33%)
  starting transfers between devices  19.4 us (33%)
    pallas_call x6, Pallas kernels, call(): pl.pallas_call(kernel, out_shape=outputs, in_specs=in_specs, out_specs=[p...  20.2 us
    ppermute x16, waiting for transfers between devices, exchanged(): lax.ppermute(block, 'elem', [(s, i) for i, s in enumerate(table[name])])  19.7 us
    ppermute x16, starting transfers between devices, exchanged(): lax.ppermute(block, 'elem', [(s, i) for i, s in enumerate(table[name])])  19.4 us
  transfers between devices with their start and end apart: 16, of which 9 were waited for; matrix products, arithmetic and copies ran while one was open for 0% of the time, Pallas kernels for 19%

profile of v2, /device:TPU:0, one launch (start us, length us, event | category | flops | bytes accessed | tf_op | source)
XLA Modules:
  0.0 59.4 jit_solution(17832281260938422695)
XLA Ops:
  0.0 4.1 %collective-permute-start = (f32[32,320]{1,0:T(8,128)}, f32[32,320]{1,0:T(8,128)S(1)}, u32[]{:S(2)}, u32[]{:S(2)}) collective-permute-start(f32[32,320]{1,0:T(8,128)} %u_ref.1), channel_id=1, source_target_pairs={{32,0},{34,2},{36,4},{38,6},{40,8},{42,10},{44,12},{46,14},{48,16}... | collective-permute-start | bytes 122888 | tf_op jit(solution)/shard_map/ppermute | solution.py:513
  4.1 2.8 %collective-permute-start.1 = (f32[32,320]{1,0:T(8,128)}, f32[32,320]{1,0:T(8,128)S(1)}, u32[]{:S(2)}, u32[]{:S(2)}) collective-permute-start(f32[32,320]{1,0:T(8,128)} %u_ref.1), channel_id=1, source_target_pairs={{2,0},{4,2},{6,4},{8,6},{10,8},{12,10},{14,12},{16,14},{18,16},{20... | collective-permute-start | bytes 122888 | tf_op jit(solution)/shard_map/ppermute | solution.py:513
  6.9 0.0 collective-permute-start.2
  6.9 4.5 %collective-permute-start.3 = (f32[32,320]{1,0:T(8,128)}, f32[32,320]{1,0:T(8,128)S(1)}, u32[]{:S(2)}, u32[]{:S(2)}) collective-permute-start(f32[32,320]{1,0:T(8,128)} %u_ref.1), channel_id=1, source_target_pairs={{34,0},{36,2},{38,4},{40,6},{42,8},{44,10},{46,12},{48,14},{50,16}... | collective-permute-start | bytes 122888 | tf_op jit(solution)/shard_map/ppermute | solution.py:513
  11.4 10.9 %shard_map.46 = (f32[80,320,128]{2,1,0:T(8,128)S(1)}, s32[6,8,128]{2,1,0:T(8,128)S(1)}, f32[5,4,2,8,128]{4,3,2,1,0:T(8,128)S(1)}, f32[5,4,2,8,128]{4,3,2,1,0:T(8,128)S(1)}) custom-call(f32[32,320,320]{2,1,0:T(8,128)} %inv_ref.1, s32[5,32]{1,0:T(8,128)} %bitcast.3, s32[16,128]{1,0:T(8,128)} %bitcast.2, f32[32,320]{1,0:T(8,128)} %u_ref.1), custom_call_target="tpu_custom_call" | custom-call | flops 1000000000 | bytes 1000000 | tf_op jit(solution)/shard_map/pallas_call | solution.py:475
  22.3 0.0 collective-permute-done.refs_4_
  22.3 0.0 collective-permute-done.1.refs_5_
  22.3 0.0 collective-permute-done.2.refs_6_
  22.4 0.0 collective-permute-done.3.refs_7_
  22.4 1.4 %shard_map.47 = (f32[80,128]{1,0:T(8,128)S(1)}, f32[5,2,2,8,128]{4,3,2,1,0:T(8,128)S(1)}, f32[5,4,2,8,128]{4,3,2,1,0:T(8,128)S(1)}, f32[5,4,2,8,128]{4,3,2,1,0:T(8,128)S(1)}) custom-call(f32[80,320,128]{2,1,0:T(8,128)S(1)} %get-tuple-element.26.refs_0_, s32[6,8,128]{2,1,0:T(8,128)S(1)} %get-tuple-element.27.refs_1_, ...), custom_call_target="tpu_custom_call" | custom-call | flops 10000000 | bytes 1000000 | tf_op jit(solution)/shard_map/pallas_call | solution.py:475
  23.8 0.1 collective-permute-start.4
  23.8 0.9 %collective-permute-start.5 = (f32[80,128]{1,0:T(8,128)S(1)}, f32[80,128]{1,0:T(8,128)S(1)}, u32[]{:S(2)}, u32[]{:S(2)}) collective-permute-start(f32[80,128]{1,0:T(8,128)S(1)} %get-tuple-element.30.refs_2_.x_ref), channel_id=1, source_target_pairs={{32,0},{34,2},{36,4},{38,6},{40,8},{42,10},{44,12},{46,14},{48,16}... | collective-permute-start | bytes 122888 | tf_op jit(solution)/shard_map/ppermute | solution.py:513
  24.7 0.8 %collective-permute-start.6 = (f32[80,128]{1,0:T(8,128)S(1)}, f32[80,128]{1,0:T(8,128)S(1)}, u32[]{:S(2)}, u32[]{:S(2)}) collective-permute-start(f32[80,128]{1,0:T(8,128)S(1)} %get-tuple-element.30.refs_2_.x_ref), channel_id=1, source_target_pairs={{2,0},{4,2},{6,4},{8,6},{10,8},{12,10},{14,12},{16,14},{18,16},{20... | collective-permute-start | bytes 122888 | tf_op jit(solution)/shard_map/ppermute | solution.py:513
  25.5 2.2 %collective-permute-start.7 = (f32[80,128]{1,0:T(8,128)S(1)}, f32[80,128]{1,0:T(8,128)S(1)}, u32[]{:S(2)}, u32[]{:S(2)}) collective-permute-start(f32[80,128]{1,0:T(8,128)S(1)} %get-tuple-element.30.refs_2_.x_ref), channel_id=1, source_target_pairs={{126,0},{0,2},{2,4},{4,6},{6,8},{8,10},{10,12},{12,14},{14,16},{16... | collective-permute-start | bytes 122888 | tf_op jit(solution)/shard_map/ppermute | solution.py:513
  27.6 0.0 collective-permute-done.4.refs_3_
  27.6 0.6 %collective-permute-done.5.refs_4_ = f32[80,128]{1,0:T(8,128)S(1)} collective-permute-done((f32[80,128]{1,0:T(8,128)S(1)}, f32[80,128]{1,0:T(8,128)S(1)}, u32[]{:S(2)}, u32[]{:S(2)}) %collective-permute-start.5) | collective-permute-done | bytes 40992 | tf_op jit(solution)/shard_map/ppermute | solution.py:513
  28.2 0.1 collective-permute-done.6.refs_5_
  28.3 4.8 %collective-permute-done.7.refs_6_ = f32[80,128]{1,0:T(8,128)S(1)} collective-permute-done((f32[80,128]{1,0:T(8,128)S(1)}, f32[80,128]{1,0:T(8,128)S(1)}, u32[]{:S(2)}, u32[]{:S(2)}) %collective-permute-start.7) | collective-permute-done | bytes 40992 | tf_op jit(solution)/shard_map/ppermute | solution.py:513
  33.1 1.4 %shard_map.48 = (f32[80,128]{1,0:T(8,128)S(1)}, f32[5,2,2,8,128]{4,3,2,1,0:T(8,128)S(1)}, f32[5,4,2,8,128]{4,3,2,1,0:T(8,128)S(1)}, f32[5,4,2,8,128]{4,3,2,1,0:T(8,128)S(1)}) custom-call(f32[80,320,128]{2,1,0:T(8,128)S(1)} %get-tuple-element.26.refs_0_, s32[6,8,128]{2,1,0:T(8,128)S(1)} %get-tuple-element.27.refs_1_, ...), custom_call_target="tpu_custom_call" | custom-call | flops 10000000 | bytes 1000000 | tf_op jit(solution)/shard_map/pallas_call | solution.py:475
  34.5 0.7 %collective-permute-start.10 = (f32[80,128]{1,0:T(8,128)S(1)}, f32[80,128]{1,0:T(8,128)S(1)}, u32[]{:S(2)}, u32[]{:S(2)}) collective-permute-start(f32[80,128]{1,0:T(8,128)S(1)} %get-tuple-element.31.y_ref.refs_9_), channel_id=1, source_target_pairs={{34,0},{36,2},{38,4},{40,6},{42,8},{44,10},{46,12},{48,14},{50,16}... | collective-permute-start | bytes 122888 | tf_op jit(solution)/shard_map/ppermute | solution.py:513
  35.2 1.6 %collective-permute-start.11 = (f32[80,128]{1,0:T(8,128)S(1)}, f32[80,128]{1,0:T(8,128)S(1)}, u32[]{:S(2)}, u32[]{:S(2)}) collective-permute-start(f32[80,128]{1,0:T(8,128)S(1)} %get-tuple-element.31.y_ref.refs_9_), channel_id=1, source_target_pairs={{32,0},{34,2},{36,4},{38,6},{40,8},{42,10},{44,12},{46,14},{48,16}... | collective-permute-start | bytes 122888 | tf_op jit(solution)/shard_map/ppermute | solution.py:513
  36.8 0.0 collective-permute-start.8
  36.8 0.5 collective-permute-start.9
  37.3 0.5 shard_map.49
  37.8 0.1 collective-permute-done.10.refs_12_
  38.0 1.3 %collective-permute-done.11.refs_13_ = f32[80,128]{1,0:T(8,128)S(1)} collective-permute-done((f32[80,128]{1,0:T(8,128)S(1)}, f32[80,128]{1,0:T(8,128)S(1)}, u32[]{:S(2)}, u32[]{:S(2)}) %collective-permute-start.11) | collective-permute-done | bytes 40992 | tf_op jit(solution)/shard_map/ppermute | solution.py:513
  39.3 0.0 collective-permute-done.8.refs_10_
  39.3 5.1 %collective-permute-done.9.refs_11_ = f32[80,128]{1,0:T(8,128)S(1)} collective-permute-done((f32[80,128]{1,0:T(8,128)S(1)}, f32[80,128]{1,0:T(8,128)S(1)}, u32[]{:S(2)}, u32[]{:S(2)}) %collective-permute-start.9) | collective-permute-done | bytes 40992 | tf_op jit(solution)/shard_map/ppermute | solution.py:513
  44.5 2.5 %shard_map.50 = (f32[2,80,128]{2,1,0:T(8,128)S(1)}, f32[2,80,128]{2,1,0:T(8,128)S(1)}) custom-call(f32[80,320,128]{2,1,0:T(8,128)S(1)} %get-tuple-element.26.refs_0_, s32[6,8,128]{2,1,0:T(8,128)S(1)} %get-tuple-element.27.refs_1_, f32[5,4,2,8,128]{4,3,2,1,0:T(8,128)S(1)} %get-tuple-element.38.refs_2_, f32[5,4,2,8,128]{4,3,2,1,0:T(8,128)S(1)} %get-tuple-element.39.refs_3_, ...), custom_call_target="tpu_custom_call" | custom-call | flops 10000000 | bytes 1000000 | tf_op jit(solution)/shard_map/pallas_call | solution.py:475
  47.0 0.1 collective-permute-start.12
  47.1 0.7 %collective-permute-start.13 = (f32[2,80,128]{2,1,0:T(8,128)S(1)}, f32[2,80,128]{2,1,0:T(8,128)S(1)}, u32[]{:S(2)}, u32[]{:S(2)}) collective-permute-start(f32[2,80,128]{2,1,0:T(8,128)S(1)} %get-tuple-element.46.refs_3_), channel_id=1, source_target_pairs={{32,0},{34,2},{36,4},{38,6},{40,8},{42,10},{44,12},{46,14},{48,16}... | collective-permute-start | bytes 245768 | tf_op jit(solution)/shard_map/ppermute | solution.py:513
  47.8 0.0 collective-permute-start.14
  47.8 0.5 collective-permute-start.15
  48.3 2.9 %collective-permute-done.12.refs_4_ = f32[2,80,128]{2,1,0:T(8,128)S(1)} collective-permute-done((f32[2,80,128]{2,1,0:T(8,128)S(1)}, f32[2,80,128]{2,1,0:T(8,128)S(1)}, u32[]{:S(2)}, u32[]{:S(2)}) %collective-permute-start.12) | collective-permute-done | bytes 81952 | tf_op jit(solution)/shard_map/ppermute | solution.py:513
  51.2 1.2 %collective-permute-done.13.refs_5_ = f32[2,80,128]{2,1,0:T(8,128)S(1)} collective-permute-done((f32[2,80,128]{2,1,0:T(8,128)S(1)}, f32[2,80,128]{2,1,0:T(8,128)S(1)}, u32[]{:S(2)}, u32[]{:S(2)}) %collective-permute-start.13) | collective-permute-done | bytes 81952 | tf_op jit(solution)/shard_map/ppermute | solution.py:513
  52.4 0.0 collective-permute-done.14.refs_6_
  52.4 3.5 %collective-permute-done.15.refs_7_ = f32[2,80,128]{2,1,0:T(8,128)S(1)} collective-permute-done((f32[2,80,128]{2,1,0:T(8,128)S(1)}, f32[2,80,128]{2,1,0:T(8,128)S(1)}, u32[]{:S(2)}, u32[]{:S(2)}) %collective-permute-start.15) | collective-permute-done | bytes 81952 | tf_op jit(solution)/shard_map/ppermute | solution.py:513
  55.9 3.5 %shard_map.51 = f32[2,32,320]{2,1,0:T(8,128)} custom-call(f32[80,320,128]{2,1,0:T(8,128)S(1)} %get-tuple-element.26.refs_0_, s32[6,8,128]{2,1,0:T(8,128)S(1)} %get-tuple-element.27.refs_1_, f32[2,80,128]{2,1,0:T(8,128)S(1)} %get-tuple-element.45.refs_2_, f32[2,80,128]{2,1,0:T(8,128)S(1)} %get-tuple-element.46.refs_3_, ...), custom_call_target="tpu_custom_call" | custom-call | flops 10000000 | bytes 1000000 | tf_op jit(solution)/shard_map/pallas_call | solution.py:475
Async XLA Ops:
  0.0 22.3 %collective-permute-start = (f32[32,320]{1,0:T(8,128)}, f32[32,320]{1,0:T(8,128)S(1)}, u32[]{:S(2)}, u32[]{:S(2)}) collective-permute-start(f32[32,320]{1,0:T(8,128)} %u_ref.1), channel_id=1, source_target_pairs={{32,0},{34,2},{36,4},{38,6},{40,8},{42,10},{44,12},{46,14},{48,16}... | collective-permute-start | bytes 122888 | tf_op jit(solution)/shard_map/ppermute | solution.py:513
  4.1 18.2 %collective-permute-start.1 = (f32[32,320]{1,0:T(8,128)}, f32[32,320]{1,0:T(8,128)S(1)}, u32[]{:S(2)}, u32[]{:S(2)}) collective-permute-start(f32[32,320]{1,0:T(8,128)} %u_ref.1), channel_id=1, source_target_pairs={{2,0},{4,2},{6,4},{8,6},{10,8},{12,10},{14,12},{16,14},{18,16},{20... | collective-permute-start | bytes 122888 | tf_op jit(solution)/shard_map/ppermute | solution.py:513
  6.9 15.5 %collective-permute-start.2 = (f32[32,320]{1,0:T(8,128)}, f32[32,320]{1,0:T(8,128)S(1)}, u32[]{:S(2)}, u32[]{:S(2)}) collective-permute-start(f32[32,320]{1,0:T(8,128)} %u_ref.1), channel_id=1, source_target_pairs={{126,0},{0,2},{2,4},{4,6},{6,8},{8,10},{10,12},{12,14},{14,16},{16... | collective-permute-start | bytes 122888 | tf_op jit(solution)/shard_map/ppermute | solution.py:513
  6.9 15.5 %collective-permute-start.3 = (f32[32,320]{1,0:T(8,128)}, f32[32,320]{1,0:T(8,128)S(1)}, u32[]{:S(2)}, u32[]{:S(2)}) collective-permute-start(f32[32,320]{1,0:T(8,128)} %u_ref.1), channel_id=1, source_target_pairs={{34,0},{36,2},{38,4},{40,6},{42,8},{44,10},{46,12},{48,14},{50,16}... | collective-permute-start | bytes 122888 | tf_op jit(solution)/shard_map/ppermute | solution.py:513
  23.8 3.9 %collective-permute-start.4 = (f32[80,128]{1,0:T(8,128)S(1)}, f32[80,128]{1,0:T(8,128)S(1)}, u32[]{:S(2)}, u32[]{:S(2)}) collective-permute-start(f32[80,128]{1,0:T(8,128)S(1)} %get-tuple-element.30.refs_2_.x_ref), channel_id=1, source_target_pairs={{34,0},{36,2},{38,4},{40,6},{42,8},{44,10},{46,12},{48,14},{50,16}... | collective-permute-start | bytes 122888 | tf_op jit(solution)/shard_map/ppermute | solution.py:513
  23.8 4.4 %collective-permute-start.5 = (f32[80,128]{1,0:T(8,128)S(1)}, f32[80,128]{1,0:T(8,128)S(1)}, u32[]{:S(2)}, u32[]{:S(2)}) collective-permute-start(f32[80,128]{1,0:T(8,128)S(1)} %get-tuple-element.30.refs_2_.x_ref), channel_id=1, source_target_pairs={{32,0},{34,2},{36,4},{38,6},{40,8},{42,10},{44,12},{46,14},{48,16}... | collective-permute-start | bytes 122888 | tf_op jit(solution)/shard_map/ppermute | solution.py:513
  24.7 3.6 %collective-permute-start.6 = (f32[80,128]{1,0:T(8,128)S(1)}, f32[80,128]{1,0:T(8,128)S(1)}, u32[]{:S(2)}, u32[]{:S(2)}) collective-permute-start(f32[80,128]{1,0:T(8,128)S(1)} %get-tuple-element.30.refs_2_.x_ref), channel_id=1, source_target_pairs={{2,0},{4,2},{6,4},{8,6},{10,8},{12,10},{14,12},{16,14},{18,16},{20... | collective-permute-start | bytes 122888 | tf_op jit(solution)/shard_map/ppermute | solution.py:513
  25.5 7.6 %collective-permute-start.7 = (f32[80,128]{1,0:T(8,128)S(1)}, f32[80,128]{1,0:T(8,128)S(1)}, u32[]{:S(2)}, u32[]{:S(2)}) collective-permute-start(f32[80,128]{1,0:T(8,128)S(1)} %get-tuple-element.30.refs_2_.x_ref), channel_id=1, source_target_pairs={{126,0},{0,2},{2,4},{4,6},{6,8},{8,10},{10,12},{12,14},{14,16},{16... | collective-permute-start | bytes 122888 | tf_op jit(solution)/shard_map/ppermute | solution.py:513
  34.5 3.5 %collective-permute-start.10 = (f32[80,128]{1,0:T(8,128)S(1)}, f32[80,128]{1,0:T(8,128)S(1)}, u32[]{:S(2)}, u32[]{:S(2)}) collective-permute-start(f32[80,128]{1,0:T(8,128)S(1)} %get-tuple-element.31.y_ref.refs_9_), channel_id=1, source_target_pairs={{34,0},{36,2},{38,4},{40,6},{42,8},{44,10},{46,12},{48,14},{50,16}... | collective-permute-start | bytes 122888 | tf_op jit(solution)/shard_map/ppermute | solution.py:513
  35.2 4.1 %collective-permute-start.11 = (f32[80,128]{1,0:T(8,128)S(1)}, f32[80,128]{1,0:T(8,128)S(1)}, u32[]{:S(2)}, u32[]{:S(2)}) collective-permute-start(f32[80,128]{1,0:T(8,128)S(1)} %get-tuple-element.31.y_ref.refs_9_), channel_id=1, source_target_pairs={{32,0},{34,2},{36,4},{38,6},{40,8},{42,10},{44,12},{46,14},{48,16}... | collective-permute-start | bytes 122888 | tf_op jit(solution)/shard_map/ppermute | solution.py:513
  36.8 2.5 %collective-permute-start.8 = (f32[80,128]{1,0:T(8,128)S(1)}, f32[80,128]{1,0:T(8,128)S(1)}, u32[]{:S(2)}, u32[]{:S(2)}) collective-permute-start(f32[80,128]{1,0:T(8,128)S(1)} %get-tuple-element.31.y_ref.refs_9_), channel_id=1, source_target_pairs={{2,0},{4,2},{6,4},{8,6},{10,8},{12,10},{14,12},{16,14},{18,16},{20... | collective-permute-start | bytes 122888 | tf_op jit(solution)/shard_map/ppermute | solution.py:513
  36.8 7.6 %collective-permute-start.9 = (f32[80,128]{1,0:T(8,128)S(1)}, f32[80,128]{1,0:T(8,128)S(1)}, u32[]{:S(2)}, u32[]{:S(2)}) collective-permute-start(f32[80,128]{1,0:T(8,128)S(1)} %get-tuple-element.31.y_ref.refs_9_), channel_id=1, source_target_pairs={{126,0},{0,2},{2,4},{4,6},{6,8},{8,10},{10,12},{12,14},{14,16},{16... | collective-permute-start | bytes 122888 | tf_op jit(solution)/shard_map/ppermute | solution.py:513
  47.0 4.2 %collective-permute-start.12 = (f32[2,80,128]{2,1,0:T(8,128)S(1)}, f32[2,80,128]{2,1,0:T(8,128)S(1)}, u32[]{:S(2)}, u32[]{:S(2)}) collective-permute-start(f32[2,80,128]{2,1,0:T(8,128)S(1)} %get-tuple-element.46.refs_3_), channel_id=1, source_target_pairs={{34,0},{36,2},{38,4},{40,6},{42,8},{44,10},{46,12},{48,14},{50,16}... | collective-permute-start | bytes 245768 | tf_op jit(solution)/shard_map/ppermute | solution.py:513
  47.1 5.3 %collective-permute-start.13 = (f32[2,80,128]{2,1,0:T(8,128)S(1)}, f32[2,80,128]{2,1,0:T(8,128)S(1)}, u32[]{:S(2)}, u32[]{:S(2)}) collective-permute-start(f32[2,80,128]{2,1,0:T(8,128)S(1)} %get-tuple-element.46.refs_3_), channel_id=1, source_target_pairs={{32,0},{34,2},{36,4},{38,6},{40,8},{42,10},{44,12},{46,14},{48,16}... | collective-permute-start | bytes 245768 | tf_op jit(solution)/shard_map/ppermute | solution.py:513
  47.8 4.6 %collective-permute-start.14 = (f32[2,80,128]{2,1,0:T(8,128)S(1)}, f32[2,80,128]{2,1,0:T(8,128)S(1)}, u32[]{:S(2)}, u32[]{:S(2)}) collective-permute-start(f32[2,80,128]{2,1,0:T(8,128)S(1)} %get-tuple-element.46.refs_3_), channel_id=1, source_target_pairs={{2,0},{4,2},{6,4},{8,6},{10,8},{12,10},{14,12},{16,14},{18,16},{20... | collective-permute-start | bytes 245768 | tf_op jit(solution)/shard_map/ppermute | solution.py:513
  47.8 8.1 %collective-permute-start.15 = (f32[2,80,128]{2,1,0:T(8,128)S(1)}, f32[2,80,128]{2,1,0:T(8,128)S(1)}, u32[]{:S(2)}, u32[]{:S(2)}) collective-permute-start(f32[2,80,128]{2,1,0:T(8,128)S(1)} %get-tuple-element.46.refs_3_), channel_id=1, source_target_pairs={{126,0},{0,2},{2,4},{4,6},{6,8},{8,10},{10,12},{12,14},{14,16},{16... | collective-permute-start | bytes 245768 | tf_op jit(solution)/shard_map/ppermute | solution.py:513

commit v3 on v2

--- a/solution.py
+++ b/solution.py
@@ -14,7 +14,6 @@
 ROWS = 80
 LANES = 128
 GROUPS = 10
-EARLY = 3
 SECTIONS = 4
 
 time_step = 0.03
@@ -334,7 +333,7 @@
             t_ref[g * 8 + r, 256:320] = tail[g, :, :, r, :].reshape(LANES, 64).T
         return carry
 
-    lax.fori_loop(0, EARLY, turn_group, 0)
+    lax.fori_loop(0, GROUPS, turn_group, 0)
     for copy in smalls:
         copy.wait()
     count = lax.axis_size("elem")
@@ -358,7 +357,6 @@
     u = flipped(jnp.concatenate([own[...]] * 4, axis=0))
     nodes_ref[...] = u
     acc_ref[...] = volume(u)
-    lax.fori_loop(EARLY, GROUPS, turn_group, 0)
 
 
 def first_kernel(t_ref, index_ref, nodes_ref, acc_ref, moved,

time: 59.5 us -> 57.1 us (0.960)
  Pallas kernels: 20.2 us -> 17.8 us
    pallas_call x6, Pallas kernels: 20.2 us -> 17.8 us  [call(): pl.pallas_call(kernel, out_shape=outputs, in_specs=in_specs, out_specs=[p...]
  transfers between devices with their start and end apart: 16 -> 16, of which waited for: 9 -> 9; matrix products, arithmetic and copies ran while one was open for 0% -> 0% of each run, Pallas kernels for 19% -> 16%
where the time goes in v3:
time: 57.1 us; the launch traced here: 57 us
  waiting for transfers between devices  19.7 us (35%)
  starting transfers between devices  19.4 us (34%)
  Pallas kernels  17.8 us (31%)
    ppermute x16, waiting for transfers between devices, exchanged(): lax.ppermute(block, 'elem', [(s, i) for i, s in enumerate(table[name])])  19.7 us
    ppermute x16, starting transfers between devices, exchanged(): lax.ppermute(block, 'elem', [(s, i) for i, s in enumerate(table[name])])  19.4 us
    pallas_call x6, Pallas kernels, call(): pl.pallas_call(kernel, out_shape=outputs, in_specs=in_specs, out_specs=[p...  17.8 us
  transfers between devices with their start and end apart: 16, of which 9 were waited for; matrix products, arithmetic and copies ran while one was open for 0% of the time, Pallas kernels for 16%

profile of v3, /device:TPU:0, one launch (start us, length us, event | category | flops | bytes accessed | tf_op | source)
XLA Modules:
  0.0 57.0 jit_solution(11330610002282168)
XLA Ops:
  0.0 4.1 %collective-permute-start = (f32[32,320]{1,0:T(8,128)}, f32[32,320]{1,0:T(8,128)S(1)}, u32[]{:S(2)}, u32[]{:S(2)}) collective-permute-start(f32[32,320]{1,0:T(8,128)} %u_ref.1), channel_id=1, source_target_pairs={{32,0},{34,2},{36,4},{38,6},{40,8},{42,10},{44,12},{46,14},{48,16}... | collective-permute-start | bytes 122888 | tf_op jit(solution)/shard_map/ppermute | solution.py:511
  4.1 2.8 %collective-permute-start.1 = (f32[32,320]{1,0:T(8,128)}, f32[32,320]{1,0:T(8,128)S(1)}, u32[]{:S(2)}, u32[]{:S(2)}) collective-permute-start(f32[32,320]{1,0:T(8,128)} %u_ref.1), channel_id=1, source_target_pairs={{2,0},{4,2},{6,4},{8,6},{10,8},{12,10},{14,12},{16,14},{18,16},{20... | collective-permute-start | bytes 122888 | tf_op jit(solution)/shard_map/ppermute | solution.py:511
  6.9 0.0 collective-permute-start.2
  6.9 4.5 %collective-permute-start.3 = (f32[32,320]{1,0:T(8,128)}, f32[32,320]{1,0:T(8,128)S(1)}, u32[]{:S(2)}, u32[]{:S(2)}) collective-permute-start(f32[32,320]{1,0:T(8,128)} %u_ref.1), channel_id=1, source_target_pairs={{34,0},{36,2},{38,4},{40,6},{42,8},{44,10},{46,12},{48,14},{50,16}... | collective-permute-start | bytes 122888 | tf_op jit(solution)/shard_map/ppermute | solution.py:511
  11.4 8.5 %shard_map.46 = (f32[80,320,128]{2,1,0:T(8,128)S(1)}, s32[6,8,128]{2,1,0:T(8,128)S(1)}, f32[5,4,2,8,128]{4,3,2,1,0:T(8,128)S(1)}, f32[5,4,2,8,128]{4,3,2,1,0:T(8,128)S(1)}) custom-call(f32[32,320,320]{2,1,0:T(8,128)} %inv_ref.1, s32[5,32]{1,0:T(8,128)} %bitcast.3, s32[16,128]{1,0:T(8,128)} %bitcast.2, f32[32,320]{1,0:T(8,128)} %u_ref.1), custom_call_target="tpu_custom_call" | custom-call | flops 1000000000 | bytes 1000000 | tf_op jit(solution)/shard_map/pallas_call | solution.py:473
  19.9 0.0 collective-permute-done.refs_4_
  19.9 0.0 collective-permute-done.1.refs_5_
  19.9 0.0 collective-permute-done.2.refs_6_
  19.9 0.0 collective-permute-done.3.refs_7_
  19.9 1.4 %shard_map.47 = (f32[80,128]{1,0:T(8,128)S(1)}, f32[5,2,2,8,128]{4,3,2,1,0:T(8,128)S(1)}, f32[5,4,2,8,128]{4,3,2,1,0:T(8,128)S(1)}, f32[5,4,2,8,128]{4,3,2,1,0:T(8,128)S(1)}) custom-call(f32[80,320,128]{2,1,0:T(8,128)S(1)} %get-tuple-element.26.refs_0_, s32[6,8,128]{2,1,0:T(8,128)S(1)} %get-tuple-element.27.refs_1_, ...), custom_call_target="tpu_custom_call" | custom-call | flops 10000000 | bytes 1000000 | tf_op jit(solution)/shard_map/pallas_call | solution.py:473
  21.3 0.1 collective-permute-start.4
  21.4 0.9 %collective-permute-start.5 = (f32[80,128]{1,0:T(8,128)S(1)}, f32[80,128]{1,0:T(8,128)S(1)}, u32[]{:S(2)}, u32[]{:S(2)}) collective-permute-start(f32[80,128]{1,0:T(8,128)S(1)} %get-tuple-element.30.refs_2_.x_ref), channel_id=1, source_target_pairs={{32,0},{34,2},{36,4},{38,6},{40,8},{42,10},{44,12},{46,14},{48,16}... | collective-permute-start | bytes 122888 | tf_op jit(solution)/shard_map/ppermute | solution.py:511
  22.3 0.8 %collective-permute-start.6 = (f32[80,128]{1,0:T(8,128)S(1)}, f32[80,128]{1,0:T(8,128)S(1)}, u32[]{:S(2)}, u32[]{:S(2)}) collective-permute-start(f32[80,128]{1,0:T(8,128)S(1)} %get-tuple-element.30.refs_2_.x_ref), channel_id=1, source_target_pairs={{2,0},{4,2},{6,4},{8,6},{10,8},{12,10},{14,12},{16,14},{18,16},{20... | collective-permute-start | bytes 122888 | tf_op jit(solution)/shard_map/ppermute | solution.py:511
  23.1 2.2 %collective-permute-start.7 = (f32[80,128]{1,0:T(8,128)S(1)}, f32[80,128]{1,0:T(8,128)S(1)}, u32[]{:S(2)}, u32[]{:S(2)}) collective-permute-start(f32[80,128]{1,0:T(8,128)S(1)} %get-tuple-element.30.refs_2_.x_ref), channel_id=1, source_target_pairs={{126,0},{0,2},{2,4},{4,6},{6,8},{8,10},{10,12},{12,14},{14,16},{16... | collective-permute-start | bytes 122888 | tf_op jit(solution)/shard_map/ppermute | solution.py:511
  25.2 0.0 collective-permute-done.4.refs_3_
  25.2 0.6 %collective-permute-done.5.refs_4_ = f32[80,128]{1,0:T(8,128)S(1)} collective-permute-done((f32[80,128]{1,0:T(8,128)S(1)}, f32[80,128]{1,0:T(8,128)S(1)}, u32[]{:S(2)}, u32[]{:S(2)}) %collective-permute-start.5) | collective-permute-done | bytes 40992 | tf_op jit(solution)/shard_map/ppermute | solution.py:511
  25.8 0.1 collective-permute-done.6.refs_5_
  25.9 4.8 %collective-permute-done.7.refs_6_ = f32[80,128]{1,0:T(8,128)S(1)} collective-permute-done((f32[80,128]{1,0:T(8,128)S(1)}, f32[80,128]{1,0:T(8,128)S(1)}, u32[]{:S(2)}, u32[]{:S(2)}) %collective-permute-start.7) | collective-permute-done | bytes 40992 | tf_op jit(solution)/shard_map/ppermute | solution.py:511
  30.7 1.4 %shard_map.48 = (f32[80,128]{1,0:T(8,128)S(1)}, f32[5,2,2,8,128]{4,3,2,1,0:T(8,128)S(1)}, f32[5,4,2,8,128]{4,3,2,1,0:T(8,128)S(1)}, f32[5,4,2,8,128]{4,3,2,1,0:T(8,128)S(1)}) custom-call(f32[80,320,128]{2,1,0:T(8,128)S(1)} %get-tuple-element.26.refs_0_, s32[6,8,128]{2,1,0:T(8,128)S(1)} %get-tuple-element.27.refs_1_, ...), custom_call_target="tpu_custom_call" | custom-call | flops 10000000 | bytes 1000000 | tf_op jit(solution)/shard_map/pallas_call | solution.py:473
  32.1 0.7 %collective-permute-start.10 = (f32[80,128]{1,0:T(8,128)S(1)}, f32[80,128]{1,0:T(8,128)S(1)}, u32[]{:S(2)}, u32[]{:S(2)}) collective-permute-start(f32[80,128]{1,0:T(8,128)S(1)} %get-tuple-element.31.y_ref.refs_9_), channel_id=1, source_target_pairs={{34,0},{36,2},{38,4},{40,6},{42,8},{44,10},{46,12},{48,14},{50,16}... | collective-permute-start | bytes 122888 | tf_op jit(solution)/shard_map/ppermute | solution.py:511
  32.8 1.6 %collective-permute-start.11 = (f32[80,128]{1,0:T(8,128)S(1)}, f32[80,128]{1,0:T(8,128)S(1)}, u32[]{:S(2)}, u32[]{:S(2)}) collective-permute-start(f32[80,128]{1,0:T(8,128)S(1)} %get-tuple-element.31.y_ref.refs_9_), channel_id=1, source_target_pairs={{32,0},{34,2},{36,4},{38,6},{40,8},{42,10},{44,12},{46,14},{48,16}... | collective-permute-start | bytes 122888 | tf_op jit(solution)/shard_map/ppermute | solution.py:511
  34.4 0.0 collective-permute-start.8
  34.4 0.5 collective-permute-start.9
  34.9 0.5 shard_map.49
  35.4 0.1 collective-permute-done.10.refs_12_
  35.6 1.3 %collective-permute-done.11.refs_13_ = f32[80,128]{1,0:T(8,128)S(1)} collective-permute-done((f32[80,128]{1,0:T(8,128)S(1)}, f32[80,128]{1,0:T(8,128)S(1)}, u32[]{:S(2)}, u32[]{:S(2)}) %collective-permute-start.11) | collective-permute-done | bytes 40992 | tf_op jit(solution)/shard_map/ppermute | solution.py:511
  36.9 0.0 collective-permute-done.8.refs_10_
  36.9 5.1 %collective-permute-done.9.refs_11_ = f32[80,128]{1,0:T(8,128)S(1)} collective-permute-done((f32[80,128]{1,0:T(8,128)S(1)}, f32[80,128]{1,0:T(8,128)S(1)}, u32[]{:S(2)}, u32[]{:S(2)}) %collective-permute-start.9) | collective-permute-done | bytes 40992 | tf_op jit(solution)/shard_map/ppermute | solution.py:511
  42.1 2.5 %shard_map.50 = (f32[2,80,128]{2,1,0:T(8,128)S(1)}, f32[2,80,128]{2,1,0:T(8,128)S(1)}) custom-call(f32[80,320,128]{2,1,0:T(8,128)S(1)} %get-tuple-element.26.refs_0_, s32[6,8,128]{2,1,0:T(8,128)S(1)} %get-tuple-element.27.refs_1_, f32[5,4,2,8,128]{4,3,2,1,0:T(8,128)S(1)} %get-tuple-element.38.refs_2_, f32[5,4,2,8,128]{4,3,2,1,0:T(8,128)S(1)} %get-tuple-element.39.refs_3_, ...), custom_call_target="tpu_custom_call" | custom-call | flops 10000000 | bytes 1000000 | tf_op jit(solution)/shard_map/pallas_call | solution.py:473
  44.6 0.1 collective-permute-start.12
  44.7 0.7 %collective-permute-start.13 = (f32[2,80,128]{2,1,0:T(8,128)S(1)}, f32[2,80,128]{2,1,0:T(8,128)S(1)}, u32[]{:S(2)}, u32[]{:S(2)}) collective-permute-start(f32[2,80,128]{2,1,0:T(8,128)S(1)} %get-tuple-element.46.refs_3_), channel_id=1, source_target_pairs={{32,0},{34,2},{36,4},{38,6},{40,8},{42,10},{44,12},{46,14},{48,16}... | collective-permute-start | bytes 245768 | tf_op jit(solution)/shard_map/ppermute | solution.py:511
  45.4 0.0 collective-permute-start.14
  45.4 0.5 collective-permute-start.15
  45.9 2.9 %collective-permute-done.12.refs_4_ = f32[2,80,128]{2,1,0:T(8,128)S(1)} collective-permute-done((f32[2,80,128]{2,1,0:T(8,128)S(1)}, f32[2,80,128]{2,1,0:T(8,128)S(1)}, u32[]{:S(2)}, u32[]{:S(2)}) %collective-permute-start.12) | collective-permute-done | bytes 81952 | tf_op jit(solution)/shard_map/ppermute | solution.py:511
  48.8 1.2 %collective-permute-done.13.refs_5_ = f32[2,80,128]{2,1,0:T(8,128)S(1)} collective-permute-done((f32[2,80,128]{2,1,0:T(8,128)S(1)}, f32[2,80,128]{2,1,0:T(8,128)S(1)}, u32[]{:S(2)}, u32[]{:S(2)}) %collective-permute-start.13) | collective-permute-done | bytes 81952 | tf_op jit(solution)/shard_map/ppermute | solution.py:511
  50.0 0.0 collective-permute-done.14.refs_6_
  50.0 3.5 %collective-permute-done.15.refs_7_ = f32[2,80,128]{2,1,0:T(8,128)S(1)} collective-permute-done((f32[2,80,128]{2,1,0:T(8,128)S(1)}, f32[2,80,128]{2,1,0:T(8,128)S(1)}, u32[]{:S(2)}, u32[]{:S(2)}) %collective-permute-start.15) | collective-permute-done | bytes 81952 | tf_op jit(solution)/shard_map/ppermute | solution.py:511
  53.5 3.5 %shard_map.51 = f32[2,32,320]{2,1,0:T(8,128)} custom-call(f32[80,320,128]{2,1,0:T(8,128)S(1)} %get-tuple-element.26.refs_0_, s32[6,8,128]{2,1,0:T(8,128)S(1)} %get-tuple-element.27.refs_1_, f32[2,80,128]{2,1,0:T(8,128)S(1)} %get-tuple-element.45.refs_2_, f32[2,80,128]{2,1,0:T(8,128)S(1)} %get-tuple-element.46.refs_3_, ...), custom_call_target="tpu_custom_call" | custom-call | flops 10000000 | bytes 1000000 | tf_op jit(solution)/shard_map/pallas_call | solution.py:473
Async XLA Ops:
  0.0 19.9 %collective-permute-start = (f32[32,320]{1,0:T(8,128)}, f32[32,320]{1,0:T(8,128)S(1)}, u32[]{:S(2)}, u32[]{:S(2)}) collective-permute-start(f32[32,320]{1,0:T(8,128)} %u_ref.1), channel_id=1, source_target_pairs={{32,0},{34,2},{36,4},{38,6},{40,8},{42,10},{44,12},{46,14},{48,16}... | collective-permute-start | bytes 122888 | tf_op jit(solution)/shard_map/ppermute | solution.py:511
  4.1 15.8 %collective-permute-start.1 = (f32[32,320]{1,0:T(8,128)}, f32[32,320]{1,0:T(8,128)S(1)}, u32[]{:S(2)}, u32[]{:S(2)}) collective-permute-start(f32[32,320]{1,0:T(8,128)} %u_ref.1), channel_id=1, source_target_pairs={{2,0},{4,2},{6,4},{8,6},{10,8},{12,10},{14,12},{16,14},{18,16},{20... | collective-permute-start | bytes 122888 | tf_op jit(solution)/shard_map/ppermute | solution.py:511
  6.9 13.0 %collective-permute-start.2 = (f32[32,320]{1,0:T(8,128)}, f32[32,320]{1,0:T(8,128)S(1)}, u32[]{:S(2)}, u32[]{:S(2)}) collective-permute-start(f32[32,320]{1,0:T(8,128)} %u_ref.1), channel_id=1, source_target_pairs={{126,0},{0,2},{2,4},{4,6},{6,8},{8,10},{10,12},{12,14},{14,16},{16... | collective-permute-start | bytes 122888 | tf_op jit(solution)/shard_map/ppermute | solution.py:511
  6.9 13.0 %collective-permute-start.3 = (f32[32,320]{1,0:T(8,128)}, f32[32,320]{1,0:T(8,128)S(1)}, u32[]{:S(2)}, u32[]{:S(2)}) collective-permute-start(f32[32,320]{1,0:T(8,128)} %u_ref.1), channel_id=1, source_target_pairs={{34,0},{36,2},{38,4},{40,6},{42,8},{44,10},{46,12},{48,14},{50,16}... | collective-permute-start | bytes 122888 | tf_op jit(solution)/shard_map/ppermute | solution.py:511
  21.3 3.9 %collective-permute-start.4 = (f32[80,128]{1,0:T(8,128)S(1)}, f32[80,128]{1,0:T(8,128)S(1)}, u32[]{:S(2)}, u32[]{:S(2)}) collective-permute-start(f32[80,128]{1,0:T(8,128)S(1)} %get-tuple-element.30.refs_2_.x_ref), channel_id=1, source_target_pairs={{34,0},{36,2},{38,4},{40,6},{42,8},{44,10},{46,12},{48,14},{50,16}... | collective-permute-start | bytes 122888 | tf_op jit(solution)/shard_map/ppermute | solution.py:511
  21.4 4.4 %collective-permute-start.5 = (f32[80,128]{1,0:T(8,128)S(1)}, f32[80,128]{1,0:T(8,128)S(1)}, u32[]{:S(2)}, u32[]{:S(2)}) collective-permute-start(f32[80,128]{1,0:T(8,128)S(1)} %get-tuple-element.30.refs_2_.x_ref), channel_id=1, source_target_pairs={{32,0},{34,2},{36,4},{38,6},{40,8},{42,10},{44,12},{46,14},{48,16}... | collective-permute-start | bytes 122888 | tf_op jit(solution)/shard_map/ppermute | solution.py:511
  22.3 3.6 %collective-permute-start.6 = (f32[80,128]{1,0:T(8,128)S(1)}, f32[80,128]{1,0:T(8,128)S(1)}, u32[]{:S(2)}, u32[]{:S(2)}) collective-permute-start(f32[80,128]{1,0:T(8,128)S(1)} %get-tuple-element.30.refs_2_.x_ref), channel_id=1, source_target_pairs={{2,0},{4,2},{6,4},{8,6},{10,8},{12,10},{14,12},{16,14},{18,16},{20... | collective-permute-start | bytes 122888 | tf_op jit(solution)/shard_map/ppermute | solution.py:511
  23.1 7.6 %collective-permute-start.7 = (f32[80,128]{1,0:T(8,128)S(1)}, f32[80,128]{1,0:T(8,128)S(1)}, u32[]{:S(2)}, u32[]{:S(2)}) collective-permute-start(f32[80,128]{1,0:T(8,128)S(1)} %get-tuple-element.30.refs_2_.x_ref), channel_id=1, source_target_pairs={{126,0},{0,2},{2,4},{4,6},{6,8},{8,10},{10,12},{12,14},{14,16},{16... | collective-permute-start | bytes 122888 | tf_op jit(solution)/shard_map/ppermute | solution.py:511
  32.1 3.5 %collective-permute-start.10 = (f32[80,128]{1,0:T(8,128)S(1)}, f32[80,128]{1,0:T(8,128)S(1)}, u32[]{:S(2)}, u32[]{:S(2)}) collective-permute-start(f32[80,128]{1,0:T(8,128)S(1)} %get-tuple-element.31.y_ref.refs_9_), channel_id=1, source_target_pairs={{34,0},{36,2},{38,4},{40,6},{42,8},{44,10},{46,12},{48,14},{50,16}... | collective-permute-start | bytes 122888 | tf_op jit(solution)/shard_map/ppermute | solution.py:511
  32.8 4.1 %collective-permute-start.11 = (f32[80,128]{1,0:T(8,128)S(1)}, f32[80,128]{1,0:T(8,128)S(1)}, u32[]{:S(2)}, u32[]{:S(2)}) collective-permute-start(f32[80,128]{1,0:T(8,128)S(1)} %get-tuple-element.31.y_ref.refs_9_), channel_id=1, source_target_pairs={{32,0},{34,2},{36,4},{38,6},{40,8},{42,10},{44,12},{46,14},{48,16}... | collective-permute-start | bytes 122888 | tf_op jit(solution)/shard_map/ppermute | solution.py:511
  34.4 2.5 %collective-permute-start.8 = (f32[80,128]{1,0:T(8,128)S(1)}, f32[80,128]{1,0:T(8,128)S(1)}, u32[]{:S(2)}, u32[]{:S(2)}) collective-permute-start(f32[80,128]{1,0:T(8,128)S(1)} %get-tuple-element.31.y_ref.refs_9_), channel_id=1, source_target_pairs={{2,0},{4,2},{6,4},{8,6},{10,8},{12,10},{14,12},{16,14},{18,16},{20... | collective-permute-start | bytes 122888 | tf_op jit(solution)/shard_map/ppermute | solution.py:511
  34.4 7.6 %collective-permute-start.9 = (f32[80,128]{1,0:T(8,128)S(1)}, f32[80,128]{1,0:T(8,128)S(1)}, u32[]{:S(2)}, u32[]{:S(2)}) collective-permute-start(f32[80,128]{1,0:T(8,128)S(1)} %get-tuple-element.31.y_ref.refs_9_), channel_id=1, source_target_pairs={{126,0},{0,2},{2,4},{4,6},{6,8},{8,10},{10,12},{12,14},{14,16},{16... | collective-permute-start | bytes 122888 | tf_op jit(solution)/shard_map/ppermute | solution.py:511
  44.6 4.2 %collective-permute-start.12 = (f32[2,80,128]{2,1,0:T(8,128)S(1)}, f32[2,80,128]{2,1,0:T(8,128)S(1)}, u32[]{:S(2)}, u32[]{:S(2)}) collective-permute-start(f32[2,80,128]{2,1,0:T(8,128)S(1)} %get-tuple-element.46.refs_3_), channel_id=1, source_target_pairs={{34,0},{36,2},{38,4},{40,6},{42,8},{44,10},{46,12},{48,14},{50,16}... | collective-permute-start | bytes 245768 | tf_op jit(solution)/shard_map/ppermute | solution.py:511
  44.7 5.3 %collective-permute-start.13 = (f32[2,80,128]{2,1,0:T(8,128)S(1)}, f32[2,80,128]{2,1,0:T(8,128)S(1)}, u32[]{:S(2)}, u32[]{:S(2)}) collective-permute-start(f32[2,80,128]{2,1,0:T(8,128)S(1)} %get-tuple-element.46.refs_3_), channel_id=1, source_target_pairs={{32,0},{34,2},{36,4},{38,6},{40,8},{42,10},{44,12},{46,14},{48,16}... | collective-permute-start | bytes 245768 | tf_op jit(solution)/shard_map/ppermute | solution.py:511
  45.4 4.6 %collective-permute-start.14 = (f32[2,80,128]{2,1,0:T(8,128)S(1)}, f32[2,80,128]{2,1,0:T(8,128)S(1)}, u32[]{:S(2)}, u32[]{:S(2)}) collective-permute-start(f32[2,80,128]{2,1,0:T(8,128)S(1)} %get-tuple-element.46.refs_3_), channel_id=1, source_target_pairs={{2,0},{4,2},{6,4},{8,6},{10,8},{12,10},{14,12},{16,14},{18,16},{20... | collective-permute-start | bytes 245768 | tf_op jit(solution)/shard_map/ppermute | solution.py:511
  45.4 8.1 %collective-permute-start.15 = (f32[2,80,128]{2,1,0:T(8,128)S(1)}, f32[2,80,128]{2,1,0:T(8,128)S(1)}, u32[]{:S(2)}, u32[]{:S(2)}) collective-permute-start(f32[2,80,128]{2,1,0:T(8,128)S(1)} %get-tuple-element.46.refs_3_), channel_id=1, source_target_pairs={{126,0},{0,2},{2,4},{4,6},{6,8},{8,10},{10,12},{12,14},{14,16},{16... | collective-permute-start | bytes 245768 | tf_op jit(solution)/shard_map/ppermute | solution.py:511

commit v4 on v3

--- a/solution.py
+++ b/solution.py
@@ -75,7 +75,7 @@
 STEP_X = [time_step * ROW_SUM[i] for i in range(SECTIONS)]
 STEP_Y = [time_step * ROW_SUM[i] * COUPLING[i] for i in range(SECTIONS)]
 
-ORDERS = [('ahead', 'after', 'before', 'beyond'), ('beyond', 'ahead', 'after', 'before'), ('after', 'before', 'beyond', 'ahead'), ('beyond', 'ahead', 'after', 'before')]
+ORDERS = [('before', 'ahead', 'after', 'beyond'), ('beyond', 'ahead', 'after', 'before'), ('after', 'before', 'beyond', 'ahead'), ('beyond', 'ahead', 'after', 'before')]
 
 
 def sublane():

time: 57.1 us -> 56.6 us (level)
  starting transfers between devices: 19.4 us -> 17.3 us
  waiting for transfers between devices: 19.7 us -> 21.4 us
    ppermute x16, starting transfers between devices: 19.4 us -> 17.3 us  [exchanged(): lax.ppermute(block, 'elem', [(s, i) for i, s in enumerate(table[name])])]
    ppermute x16, waiting for transfers between devices: 19.7 us -> 21.4 us  [exchanged(): lax.ppermute(block, 'elem', [(s, i) for i, s in enumerate(table[name])])]
  transfers between devices with their start and end apart: 16 -> 16, of which waited for: 9 -> 8; matrix products, arithmetic and copies ran while one was open for 0% -> 0% of each run, Pallas kernels for 16% -> 16%
where the time goes in v4:
time: 56.6 us; the launch traced here: 56.5 us
  waiting for transfers between devices  21.4 us (38%)
  Pallas kernels  17.8 us (31%)
  starting transfers between devices  17.3 us (31%)
    ppermute x16, waiting for transfers between devices, exchanged(): lax.ppermute(block, 'elem', [(s, i) for i, s in enumerate(table[name])])  21.4 us
    pallas_call x6, Pallas kernels, call(): pl.pallas_call(kernel, out_shape=outputs, in_specs=in_specs, out_specs=[p...  17.8 us
    ppermute x16, starting transfers between devices, exchanged(): lax.ppermute(block, 'elem', [(s, i) for i, s in enumerate(table[name])])  17.3 us
  transfers between devices with their start and end apart: 16, of which 8 were waited for; matrix products, arithmetic and copies ran while one was open for 0% of the time, Pallas kernels for 16%

profile of v4, /device:TPU:0, one launch (start us, length us, event | category | flops | bytes accessed | tf_op | source)
XLA Modules:
  0.0 56.5 jit_solution(1469711910715388044)
XLA Ops:
  0.0 0.0 collective-permute-start
  0.0 4.1 %collective-permute-start.1 = (f32[32,320]{1,0:T(8,128)}, f32[32,320]{1,0:T(8,128)S(1)}, u32[]{:S(2)}, u32[]{:S(2)}) collective-permute-start(f32[32,320]{1,0:T(8,128)} %u_ref.1), channel_id=1, source_target_pairs={{32,0},{34,2},{36,4},{38,6},{40,8},{42,10},{44,12},{46,14},{48,16}... | collective-permute-start | bytes 122888 | tf_op jit(solution)/shard_map/ppermute | solution.py:511
  4.1 4.5 %collective-permute-start.2 = (f32[32,320]{1,0:T(8,128)}, f32[32,320]{1,0:T(8,128)S(1)}, u32[]{:S(2)}, u32[]{:S(2)}) collective-permute-start(f32[32,320]{1,0:T(8,128)} %u_ref.1), channel_id=1, source_target_pairs={{2,0},{4,2},{6,4},{8,6},{10,8},{12,10},{14,12},{16,14},{18,16},{20... | collective-permute-start | bytes 122888 | tf_op jit(solution)/shard_map/ppermute | solution.py:511
  8.6 0.0 collective-permute-start.3
  8.6 8.5 %shard_map.46 = (f32[80,320,128]{2,1,0:T(8,128)S(1)}, s32[6,8,128]{2,1,0:T(8,128)S(1)}, f32[5,4,2,8,128]{4,3,2,1,0:T(8,128)S(1)}, f32[5,4,2,8,128]{4,3,2,1,0:T(8,128)S(1)}) custom-call(f32[32,320,320]{2,1,0:T(8,128)} %inv_ref.1, s32[5,32]{1,0:T(8,128)} %bitcast.3, s32[16,128]{1,0:T(8,128)} %bitcast.2, f32[32,320]{1,0:T(8,128)} %u_ref.1), custom_call_target="tpu_custom_call" | custom-call | flops 1000000000 | bytes 1000000 | tf_op jit(solution)/shard_map/pallas_call | solution.py:473
  17.1 0.0 collective-permute-done.refs_4_
  17.1 0.0 collective-permute-done.1.refs_5_
  17.2 0.0 collective-permute-done.2.refs_6_
  17.2 0.0 collective-permute-done.3.refs_7_
  17.2 1.4 %shard_map.47 = (f32[80,128]{1,0:T(8,128)S(1)}, f32[5,2,2,8,128]{4,3,2,1,0:T(8,128)S(1)}, f32[5,4,2,8,128]{4,3,2,1,0:T(8,128)S(1)}, f32[5,4,2,8,128]{4,3,2,1,0:T(8,128)S(1)}) custom-call(f32[80,320,128]{2,1,0:T(8,128)S(1)} %get-tuple-element.26.refs_0_, s32[6,8,128]{2,1,0:T(8,128)S(1)} %get-tuple-element.27.refs_1_, ...), custom_call_target="tpu_custom_call" | custom-call | flops 10000000 | bytes 1000000 | tf_op jit(solution)/shard_map/pallas_call | solution.py:473
  18.6 0.3 collective-permute-start.4
  18.8 4.4 %collective-permute-start.5 = (f32[80,128]{1,0:T(8,128)S(1)}, f32[80,128]{1,0:T(8,128)S(1)}, u32[]{:S(2)}, u32[]{:S(2)}) collective-permute-start(f32[80,128]{1,0:T(8,128)S(1)} %get-tuple-element.30.refs_2_.x_ref), channel_id=1, source_target_pairs={{32,0},{34,2},{36,4},{38,6},{40,8},{42,10},{44,12},{46,14},{48,16}... | collective-permute-start | bytes 122888 | tf_op jit(solution)/shard_map/ppermute | solution.py:511
  23.3 0.0 collective-permute-start.6
  23.3 0.5 collective-permute-start.7
  23.8 0.0 collective-permute-done.4.refs_3_
  23.8 1.2 %collective-permute-done.5.refs_4_ = f32[80,128]{1,0:T(8,128)S(1)} collective-permute-done((f32[80,128]{1,0:T(8,128)S(1)}, f32[80,128]{1,0:T(8,128)S(1)}, u32[]{:S(2)}, u32[]{:S(2)}) %collective-permute-start.5) | collective-permute-done | bytes 40992 | tf_op jit(solution)/shard_map/ppermute | solution.py:511
  24.9 0.0 collective-permute-done.6.refs_5_
  24.9 6.0 %collective-permute-done.7.refs_6_ = f32[80,128]{1,0:T(8,128)S(1)} collective-permute-done((f32[80,128]{1,0:T(8,128)S(1)}, f32[80,128]{1,0:T(8,128)S(1)}, u32[]{:S(2)}, u32[]{:S(2)}) %collective-permute-start.7) | collective-permute-done | bytes 40992 | tf_op jit(solution)/shard_map/ppermute | solution.py:511
  30.9 1.4 %shard_map.48 = (f32[80,128]{1,0:T(8,128)S(1)}, f32[5,2,2,8,128]{4,3,2,1,0:T(8,128)S(1)}, f32[5,4,2,8,128]{4,3,2,1,0:T(8,128)S(1)}, f32[5,4,2,8,128]{4,3,2,1,0:T(8,128)S(1)}) custom-call(f32[80,320,128]{2,1,0:T(8,128)S(1)} %get-tuple-element.26.refs_0_, s32[6,8,128]{2,1,0:T(8,128)S(1)} %get-tuple-element.27.refs_1_, ...), custom_call_target="tpu_custom_call" | custom-call | flops 10000000 | bytes 1000000 | tf_op jit(solution)/shard_map/pallas_call | solution.py:473
  32.3 0.1 collective-permute-start.10
  32.3 0.3 collective-permute-start.11
  32.6 0.0 collective-permute-start.8
  32.6 0.5 collective-permute-start.9
  33.1 0.5 shard_map.49
  33.7 2.1 %collective-permute-done.10.refs_12_ = f32[80,128]{1,0:T(8,128)S(1)} collective-permute-done((f32[80,128]{1,0:T(8,128)S(1)}, f32[80,128]{1,0:T(8,128)S(1)}, u32[]{:S(2)}, u32[]{:S(2)}) %collective-permute-start.10) | collective-permute-done | bytes 40992 | tf_op jit(solution)/shard_map/ppermute | solution.py:511
  35.8 0.9 %collective-permute-done.11.refs_13_ = f32[80,128]{1,0:T(8,128)S(1)} collective-permute-done((f32[80,128]{1,0:T(8,128)S(1)}, f32[80,128]{1,0:T(8,128)S(1)}, u32[]{:S(2)}, u32[]{:S(2)}) %collective-permute-start.11) | collective-permute-done | bytes 40992 | tf_op jit(solution)/shard_map/ppermute | solution.py:511
  36.6 0.0 collective-permute-done.8.refs_10_
  36.6 3.6 %collective-permute-done.9.refs_11_ = f32[80,128]{1,0:T(8,128)S(1)} collective-permute-done((f32[80,128]{1,0:T(8,128)S(1)}, f32[80,128]{1,0:T(8,128)S(1)}, u32[]{:S(2)}, u32[]{:S(2)}) %collective-permute-start.9) | collective-permute-done | bytes 40992 | tf_op jit(solution)/shard_map/ppermute | solution.py:511
  40.3 2.5 %shard_map.50 = (f32[2,80,128]{2,1,0:T(8,128)S(1)}, f32[2,80,128]{2,1,0:T(8,128)S(1)}) custom-call(f32[80,320,128]{2,1,0:T(8,128)S(1)} %get-tuple-element.26.refs_0_, s32[6,8,128]{2,1,0:T(8,128)S(1)} %get-tuple-element.27.refs_1_, f32[5,4,2,8,128]{4,3,2,1,0:T(8,128)S(1)} %get-tuple-element.38.refs_2_, f32[5,4,2,8,128]{4,3,2,1,0:T(8,128)S(1)} %get-tuple-element.39.refs_3_, ...), custom_call_target="tpu_custom_call" | custom-call | flops 10000000 | bytes 1000000 | tf_op jit(solution)/shard_map/pallas_call | solution.py:473
  42.8 0.1 collective-permute-start.12
  42.9 2.0 %collective-permute-start.13 = (f32[2,80,128]{2,1,0:T(8,128)S(1)}, f32[2,80,128]{2,1,0:T(8,128)S(1)}, u32[]{:S(2)}, u32[]{:S(2)}) collective-permute-start(f32[2,80,128]{2,1,0:T(8,128)S(1)} %get-tuple-element.46.refs_3_), channel_id=1, source_target_pairs={{32,0},{34,2},{36,4},{38,6},{40,8},{42,10},{44,12},{46,14},{48,16}... | collective-permute-start | bytes 245768 | tf_op jit(solution)/shard_map/ppermute | solution.py:511
  44.9 0.0 collective-permute-start.14
  44.9 0.5 collective-permute-start.15
  45.4 1.6 %collective-permute-done.12.refs_4_ = f32[2,80,128]{2,1,0:T(8,128)S(1)} collective-permute-done((f32[2,80,128]{2,1,0:T(8,128)S(1)}, f32[2,80,128]{2,1,0:T(8,128)S(1)}, u32[]{:S(2)}, u32[]{:S(2)}) %collective-permute-start.12) | collective-permute-done | bytes 81952 | tf_op jit(solution)/shard_map/ppermute | solution.py:511
  47.0 1.2 %collective-permute-done.13.refs_5_ = f32[2,80,128]{2,1,0:T(8,128)S(1)} collective-permute-done((f32[2,80,128]{2,1,0:T(8,128)S(1)}, f32[2,80,128]{2,1,0:T(8,128)S(1)}, u32[]{:S(2)}, u32[]{:S(2)}) %collective-permute-start.13) | collective-permute-done | bytes 81952 | tf_op jit(solution)/shard_map/ppermute | solution.py:511
  48.2 0.0 collective-permute-done.14.refs_6_
  48.2 4.8 %collective-permute-done.15.refs_7_ = f32[2,80,128]{2,1,0:T(8,128)S(1)} collective-permute-done((f32[2,80,128]{2,1,0:T(8,128)S(1)}, f32[2,80,128]{2,1,0:T(8,128)S(1)}, u32[]{:S(2)}, u32[]{:S(2)}) %collective-permute-start.15) | collective-permute-done | bytes 81952 | tf_op jit(solution)/shard_map/ppermute | solution.py:511
  53.0 3.5 %shard_map.51 = f32[2,32,320]{2,1,0:T(8,128)} custom-call(f32[80,320,128]{2,1,0:T(8,128)S(1)} %get-tuple-element.26.refs_0_, s32[6,8,128]{2,1,0:T(8,128)S(1)} %get-tuple-element.27.refs_1_, f32[2,80,128]{2,1,0:T(8,128)S(1)} %get-tuple-element.45.refs_2_, f32[2,80,128]{2,1,0:T(8,128)S(1)} %get-tuple-element.46.refs_3_, ...), custom_call_target="tpu_custom_call" | custom-call | flops 10000000 | bytes 1000000 | tf_op jit(solution)/shard_map/pallas_call | solution.py:473
Async XLA Ops:
  0.0 17.1 %collective-permute-start = (f32[32,320]{1,0:T(8,128)}, f32[32,320]{1,0:T(8,128)S(1)}, u32[]{:S(2)}, u32[]{:S(2)}) collective-permute-start(f32[32,320]{1,0:T(8,128)} %u_ref.1), channel_id=1, source_target_pairs={{126,0},{0,2},{2,4},{4,6},{6,8},{8,10},{10,12},{12,14},{14,16},{16... | collective-permute-start | bytes 122888 | tf_op jit(solution)/shard_map/ppermute | solution.py:511
  0.0 17.1 %collective-permute-start.1 = (f32[32,320]{1,0:T(8,128)}, f32[32,320]{1,0:T(8,128)S(1)}, u32[]{:S(2)}, u32[]{:S(2)}) collective-permute-start(f32[32,320]{1,0:T(8,128)} %u_ref.1), channel_id=1, source_target_pairs={{32,0},{34,2},{36,4},{38,6},{40,8},{42,10},{44,12},{46,14},{48,16}... | collective-permute-start | bytes 122888 | tf_op jit(solution)/shard_map/ppermute | solution.py:511
  4.1 13.0 %collective-permute-start.2 = (f32[32,320]{1,0:T(8,128)}, f32[32,320]{1,0:T(8,128)S(1)}, u32[]{:S(2)}, u32[]{:S(2)}) collective-permute-start(f32[32,320]{1,0:T(8,128)} %u_ref.1), channel_id=1, source_target_pairs={{2,0},{4,2},{6,4},{8,6},{10,8},{12,10},{14,12},{16,14},{18,16},{20... | collective-permute-start | bytes 122888 | tf_op jit(solution)/shard_map/ppermute | solution.py:511
  8.6 8.6 %collective-permute-start.3 = (f32[32,320]{1,0:T(8,128)}, f32[32,320]{1,0:T(8,128)S(1)}, u32[]{:S(2)}, u32[]{:S(2)}) collective-permute-start(f32[32,320]{1,0:T(8,128)} %u_ref.1), channel_id=1, source_target_pairs={{34,0},{36,2},{38,4},{40,6},{42,8},{44,10},{46,12},{48,14},{50,16}... | collective-permute-start | bytes 122888 | tf_op jit(solution)/shard_map/ppermute | solution.py:511
  18.6 5.2 %collective-permute-start.4 = (f32[80,128]{1,0:T(8,128)S(1)}, f32[80,128]{1,0:T(8,128)S(1)}, u32[]{:S(2)}, u32[]{:S(2)}) collective-permute-start(f32[80,128]{1,0:T(8,128)S(1)} %get-tuple-element.30.refs_2_.x_ref), channel_id=1, source_target_pairs={{34,0},{36,2},{38,4},{40,6},{42,8},{44,10},{46,12},{48,14},{50,16}... | collective-permute-start | bytes 122888 | tf_op jit(solution)/shard_map/ppermute | solution.py:511
  18.8 6.1 %collective-permute-start.5 = (f32[80,128]{1,0:T(8,128)S(1)}, f32[80,128]{1,0:T(8,128)S(1)}, u32[]{:S(2)}, u32[]{:S(2)}) collective-permute-start(f32[80,128]{1,0:T(8,128)S(1)} %get-tuple-element.30.refs_2_.x_ref), channel_id=1, source_target_pairs={{32,0},{34,2},{36,4},{38,6},{40,8},{42,10},{44,12},{46,14},{48,16}... | collective-permute-start | bytes 122888 | tf_op jit(solution)/shard_map/ppermute | solution.py:511
  23.3 1.7 %collective-permute-start.6 = (f32[80,128]{1,0:T(8,128)S(1)}, f32[80,128]{1,0:T(8,128)S(1)}, u32[]{:S(2)}, u32[]{:S(2)}) collective-permute-start(f32[80,128]{1,0:T(8,128)S(1)} %get-tuple-element.30.refs_2_.x_ref), channel_id=1, source_target_pairs={{2,0},{4,2},{6,4},{8,6},{10,8},{12,10},{14,12},{16,14},{18,16},{20... | collective-permute-start | bytes 122888 | tf_op jit(solution)/shard_map/ppermute | solution.py:511
  23.3 7.6 %collective-permute-start.7 = (f32[80,128]{1,0:T(8,128)S(1)}, f32[80,128]{1,0:T(8,128)S(1)}, u32[]{:S(2)}, u32[]{:S(2)}) collective-permute-start(f32[80,128]{1,0:T(8,128)S(1)} %get-tuple-element.30.refs_2_.x_ref), channel_id=1, source_target_pairs={{126,0},{0,2},{2,4},{4,6},{6,8},{8,10},{10,12},{12,14},{14,16},{16... | collective-permute-start | bytes 122888 | tf_op jit(solution)/shard_map/ppermute | solution.py:511
  32.3 3.5 %collective-permute-start.10 = (f32[80,128]{1,0:T(8,128)S(1)}, f32[80,128]{1,0:T(8,128)S(1)}, u32[]{:S(2)}, u32[]{:S(2)}) collective-permute-start(f32[80,128]{1,0:T(8,128)S(1)} %get-tuple-element.31.y_ref.refs_9_), channel_id=1, source_target_pairs={{34,0},{36,2},{38,4},{40,6},{42,8},{44,10},{46,12},{48,14},{50,16}... | collective-permute-start | bytes 122888 | tf_op jit(solution)/shard_map/ppermute | solution.py:511
  32.3 4.3 %collective-permute-start.11 = (f32[80,128]{1,0:T(8,128)S(1)}, f32[80,128]{1,0:T(8,128)S(1)}, u32[]{:S(2)}, u32[]{:S(2)}) collective-permute-start(f32[80,128]{1,0:T(8,128)S(1)} %get-tuple-element.31.y_ref.refs_9_), channel_id=1, source_target_pairs={{32,0},{34,2},{36,4},{38,6},{40,8},{42,10},{44,12},{46,14},{48,16}... | collective-permute-start | bytes 122888 | tf_op jit(solution)/shard_map/ppermute | solution.py:511
  32.6 4.0 %collective-permute-start.8 = (f32[80,128]{1,0:T(8,128)S(1)}, f32[80,128]{1,0:T(8,128)S(1)}, u32[]{:S(2)}, u32[]{:S(2)}) collective-permute-start(f32[80,128]{1,0:T(8,128)S(1)} %get-tuple-element.31.y_ref.refs_9_), channel_id=1, source_target_pairs={{2,0},{4,2},{6,4},{8,6},{10,8},{12,10},{14,12},{16,14},{18,16},{20... | collective-permute-start | bytes 122888 | tf_op jit(solution)/shard_map/ppermute | solution.py:511
  32.6 7.6 %collective-permute-start.9 = (f32[80,128]{1,0:T(8,128)S(1)}, f32[80,128]{1,0:T(8,128)S(1)}, u32[]{:S(2)}, u32[]{:S(2)}) collective-permute-start(f32[80,128]{1,0:T(8,128)S(1)} %get-tuple-element.31.y_ref.refs_9_), channel_id=1, source_target_pairs={{126,0},{0,2},{2,4},{4,6},{6,8},{8,10},{10,12},{12,14},{14,16},{16... | collective-permute-start | bytes 122888 | tf_op jit(solution)/shard_map/ppermute | solution.py:511
  42.8 4.2 %collective-permute-start.12 = (f32[2,80,128]{2,1,0:T(8,128)S(1)}, f32[2,80,128]{2,1,0:T(8,128)S(1)}, u32[]{:S(2)}, u32[]{:S(2)}) collective-permute-start(f32[2,80,128]{2,1,0:T(8,128)S(1)} %get-tuple-element.46.refs_3_), channel_id=1, source_target_pairs={{34,0},{36,2},{38,4},{40,6},{42,8},{44,10},{46,12},{48,14},{50,16}... | collective-permute-start | bytes 245768 | tf_op jit(solution)/shard_map/ppermute | solution.py:511
  42.9 5.3 %collective-permute-start.13 = (f32[2,80,128]{2,1,0:T(8,128)S(1)}, f32[2,80,128]{2,1,0:T(8,128)S(1)}, u32[]{:S(2)}, u32[]{:S(2)}) collective-permute-start(f32[2,80,128]{2,1,0:T(8,128)S(1)} %get-tuple-element.46.refs_3_), channel_id=1, source_target_pairs={{32,0},{34,2},{36,4},{38,6},{40,8},{42,10},{44,12},{46,14},{48,16}... | collective-permute-start | bytes 245768 | tf_op jit(solution)/shard_map/ppermute | solution.py:511
  44.9 3.3 %collective-permute-start.14 = (f32[2,80,128]{2,1,0:T(8,128)S(1)}, f32[2,80,128]{2,1,0:T(8,128)S(1)}, u32[]{:S(2)}, u32[]{:S(2)}) collective-permute-start(f32[2,80,128]{2,1,0:T(8,128)S(1)} %get-tuple-element.46.refs_3_), channel_id=1, source_target_pairs={{2,0},{4,2},{6,4},{8,6},{10,8},{12,10},{14,12},{16,14},{18,16},{20... | collective-permute-start | bytes 245768 | tf_op jit(solution)/shard_map/ppermute | solution.py:511
  44.9 8.1 %collective-permute-start.15 = (f32[2,80,128]{2,1,0:T(8,128)S(1)}, f32[2,80,128]{2,1,0:T(8,128)S(1)}, u32[]{:S(2)}, u32[]{:S(2)}) collective-permute-start(f32[2,80,128]{2,1,0:T(8,128)S(1)} %get-tuple-element.46.refs_3_), channel_id=1, source_target_pairs={{126,0},{0,2},{2,4},{4,6},{6,8},{8,10},{10,12},{12,14},{14,16},{16... | collective-permute-start | bytes 245768 | tf_op jit(solution)/shard_map/ppermute | solution.py:511

commit v5 on v4

--- a/solution.py
+++ b/solution.py
@@ -75,7 +75,7 @@
 STEP_X = [time_step * ROW_SUM[i] for i in range(SECTIONS)]
 STEP_Y = [time_step * ROW_SUM[i] * COUPLING[i] for i in range(SECTIONS)]
 
-ORDERS = [('before', 'ahead', 'after', 'beyond'), ('beyond', 'ahead', 'after', 'before'), ('after', 'before', 'beyond', 'ahead'), ('beyond', 'ahead', 'after', 'before')]
+ORDERS = [('before', 'ahead', 'after', 'beyond'), ('beyond', 'ahead', 'after', 'before'), ('after', 'before', 'beyond', 'ahead'), ('ahead', 'beyond', 'after', 'before')]
 
 
 def sublane():

time: 56.6 us -> 55.7 us (0.984)
  transfers between devices with their start and end apart: 16 -> 16, of which waited for: 8 -> 7; matrix products, arithmetic and copies ran while one was open for 0% -> 0% of each run, Pallas kernels for 16% -> 16%
where the time goes in v5:
time: 55.7 us; the launch traced here: 55.6 us
  waiting for transfers between devices  20.9 us (38%)
  Pallas kernels  17.8 us (32%)
  starting transfers between devices  16.8 us (30%)
    ppermute x16, waiting for transfers between devices, exchanged(): lax.ppermute(block, 'elem', [(s, i) for i, s in enumerate(table[name])])  20.9 us
    pallas_call x6, Pallas kernels, call(): pl.pallas_call(kernel, out_shape=outputs, in_specs=in_specs, out_specs=[p...  17.8 us
    ppermute x16, starting transfers between devices, exchanged(): lax.ppermute(block, 'elem', [(s, i) for i, s in enumerate(table[name])])  16.8 us
  transfers between devices with their start and end apart: 16, of which 7 were waited for; matrix products, arithmetic and copies ran while one was open for 0% of the time, Pallas kernels for 16%

profile of v5, /device:TPU:0, one launch (start us, length us, event | category | flops | bytes accessed | tf_op | source)
XLA Modules:
  0.0 55.6 jit_solution(13362085099703245888)
XLA Ops:
  0.0 0.0 collective-permute-start
  0.0 4.1 %collective-permute-start.1 = (f32[32,320]{1,0:T(8,128)}, f32[32,320]{1,0:T(8,128)S(1)}, u32[]{:S(2)}, u32[]{:S(2)}) collective-permute-start(f32[32,320]{1,0:T(8,128)} %u_ref.1), channel_id=1, source_target_pairs={{32,0},{34,2},{36,4},{38,6},{40,8},{42,10},{44,12},{46,14},{48,16}... | collective-permute-start | bytes 122888 | tf_op jit(solution)/shard_map/ppermute | solution.py:511
  4.1 4.5 %collective-permute-start.2 = (f32[32,320]{1,0:T(8,128)}, f32[32,320]{1,0:T(8,128)S(1)}, u32[]{:S(2)}, u32[]{:S(2)}) collective-permute-start(f32[32,320]{1,0:T(8,128)} %u_ref.1), channel_id=1, source_target_pairs={{2,0},{4,2},{6,4},{8,6},{10,8},{12,10},{14,12},{16,14},{18,16},{20... | collective-permute-start | bytes 122888 | tf_op jit(solution)/shard_map/ppermute | solution.py:511
  8.6 0.0 collective-permute-start.3
  8.6 8.5 %shard_map.46 = (f32[80,320,128]{2,1,0:T(8,128)S(1)}, s32[6,8,128]{2,1,0:T(8,128)S(1)}, f32[5,4,2,8,128]{4,3,2,1,0:T(8,128)S(1)}, f32[5,4,2,8,128]{4,3,2,1,0:T(8,128)S(1)}) custom-call(f32[32,320,320]{2,1,0:T(8,128)} %inv_ref.1, s32[5,32]{1,0:T(8,128)} %bitcast.3, s32[16,128]{1,0:T(8,128)} %bitcast.2, f32[32,320]{1,0:T(8,128)} %u_ref.1), custom_call_target="tpu_custom_call" | custom-call | flops 1000000000 | bytes 1000000 | tf_op jit(solution)/shard_map/pallas_call | solution.py:473
  17.1 0.0 collective-permute-done.refs_4_
  17.1 0.0 collective-permute-done.1.refs_5_
  17.2 0.0 collective-permute-done.2.refs_6_
  17.2 0.0 collective-permute-done.3.refs_7_
  17.2 1.4 %shard_map.47 = (f32[80,128]{1,0:T(8,128)S(1)}, f32[5,2,2,8,128]{4,3,2,1,0:T(8,128)S(1)}, f32[5,4,2,8,128]{4,3,2,1,0:T(8,128)S(1)}, f32[5,4,2,8,128]{4,3,2,1,0:T(8,128)S(1)}) custom-call(f32[80,320,128]{2,1,0:T(8,128)S(1)} %get-tuple-element.26.refs_0_, s32[6,8,128]{2,1,0:T(8,128)S(1)} %get-tuple-element.27.refs_1_, ...), custom_call_target="tpu_custom_call" | custom-call | flops 10000000 | bytes 1000000 | tf_op jit(solution)/shard_map/pallas_call | solution.py:473
  18.6 0.3 collective-permute-start.4
  18.8 4.4 %collective-permute-start.5 = (f32[80,128]{1,0:T(8,128)S(1)}, f32[80,128]{1,0:T(8,128)S(1)}, u32[]{:S(2)}, u32[]{:S(2)}) collective-permute-start(f32[80,128]{1,0:T(8,128)S(1)} %get-tuple-element.30.refs_2_.x_ref), channel_id=1, source_target_pairs={{32,0},{34,2},{36,4},{38,6},{40,8},{42,10},{44,12},{46,14},{48,16}... | collective-permute-start | bytes 122888 | tf_op jit(solution)/shard_map/ppermute | solution.py:511
  23.3 0.0 collective-permute-start.6
  23.3 0.5 collective-permute-start.7
  23.8 0.0 collective-permute-done.4.refs_3_
  23.8 1.2 %collective-permute-done.5.refs_4_ = f32[80,128]{1,0:T(8,128)S(1)} collective-permute-done((f32[80,128]{1,0:T(8,128)S(1)}, f32[80,128]{1,0:T(8,128)S(1)}, u32[]{:S(2)}, u32[]{:S(2)}) %collective-permute-start.5) | collective-permute-done | bytes 40992 | tf_op jit(solution)/shard_map/ppermute | solution.py:511
  24.9 0.0 collective-permute-done.6.refs_5_
  24.9 6.0 %collective-permute-done.7.refs_6_ = f32[80,128]{1,0:T(8,128)S(1)} collective-permute-done((f32[80,128]{1,0:T(8,128)S(1)}, f32[80,128]{1,0:T(8,128)S(1)}, u32[]{:S(2)}, u32[]{:S(2)}) %collective-permute-start.7) | collective-permute-done | bytes 40992 | tf_op jit(solution)/shard_map/ppermute | solution.py:511
  30.9 1.4 %shard_map.48 = (f32[80,128]{1,0:T(8,128)S(1)}, f32[5,2,2,8,128]{4,3,2,1,0:T(8,128)S(1)}, f32[5,4,2,8,128]{4,3,2,1,0:T(8,128)S(1)}, f32[5,4,2,8,128]{4,3,2,1,0:T(8,128)S(1)}) custom-call(f32[80,320,128]{2,1,0:T(8,128)S(1)} %get-tuple-element.26.refs_0_, s32[6,8,128]{2,1,0:T(8,128)S(1)} %get-tuple-element.27.refs_1_, ...), custom_call_target="tpu_custom_call" | custom-call | flops 10000000 | bytes 1000000 | tf_op jit(solution)/shard_map/pallas_call | solution.py:473
  32.3 0.1 collective-permute-start.10
  32.3 0.3 collective-permute-start.11
  32.6 0.0 collective-permute-start.8
  32.6 0.5 collective-permute-start.9
  33.1 0.5 shard_map.49
  33.7 2.1 %collective-permute-done.10.refs_12_ = f32[80,128]{1,0:T(8,128)S(1)} collective-permute-done((f32[80,128]{1,0:T(8,128)S(1)}, f32[80,128]{1,0:T(8,128)S(1)}, u32[]{:S(2)}, u32[]{:S(2)}) %collective-permute-start.10) | collective-permute-done | bytes 40992 | tf_op jit(solution)/shard_map/ppermute | solution.py:511
  35.8 0.9 %collective-permute-done.11.refs_13_ = f32[80,128]{1,0:T(8,128)S(1)} collective-permute-done((f32[80,128]{1,0:T(8,128)S(1)}, f32[80,128]{1,0:T(8,128)S(1)}, u32[]{:S(2)}, u32[]{:S(2)}) %collective-permute-start.11) | collective-permute-done | bytes 40992 | tf_op jit(solution)/shard_map/ppermute | solution.py:511
  36.6 0.0 collective-permute-done.8.refs_10_
  36.6 3.6 %collective-permute-done.9.refs_11_ = f32[80,128]{1,0:T(8,128)S(1)} collective-permute-done((f32[80,128]{1,0:T(8,128)S(1)}, f32[80,128]{1,0:T(8,128)S(1)}, u32[]{:S(2)}, u32[]{:S(2)}) %collective-permute-start.9) | collective-permute-done | bytes 40992 | tf_op jit(solution)/shard_map/ppermute | solution.py:511
  40.3 2.5 %shard_map.50 = (f32[2,80,128]{2,1,0:T(8,128)S(1)}, f32[2,80,128]{2,1,0:T(8,128)S(1)}) custom-call(f32[80,320,128]{2,1,0:T(8,128)S(1)} %get-tuple-element.26.refs_0_, s32[6,8,128]{2,1,0:T(8,128)S(1)} %get-tuple-element.27.refs_1_, f32[5,4,2,8,128]{4,3,2,1,0:T(8,128)S(1)} %get-tuple-element.38.refs_2_, f32[5,4,2,8,128]{4,3,2,1,0:T(8,128)S(1)} %get-tuple-element.39.refs_3_, ...), custom_call_target="tpu_custom_call" | custom-call | flops 10000000 | bytes 1000000 | tf_op jit(solution)/shard_map/pallas_call | solution.py:473
  42.8 0.1 collective-permute-start.12
  42.9 1.1 %collective-permute-start.13 = (f32[2,80,128]{2,1,0:T(8,128)S(1)}, f32[2,80,128]{2,1,0:T(8,128)S(1)}, u32[]{:S(2)}, u32[]{:S(2)}) collective-permute-start(f32[2,80,128]{2,1,0:T(8,128)S(1)} %get-tuple-element.46.refs_3_), channel_id=1, source_target_pairs={{34,0},{36,2},{38,4},{40,6},{42,8},{44,10},{46,12},{48,14},{50,16}... | collective-permute-start | bytes 245768 | tf_op jit(solution)/shard_map/ppermute | solution.py:511
  44.0 0.0 collective-permute-start.14
  44.0 1.0 %collective-permute-start.15 = (f32[2,80,128]{2,1,0:T(8,128)S(1)}, f32[2,80,128]{2,1,0:T(8,128)S(1)}, u32[]{:S(2)}, u32[]{:S(2)}) collective-permute-start(f32[2,80,128]{2,1,0:T(8,128)S(1)} %get-tuple-element.46.refs_3_), channel_id=1, source_target_pairs={{126,0},{0,2},{2,4},{4,6},{6,8},{8,10},{10,12},{12,14},{14,16},{16... | collective-permute-start | bytes 245768 | tf_op jit(solution)/shard_map/ppermute | solution.py:511
  45.0 2.7 %collective-permute-done.12.refs_4_ = f32[2,80,128]{2,1,0:T(8,128)S(1)} collective-permute-done((f32[2,80,128]{2,1,0:T(8,128)S(1)}, f32[2,80,128]{2,1,0:T(8,128)S(1)}, u32[]{:S(2)}, u32[]{:S(2)}) %collective-permute-start.12) | collective-permute-done | bytes 81952 | tf_op jit(solution)/shard_map/ppermute | solution.py:511
  47.7 0.0 collective-permute-done.13.refs_5_
  47.7 0.0 collective-permute-done.14.refs_6_
  47.7 4.4 %collective-permute-done.15.refs_7_ = f32[2,80,128]{2,1,0:T(8,128)S(1)} collective-permute-done((f32[2,80,128]{2,1,0:T(8,128)S(1)}, f32[2,80,128]{2,1,0:T(8,128)S(1)}, u32[]{:S(2)}, u32[]{:S(2)}) %collective-permute-start.15) | collective-permute-done | bytes 81952 | tf_op jit(solution)/shard_map/ppermute | solution.py:511
  52.1 3.5 %shard_map.51 = f32[2,32,320]{2,1,0:T(8,128)} custom-call(f32[80,320,128]{2,1,0:T(8,128)S(1)} %get-tuple-element.26.refs_0_, s32[6,8,128]{2,1,0:T(8,128)S(1)} %get-tuple-element.27.refs_1_, f32[2,80,128]{2,1,0:T(8,128)S(1)} %get-tuple-element.45.refs_2_, f32[2,80,128]{2,1,0:T(8,128)S(1)} %get-tuple-element.46.refs_3_, ...), custom_call_target="tpu_custom_call" | custom-call | flops 10000000 | bytes 1000000 | tf_op jit(solution)/shard_map/pallas_call | solution.py:473
Async XLA Ops:
  0.0 17.1 %collective-permute-start = (f32[32,320]{1,0:T(8,128)}, f32[32,320]{1,0:T(8,128)S(1)}, u32[]{:S(2)}, u32[]{:S(2)}) collective-permute-start(f32[32,320]{1,0:T(8,128)} %u_ref.1), channel_id=1, source_target_pairs={{126,0},{0,2},{2,4},{4,6},{6,8},{8,10},{10,12},{12,14},{14,16},{16... | collective-permute-start | bytes 122888 | tf_op jit(solution)/shard_map/ppermute | solution.py:511
  0.0 17.1 %collective-permute-start.1 = (f32[32,320]{1,0:T(8,128)}, f32[32,320]{1,0:T(8,128)S(1)}, u32[]{:S(2)}, u32[]{:S(2)}) collective-permute-start(f32[32,320]{1,0:T(8,128)} %u_ref.1), channel_id=1, source_target_pairs={{32,0},{34,2},{36,4},{38,6},{40,8},{42,10},{44,12},{46,14},{48,16}... | collective-permute-start | bytes 122888 | tf_op jit(solution)/shard_map/ppermute | solution.py:511
  4.1 13.0 %collective-permute-start.2 = (f32[32,320]{1,0:T(8,128)}, f32[32,320]{1,0:T(8,128)S(1)}, u32[]{:S(2)}, u32[]{:S(2)}) collective-permute-start(f32[32,320]{1,0:T(8,128)} %u_ref.1), channel_id=1, source_target_pairs={{2,0},{4,2},{6,4},{8,6},{10,8},{12,10},{14,12},{16,14},{18,16},{20... | collective-permute-start | bytes 122888 | tf_op jit(solution)/shard_map/ppermute | solution.py:511
  8.6 8.6 %collective-permute-start.3 = (f32[32,320]{1,0:T(8,128)}, f32[32,320]{1,0:T(8,128)S(1)}, u32[]{:S(2)}, u32[]{:S(2)}) collective-permute-start(f32[32,320]{1,0:T(8,128)} %u_ref.1), channel_id=1, source_target_pairs={{34,0},{36,2},{38,4},{40,6},{42,8},{44,10},{46,12},{48,14},{50,16}... | collective-permute-start | bytes 122888 | tf_op jit(solution)/shard_map/ppermute | solution.py:511
  18.6 5.2 %collective-permute-start.4 = (f32[80,128]{1,0:T(8,128)S(1)}, f32[80,128]{1,0:T(8,128)S(1)}, u32[]{:S(2)}, u32[]{:S(2)}) collective-permute-start(f32[80,128]{1,0:T(8,128)S(1)} %get-tuple-element.30.refs_2_.x_ref), channel_id=1, source_target_pairs={{34,0},{36,2},{38,4},{40,6},{42,8},{44,10},{46,12},{48,14},{50,16}... | collective-permute-start | bytes 122888 | tf_op jit(solution)/shard_map/ppermute | solution.py:511
  18.8 6.1 %collective-permute-start.5 = (f32[80,128]{1,0:T(8,128)S(1)}, f32[80,128]{1,0:T(8,128)S(1)}, u32[]{:S(2)}, u32[]{:S(2)}) collective-permute-start(f32[80,128]{1,0:T(8,128)S(1)} %get-tuple-element.30.refs_2_.x_ref), channel_id=1, source_target_pairs={{32,0},{34,2},{36,4},{38,6},{40,8},{42,10},{44,12},{46,14},{48,16}... | collective-permute-start | bytes 122888 | tf_op jit(solution)/shard_map/ppermute | solution.py:511
  23.3 1.7 %collective-permute-start.6 = (f32[80,128]{1,0:T(8,128)S(1)}, f32[80,128]{1,0:T(8,128)S(1)}, u32[]{:S(2)}, u32[]{:S(2)}) collective-permute-start(f32[80,128]{1,0:T(8,128)S(1)} %get-tuple-element.30.refs_2_.x_ref), channel_id=1, source_target_pairs={{2,0},{4,2},{6,4},{8,6},{10,8},{12,10},{14,12},{16,14},{18,16},{20... | collective-permute-start | bytes 122888 | tf_op jit(solution)/shard_map/ppermute | solution.py:511
  23.3 7.6 %collective-permute-start.7 = (f32[80,128]{1,0:T(8,128)S(1)}, f32[80,128]{1,0:T(8,128)S(1)}, u32[]{:S(2)}, u32[]{:S(2)}) collective-permute-start(f32[80,128]{1,0:T(8,128)S(1)} %get-tuple-element.30.refs_2_.x_ref), channel_id=1, source_target_pairs={{126,0},{0,2},{2,4},{4,6},{6,8},{8,10},{10,12},{12,14},{14,16},{16... | collective-permute-start | bytes 122888 | tf_op jit(solution)/shard_map/ppermute | solution.py:511
  32.3 3.5 %collective-permute-start.10 = (f32[80,128]{1,0:T(8,128)S(1)}, f32[80,128]{1,0:T(8,128)S(1)}, u32[]{:S(2)}, u32[]{:S(2)}) collective-permute-start(f32[80,128]{1,0:T(8,128)S(1)} %get-tuple-element.31.y_ref.refs_9_), channel_id=1, source_target_pairs={{34,0},{36,2},{38,4},{40,6},{42,8},{44,10},{46,12},{48,14},{50,16}... | collective-permute-start | bytes 122888 | tf_op jit(solution)/shard_map/ppermute | solution.py:511
  32.3 4.3 %collective-permute-start.11 = (f32[80,128]{1,0:T(8,128)S(1)}, f32[80,128]{1,0:T(8,128)S(1)}, u32[]{:S(2)}, u32[]{:S(2)}) collective-permute-start(f32[80,128]{1,0:T(8,128)S(1)} %get-tuple-element.31.y_ref.refs_9_), channel_id=1, source_target_pairs={{32,0},{34,2},{36,4},{38,6},{40,8},{42,10},{44,12},{46,14},{48,16}... | collective-permute-start | bytes 122888 | tf_op jit(solution)/shard_map/ppermute | solution.py:511
  32.6 4.0 %collective-permute-start.8 = (f32[80,128]{1,0:T(8,128)S(1)}, f32[80,128]{1,0:T(8,128)S(1)}, u32[]{:S(2)}, u32[]{:S(2)}) collective-permute-start(f32[80,128]{1,0:T(8,128)S(1)} %get-tuple-element.31.y_ref.refs_9_), channel_id=1, source_target_pairs={{2,0},{4,2},{6,4},{8,6},{10,8},{12,10},{14,12},{16,14},{18,16},{20... | collective-permute-start | bytes 122888 | tf_op jit(solution)/shard_map/ppermute | solution.py:511
  32.6 7.6 %collective-permute-start.9 = (f32[80,128]{1,0:T(8,128)S(1)}, f32[80,128]{1,0:T(8,128)S(1)}, u32[]{:S(2)}, u32[]{:S(2)}) collective-permute-start(f32[80,128]{1,0:T(8,128)S(1)} %get-tuple-element.31.y_ref.refs_9_), channel_id=1, source_target_pairs={{126,0},{0,2},{2,4},{4,6},{6,8},{8,10},{10,12},{12,14},{14,16},{16... | collective-permute-start | bytes 122888 | tf_op jit(solution)/shard_map/ppermute | solution.py:511
  42.8 4.9 %collective-permute-start.12 = (f32[2,80,128]{2,1,0:T(8,128)S(1)}, f32[2,80,128]{2,1,0:T(8,128)S(1)}, u32[]{:S(2)}, u32[]{:S(2)}) collective-permute-start(f32[2,80,128]{2,1,0:T(8,128)S(1)} %get-tuple-element.46.refs_3_), channel_id=1, source_target_pairs={{32,0},{34,2},{36,4},{38,6},{40,8},{42,10},{44,12},{46,14},{48,16}... | collective-permute-start | bytes 245768 | tf_op jit(solution)/shard_map/ppermute | solution.py:511
  42.9 4.8 %collective-permute-start.13 = (f32[2,80,128]{2,1,0:T(8,128)S(1)}, f32[2,80,128]{2,1,0:T(8,128)S(1)}, u32[]{:S(2)}, u32[]{:S(2)}) collective-permute-start(f32[2,80,128]{2,1,0:T(8,128)S(1)} %get-tuple-element.46.refs_3_), channel_id=1, source_target_pairs={{34,0},{36,2},{38,4},{40,6},{42,8},{44,10},{46,12},{48,14},{50,16}... | collective-permute-start | bytes 245768 | tf_op jit(solution)/shard_map/ppermute | solution.py:511
  44.0 3.7 %collective-permute-start.14 = (f32[2,80,128]{2,1,0:T(8,128)S(1)}, f32[2,80,128]{2,1,0:T(8,128)S(1)}, u32[]{:S(2)}, u32[]{:S(2)}) collective-permute-start(f32[2,80,128]{2,1,0:T(8,128)S(1)} %get-tuple-element.46.refs_3_), channel_id=1, source_target_pairs={{2,0},{4,2},{6,4},{8,6},{10,8},{12,10},{14,12},{16,14},{18,16},{20... | collective-permute-start | bytes 245768 | tf_op jit(solution)/shard_map/ppermute | solution.py:511
  44.0 8.1 %collective-permute-start.15 = (f32[2,80,128]{2,1,0:T(8,128)S(1)}, f32[2,80,128]{2,1,0:T(8,128)S(1)}, u32[]{:S(2)}, u32[]{:S(2)}) collective-permute-start(f32[2,80,128]{2,1,0:T(8,128)S(1)} %get-tuple-element.46.refs_3_), channel_id=1, source_target_pairs={{126,0},{0,2},{2,4},{4,6},{6,8},{8,10},{10,12},{12,14},{14,16},{16... | collective-permute-start | bytes 245768 | tf_op jit(solution)/shard_map/ppermute | solution.py:511

commit v6 on v5

--- a/solution.py
+++ b/solution.py
@@ -75,7 +75,7 @@
 STEP_X = [time_step * ROW_SUM[i] for i in range(SECTIONS)]
 STEP_Y = [time_step * ROW_SUM[i] * COUPLING[i] for i in range(SECTIONS)]
 
-ORDERS = [('before', 'ahead', 'after', 'beyond'), ('beyond', 'ahead', 'after', 'before'), ('after', 'before', 'beyond', 'ahead'), ('ahead', 'beyond', 'after', 'before')]
+ORDERS = [('before', 'ahead', 'beyond', 'after'), ('beyond', 'ahead', 'after', 'before'), ('after', 'before', 'beyond', 'ahead'), ('ahead', 'beyond', 'after', 'before')]
 
 
 def sublane():

time: 55.7 us -> 55.5 us (level)
  no operation moved by 1% of the time
where the time goes in v6:
time: 55.5 us; the launch traced here: 55.4 us
  waiting for transfers between devices  20.9 us (38%)
  Pallas kernels  17.8 us (32%)
  starting transfers between devices  16.6 us (30%)
    ppermute x16, waiting for transfers between devices, exchanged(): lax.ppermute(block, 'elem', [(s, i) for i, s in enumerate(table[name])])  20.9 us
    pallas_call x6, Pallas kernels, call(): pl.pallas_call(kernel, out_shape=outputs, in_specs=in_specs, out_specs=[p...  17.8 us
    ppermute x16, starting transfers between devices, exchanged(): lax.ppermute(block, 'elem', [(s, i) for i, s in enumerate(table[name])])  16.6 us
  transfers between devices with their start and end apart: 16, of which 7 were waited for; matrix products, arithmetic and copies ran while one was open for 0% of the time, Pallas kernels for 16%

profile of v6, /device:TPU:0, one launch (start us, length us, event | category | flops | bytes accessed | tf_op | source)
XLA Modules:
  0.0 55.4 jit_solution(5636885861693863259)
XLA Ops:
  0.0 0.0 collective-permute-start
  0.0 4.1 %collective-permute-start.1 = (f32[32,320]{1,0:T(8,128)}, f32[32,320]{1,0:T(8,128)S(1)}, u32[]{:S(2)}, u32[]{:S(2)}) collective-permute-start(f32[32,320]{1,0:T(8,128)} %u_ref.1), channel_id=1, source_target_pairs={{32,0},{34,2},{36,4},{38,6},{40,8},{42,10},{44,12},{46,14},{48,16}... | collective-permute-start | bytes 122888 | tf_op jit(solution)/shard_map/ppermute | solution.py:511
  4.1 4.3 %collective-permute-start.2 = (f32[32,320]{1,0:T(8,128)}, f32[32,320]{1,0:T(8,128)S(1)}, u32[]{:S(2)}, u32[]{:S(2)}) collective-permute-start(f32[32,320]{1,0:T(8,128)} %u_ref.1), channel_id=1, source_target_pairs={{34,0},{36,2},{38,4},{40,6},{42,8},{44,10},{46,12},{48,14},{50,16}... | collective-permute-start | bytes 122888 | tf_op jit(solution)/shard_map/ppermute | solution.py:511
  8.4 0.2 collective-permute-start.3
  8.6 8.5 %shard_map.46 = (f32[80,320,128]{2,1,0:T(8,128)S(1)}, s32[6,8,128]{2,1,0:T(8,128)S(1)}, f32[5,4,2,8,128]{4,3,2,1,0:T(8,128)S(1)}, f32[5,4,2,8,128]{4,3,2,1,0:T(8,128)S(1)}) custom-call(f32[32,320,320]{2,1,0:T(8,128)} %inv_ref.1, s32[5,32]{1,0:T(8,128)} %bitcast.3, s32[16,128]{1,0:T(8,128)} %bitcast.2, f32[32,320]{1,0:T(8,128)} %u_ref.1), custom_call_target="tpu_custom_call" | custom-call | flops 1000000000 | bytes 1000000 | tf_op jit(solution)/shard_map/pallas_call | solution.py:473
  17.1 0.0 collective-permute-done.refs_4_
  17.1 0.0 collective-permute-done.1.refs_5_
  17.2 0.0 collective-permute-done.2.refs_6_
  17.2 0.0 collective-permute-done.3.refs_7_
  17.2 1.4 %shard_map.47 = (f32[80,128]{1,0:T(8,128)S(1)}, f32[5,2,2,8,128]{4,3,2,1,0:T(8,128)S(1)}, f32[5,4,2,8,128]{4,3,2,1,0:T(8,128)S(1)}, f32[5,4,2,8,128]{4,3,2,1,0:T(8,128)S(1)}) custom-call(f32[80,320,128]{2,1,0:T(8,128)S(1)} %get-tuple-element.26.refs_0_, s32[6,8,128]{2,1,0:T(8,128)S(1)} %get-tuple-element.27.refs_1_, ...), custom_call_target="tpu_custom_call" | custom-call | flops 10000000 | bytes 1000000 | tf_op jit(solution)/shard_map/pallas_call | solution.py:473
  18.6 0.1 collective-permute-start.4
  18.7 4.4 %collective-permute-start.5 = (f32[80,128]{1,0:T(8,128)S(1)}, f32[80,128]{1,0:T(8,128)S(1)}, u32[]{:S(2)}, u32[]{:S(2)}) collective-permute-start(f32[80,128]{1,0:T(8,128)S(1)} %get-tuple-element.30.refs_2_.x_ref), channel_id=1, source_target_pairs={{32,0},{34,2},{36,4},{38,6},{40,8},{42,10},{44,12},{46,14},{48,16}... | collective-permute-start | bytes 122888 | tf_op jit(solution)/shard_map/ppermute | solution.py:511
  23.1 0.0 collective-permute-start.6
  23.1 0.5 collective-permute-start.7
  23.6 0.0 collective-permute-done.4.refs_3_
  23.6 1.2 %collective-permute-done.5.refs_4_ = f32[80,128]{1,0:T(8,128)S(1)} collective-permute-done((f32[80,128]{1,0:T(8,128)S(1)}, f32[80,128]{1,0:T(8,128)S(1)}, u32[]{:S(2)}, u32[]{:S(2)}) %collective-permute-start.5) | collective-permute-done | bytes 40992 | tf_op jit(solution)/shard_map/ppermute | solution.py:511
  24.8 0.0 collective-permute-done.6.refs_5_
  24.8 6.0 %collective-permute-done.7.refs_6_ = f32[80,128]{1,0:T(8,128)S(1)} collective-permute-done((f32[80,128]{1,0:T(8,128)S(1)}, f32[80,128]{1,0:T(8,128)S(1)}, u32[]{:S(2)}, u32[]{:S(2)}) %collective-permute-start.7) | collective-permute-done | bytes 40992 | tf_op jit(solution)/shard_map/ppermute | solution.py:511
  30.7 1.4 %shard_map.48 = (f32[80,128]{1,0:T(8,128)S(1)}, f32[5,2,2,8,128]{4,3,2,1,0:T(8,128)S(1)}, f32[5,4,2,8,128]{4,3,2,1,0:T(8,128)S(1)}, f32[5,4,2,8,128]{4,3,2,1,0:T(8,128)S(1)}) custom-call(f32[80,320,128]{2,1,0:T(8,128)S(1)} %get-tuple-element.26.refs_0_, s32[6,8,128]{2,1,0:T(8,128)S(1)} %get-tuple-element.27.refs_1_, ...), custom_call_target="tpu_custom_call" | custom-call | flops 10000000 | bytes 1000000 | tf_op jit(solution)/shard_map/pallas_call | solution.py:473
  32.1 0.1 collective-permute-start.10
  32.2 0.3 collective-permute-start.11
  32.5 0.0 collective-permute-start.8
  32.5 0.5 collective-permute-start.9
  33.0 0.5 shard_map.49
  33.5 2.1 %collective-permute-done.10.refs_12_ = f32[80,128]{1,0:T(8,128)S(1)} collective-permute-done((f32[80,128]{1,0:T(8,128)S(1)}, f32[80,128]{1,0:T(8,128)S(1)}, u32[]{:S(2)}, u32[]{:S(2)}) %collective-permute-start.10) | collective-permute-done | bytes 40992 | tf_op jit(solution)/shard_map/ppermute | solution.py:511
  35.6 0.9 %collective-permute-done.11.refs_13_ = f32[80,128]{1,0:T(8,128)S(1)} collective-permute-done((f32[80,128]{1,0:T(8,128)S(1)}, f32[80,128]{1,0:T(8,128)S(1)}, u32[]{:S(2)}, u32[]{:S(2)}) %collective-permute-start.11) | collective-permute-done | bytes 40992 | tf_op jit(solution)/shard_map/ppermute | solution.py:511
  36.5 0.0 collective-permute-done.8.refs_10_
  36.5 3.6 %collective-permute-done.9.refs_11_ = f32[80,128]{1,0:T(8,128)S(1)} collective-permute-done((f32[80,128]{1,0:T(8,128)S(1)}, f32[80,128]{1,0:T(8,128)S(1)}, u32[]{:S(2)}, u32[]{:S(2)}) %collective-permute-start.9) | collective-permute-done | bytes 40992 | tf_op jit(solution)/shard_map/ppermute | solution.py:511
  40.1 2.5 %shard_map.50 = (f32[2,80,128]{2,1,0:T(8,128)S(1)}, f32[2,80,128]{2,1,0:T(8,128)S(1)}) custom-call(f32[80,320,128]{2,1,0:T(8,128)S(1)} %get-tuple-element.26.refs_0_, s32[6,8,128]{2,1,0:T(8,128)S(1)} %get-tuple-element.27.refs_1_, f32[5,4,2,8,128]{4,3,2,1,0:T(8,128)S(1)} %get-tuple-element.38.refs_2_, f32[5,4,2,8,128]{4,3,2,1,0:T(8,128)S(1)} %get-tuple-element.39.refs_3_, ...), custom_call_target="tpu_custom_call" | custom-call | flops 10000000 | bytes 1000000 | tf_op jit(solution)/shard_map/pallas_call | solution.py:473
  42.6 0.1 collective-permute-start.12
  42.7 1.1 %collective-permute-start.13 = (f32[2,80,128]{2,1,0:T(8,128)S(1)}, f32[2,80,128]{2,1,0:T(8,128)S(1)}, u32[]{:S(2)}, u32[]{:S(2)}) collective-permute-start(f32[2,80,128]{2,1,0:T(8,128)S(1)} %get-tuple-element.46.refs_3_), channel_id=1, source_target_pairs={{34,0},{36,2},{38,4},{40,6},{42,8},{44,10},{46,12},{48,14},{50,16}... | collective-permute-start | bytes 245768 | tf_op jit(solution)/shard_map/ppermute | solution.py:511
  43.8 0.0 collective-permute-start.14
  43.8 1.0 %collective-permute-start.15 = (f32[2,80,128]{2,1,0:T(8,128)S(1)}, f32[2,80,128]{2,1,0:T(8,128)S(1)}, u32[]{:S(2)}, u32[]{:S(2)}) collective-permute-start(f32[2,80,128]{2,1,0:T(8,128)S(1)} %get-tuple-element.46.refs_3_), channel_id=1, source_target_pairs={{126,0},{0,2},{2,4},{4,6},{6,8},{8,10},{10,12},{12,14},{14,16},{16... | collective-permute-start | bytes 245768 | tf_op jit(solution)/shard_map/ppermute | solution.py:511
  44.8 2.7 %collective-permute-done.12.refs_4_ = f32[2,80,128]{2,1,0:T(8,128)S(1)} collective-permute-done((f32[2,80,128]{2,1,0:T(8,128)S(1)}, f32[2,80,128]{2,1,0:T(8,128)S(1)}, u32[]{:S(2)}, u32[]{:S(2)}) %collective-permute-start.12) | collective-permute-done | bytes 81952 | tf_op jit(solution)/shard_map/ppermute | solution.py:511
  47.5 0.0 collective-permute-done.13.refs_5_
  47.5 0.0 collective-permute-done.14.refs_6_
  47.5 4.4 %collective-permute-done.15.refs_7_ = f32[2,80,128]{2,1,0:T(8,128)S(1)} collective-permute-done((f32[2,80,128]{2,1,0:T(8,128)S(1)}, f32[2,80,128]{2,1,0:T(8,128)S(1)}, u32[]{:S(2)}, u32[]{:S(2)}) %collective-permute-start.15) | collective-permute-done | bytes 81952 | tf_op jit(solution)/shard_map/ppermute | solution.py:511
  51.9 3.5 %shard_map.51 = f32[2,32,320]{2,1,0:T(8,128)} custom-call(f32[80,320,128]{2,1,0:T(8,128)S(1)} %get-tuple-element.26.refs_0_, s32[6,8,128]{2,1,0:T(8,128)S(1)} %get-tuple-element.27.refs_1_, f32[2,80,128]{2,1,0:T(8,128)S(1)} %get-tuple-element.45.refs_2_, f32[2,80,128]{2,1,0:T(8,128)S(1)} %get-tuple-element.46.refs_3_, ...), custom_call_target="tpu_custom_call" | custom-call | flops 10000000 | bytes 1000000 | tf_op jit(solution)/shard_map/pallas_call | solution.py:473
Async XLA Ops:
  0.0 17.1 %collective-permute-start = (f32[32,320]{1,0:T(8,128)}, f32[32,320]{1,0:T(8,128)S(1)}, u32[]{:S(2)}, u32[]{:S(2)}) collective-permute-start(f32[32,320]{1,0:T(8,128)} %u_ref.1), channel_id=1, source_target_pairs={{126,0},{0,2},{2,4},{4,6},{6,8},{8,10},{10,12},{12,14},{14,16},{16... | collective-permute-start | bytes 122888 | tf_op jit(solution)/shard_map/ppermute | solution.py:511
  0.0 17.1 %collective-permute-start.1 = (f32[32,320]{1,0:T(8,128)}, f32[32,320]{1,0:T(8,128)S(1)}, u32[]{:S(2)}, u32[]{:S(2)}) collective-permute-start(f32[32,320]{1,0:T(8,128)} %u_ref.1), channel_id=1, source_target_pairs={{32,0},{34,2},{36,4},{38,6},{40,8},{42,10},{44,12},{46,14},{48,16}... | collective-permute-start | bytes 122888 | tf_op jit(solution)/shard_map/ppermute | solution.py:511
  4.1 13.0 %collective-permute-start.2 = (f32[32,320]{1,0:T(8,128)}, f32[32,320]{1,0:T(8,128)S(1)}, u32[]{:S(2)}, u32[]{:S(2)}) collective-permute-start(f32[32,320]{1,0:T(8,128)} %u_ref.1), channel_id=1, source_target_pairs={{34,0},{36,2},{38,4},{40,6},{42,8},{44,10},{46,12},{48,14},{50,16}... | collective-permute-start | bytes 122888 | tf_op jit(solution)/shard_map/ppermute | solution.py:511
  8.4 8.7 %collective-permute-start.3 = (f32[32,320]{1,0:T(8,128)}, f32[32,320]{1,0:T(8,128)S(1)}, u32[]{:S(2)}, u32[]{:S(2)}) collective-permute-start(f32[32,320]{1,0:T(8,128)} %u_ref.1), channel_id=1, source_target_pairs={{2,0},{4,2},{6,4},{8,6},{10,8},{12,10},{14,12},{16,14},{18,16},{20... | collective-permute-start | bytes 122888 | tf_op jit(solution)/shard_map/ppermute | solution.py:511
  18.6 5.0 %collective-permute-start.4 = (f32[80,128]{1,0:T(8,128)S(1)}, f32[80,128]{1,0:T(8,128)S(1)}, u32[]{:S(2)}, u32[]{:S(2)}) collective-permute-start(f32[80,128]{1,0:T(8,128)S(1)} %get-tuple-element.30.refs_2_.x_ref), channel_id=1, source_target_pairs={{34,0},{36,2},{38,4},{40,6},{42,8},{44,10},{46,12},{48,14},{50,16}... | collective-permute-start | bytes 122888 | tf_op jit(solution)/shard_map/ppermute | solution.py:511
  18.7 6.1 %collective-permute-start.5 = (f32[80,128]{1,0:T(8,128)S(1)}, f32[80,128]{1,0:T(8,128)S(1)}, u32[]{:S(2)}, u32[]{:S(2)}) collective-permute-start(f32[80,128]{1,0:T(8,128)S(1)} %get-tuple-element.30.refs_2_.x_ref), channel_id=1, source_target_pairs={{32,0},{34,2},{36,4},{38,6},{40,8},{42,10},{44,12},{46,14},{48,16}... | collective-permute-start | bytes 122888 | tf_op jit(solution)/shard_map/ppermute | solution.py:511
  23.1 1.7 %collective-permute-start.6 = (f32[80,128]{1,0:T(8,128)S(1)}, f32[80,128]{1,0:T(8,128)S(1)}, u32[]{:S(2)}, u32[]{:S(2)}) collective-permute-start(f32[80,128]{1,0:T(8,128)S(1)} %get-tuple-element.30.refs_2_.x_ref), channel_id=1, source_target_pairs={{2,0},{4,2},{6,4},{8,6},{10,8},{12,10},{14,12},{16,14},{18,16},{20... | collective-permute-start | bytes 122888 | tf_op jit(solution)/shard_map/ppermute | solution.py:511
  23.1 7.6 %collective-permute-start.7 = (f32[80,128]{1,0:T(8,128)S(1)}, f32[80,128]{1,0:T(8,128)S(1)}, u32[]{:S(2)}, u32[]{:S(2)}) collective-permute-start(f32[80,128]{1,0:T(8,128)S(1)} %get-tuple-element.30.refs_2_.x_ref), channel_id=1, source_target_pairs={{126,0},{0,2},{2,4},{4,6},{6,8},{8,10},{10,12},{12,14},{14,16},{16... | collective-permute-start | bytes 122888 | tf_op jit(solution)/shard_map/ppermute | solution.py:511
  32.1 3.5 %collective-permute-start.10 = (f32[80,128]{1,0:T(8,128)S(1)}, f32[80,128]{1,0:T(8,128)S(1)}, u32[]{:S(2)}, u32[]{:S(2)}) collective-permute-start(f32[80,128]{1,0:T(8,128)S(1)} %get-tuple-element.31.y_ref.refs_9_), channel_id=1, source_target_pairs={{34,0},{36,2},{38,4},{40,6},{42,8},{44,10},{46,12},{48,14},{50,16}... | collective-permute-start | bytes 122888 | tf_op jit(solution)/shard_map/ppermute | solution.py:511
  32.2 4.3 %collective-permute-start.11 = (f32[80,128]{1,0:T(8,128)S(1)}, f32[80,128]{1,0:T(8,128)S(1)}, u32[]{:S(2)}, u32[]{:S(2)}) collective-permute-start(f32[80,128]{1,0:T(8,128)S(1)} %get-tuple-element.31.y_ref.refs_9_), channel_id=1, source_target_pairs={{32,0},{34,2},{36,4},{38,6},{40,8},{42,10},{44,12},{46,14},{48,16}... | collective-permute-start | bytes 122888 | tf_op jit(solution)/shard_map/ppermute | solution.py:511
  32.5 4.0 %collective-permute-start.8 = (f32[80,128]{1,0:T(8,128)S(1)}, f32[80,128]{1,0:T(8,128)S(1)}, u32[]{:S(2)}, u32[]{:S(2)}) collective-permute-start(f32[80,128]{1,0:T(8,128)S(1)} %get-tuple-element.31.y_ref.refs_9_), channel_id=1, source_target_pairs={{2,0},{4,2},{6,4},{8,6},{10,8},{12,10},{14,12},{16,14},{18,16},{20... | collective-permute-start | bytes 122888 | tf_op jit(solution)/shard_map/ppermute | solution.py:511
  32.5 7.6 %collective-permute-start.9 = (f32[80,128]{1,0:T(8,128)S(1)}, f32[80,128]{1,0:T(8,128)S(1)}, u32[]{:S(2)}, u32[]{:S(2)}) collective-permute-start(f32[80,128]{1,0:T(8,128)S(1)} %get-tuple-element.31.y_ref.refs_9_), channel_id=1, source_target_pairs={{126,0},{0,2},{2,4},{4,6},{6,8},{8,10},{10,12},{12,14},{14,16},{16... | collective-permute-start | bytes 122888 | tf_op jit(solution)/shard_map/ppermute | solution.py:511
  42.6 4.9 %collective-permute-start.12 = (f32[2,80,128]{2,1,0:T(8,128)S(1)}, f32[2,80,128]{2,1,0:T(8,128)S(1)}, u32[]{:S(2)}, u32[]{:S(2)}) collective-permute-start(f32[2,80,128]{2,1,0:T(8,128)S(1)} %get-tuple-element.46.refs_3_), channel_id=1, source_target_pairs={{32,0},{34,2},{36,4},{38,6},{40,8},{42,10},{44,12},{46,14},{48,16}... | collective-permute-start | bytes 245768 | tf_op jit(solution)/shard_map/ppermute | solution.py:511
  42.7 4.8 %collective-permute-start.13 = (f32[2,80,128]{2,1,0:T(8,128)S(1)}, f32[2,80,128]{2,1,0:T(8,128)S(1)}, u32[]{:S(2)}, u32[]{:S(2)}) collective-permute-start(f32[2,80,128]{2,1,0:T(8,128)S(1)} %get-tuple-element.46.refs_3_), channel_id=1, source_target_pairs={{34,0},{36,2},{38,4},{40,6},{42,8},{44,10},{46,12},{48,14},{50,16}... | collective-permute-start | bytes 245768 | tf_op jit(solution)/shard_map/ppermute | solution.py:511
  43.8 3.7 %collective-permute-start.14 = (f32[2,80,128]{2,1,0:T(8,128)S(1)}, f32[2,80,128]{2,1,0:T(8,128)S(1)}, u32[]{:S(2)}, u32[]{:S(2)}) collective-permute-start(f32[2,80,128]{2,1,0:T(8,128)S(1)} %get-tuple-element.46.refs_3_), channel_id=1, source_target_pairs={{2,0},{4,2},{6,4},{8,6},{10,8},{12,10},{14,12},{16,14},{18,16},{20... | collective-permute-start | bytes 245768 | tf_op jit(solution)/shard_map/ppermute | solution.py:511
  43.8 8.1 %collective-permute-start.15 = (f32[2,80,128]{2,1,0:T(8,128)S(1)}, f32[2,80,128]{2,1,0:T(8,128)S(1)}, u32[]{:S(2)}, u32[]{:S(2)}) collective-permute-start(f32[2,80,128]{2,1,0:T(8,128)S(1)} %get-tuple-element.46.refs_3_), channel_id=1, source_target_pairs={{126,0},{0,2},{2,4},{4,6},{6,8},{8,10},{10,12},{12,14},{14,16},{16... | collective-permute-start | bytes 245768 | tf_op jit(solution)/shard_map/ppermute | solution.py:511
